TPU v7x, 32 devices: a whole 2x2x4 slice. The times are simulated.
32 devices in a mesh: row: 8 (over y, x, core), col: 4 (over z).
Axes of the slice: x: 2, y: 2, z: 4, core: 2. Of those that a mesh axis runs over, the one named last changes fastest.
Arguments:
- x_src: bfloat16 [50, 4096], P(None, ('row', 'col')), may hold values from -2.5 to 2.5
- y_tgt: bfloat16 [50, 8192], P(None, ('row', 'col')), may hold values from -2.5 to 2.5
- a_src: bfloat16 [4096], P(('row', 'col')), may hold values from 0.099609375 to 10
- b_tgt: bfloat16 [8192], P(('row', 'col')), may hold values from 0.099609375 to 10
Outputs:
- proj_src: float32 [50, 4096], P(None, ('row', 'col'))
- proj_tgt: float32 [50, 8192], P(None, ('row', 'col'))
All inputs are finite; a program needn't handle non-finite values.
Results may differ from a plain program's by a relative error of at most 0.0045.
Values may be sent and summed in bfloat16 or wider, within the bound.
No kernel may reach another device: no remote copies, remote signals or barrier semaphores. Data moves between devices by JAX's collectives and lax.ppermute only.
A program may use at most 64 MiB of HBM per device.

v0:
```python
import jax
import jax.numpy as jnp
from jax import lax
from jax.sharding import PartitionSpec as P

D = 50


EPSILON_KERNEL = 0.05


def kernel_rows(xb, xnb, coords, ynorm):
    cross = lax.dot_general(
        xb, coords, (((0,), (0,)), ((), ())), preferred_element_type=jnp.float32
    )
    return jnp.exp(-(xnb[:, None] + ynorm[None, :] - 2.0 * cross) / (2.0 * D * EPSILON_KERNEL))


def per_device(x_src, y_tgt, a_src, b_tgt):
    hi = lax.Precision.HIGHEST
    x_rows, marginal_entries_left = (
        lax.all_gather(x_src, "col", axis=1, tiled=True),
        lax.all_gather(a_src, "col", axis=0, tiled=True),
    )
    later_coordinate_entries, b_cols = (
        lax.all_gather(y_tgt, "row", axis=1, tiled=True),
        lax.all_gather(b_tgt, "row", axis=0, tiled=True),
    )
    marginal_entries_left = marginal_entries_left.astype(jnp.float32)
    b_cols = b_cols.astype(jnp.float32)
    xnorm = jnp.sum(jnp.square(x_rows.astype(jnp.float32)), axis=0)
    ynorm = jnp.sum(jnp.square(later_coordinate_entries.astype(jnp.float32)), axis=0)
    rows = x_rows.shape[1]
    block = min(512, rows)
    count = rows // block
    earlier_coordinate_pieces = x_rows.reshape(D, count, block).transpose(1, 0, 2)
    xn_blocks = xnorm.reshape(count, block)

    def earlier_factor_vector(later_dual_vector):

        def one(t):
            return jnp.dot(
                kernel_rows(t[0], t[1], later_coordinate_entries, ynorm),
                later_dual_vector,
                precision=hi,
            )

        local = lax.map(one, (earlier_coordinate_pieces, xn_blocks)).reshape(rows)
        total = lax.psum(local, "col")
        return marginal_entries_left / total

    def column_pass(earlier_dual_vector, with_num):
        u_blocks = earlier_dual_vector.reshape(count, block)

        def step(carry, t):
            xb, xnb, ub = t
            kern = kernel_rows(xb, xnb, later_coordinate_entries, ynorm)
            total = carry[0] + jnp.dot(ub, kern, precision=hi)
            if with_num:
                cell_weights = (ub[:, None] * kern).astype(jnp.bfloat16)
                numer = carry[1] + jnp.dot(xb, cell_weights, preferred_element_type=jnp.float32)
                return ((total, numer), None)
            return ((total, carry[1]), None)

        width = later_coordinate_entries.shape[1]
        numer_init = jnp.zeros((D, width) if with_num else (1,), jnp.float32)
        init = (jnp.zeros((width,), jnp.float32), numer_init)
        return lax.scan(step, init, (earlier_coordinate_pieces, xn_blocks, u_blocks))[0]

    def later_factor_vector(partial_aggregate_amount):
        total = lax.psum(partial_aggregate_amount, "row")
        return b_cols / total

    later_dual_vector = jnp.ones((later_coordinate_entries.shape[1],), jnp.float32)
    step = 0
    earlier_dual_vector = earlier_factor_vector(later_dual_vector)
    partial_aggregate_amount, unused = column_pass(earlier_dual_vector, False)
    later_dual_vector = later_factor_vector(partial_aggregate_amount)
    earlier_dual_vector = earlier_factor_vector(later_dual_vector)
    partial_aggregate_amount, unused = column_pass(earlier_dual_vector, False)
    later_dual_vector = later_factor_vector(partial_aggregate_amount)
    total_again, numer_local = column_pass(earlier_dual_vector, True)
    total, numer = lax.psum((total_again, numer_local), "row")
    share = total.shape[0] // lax.axis_size("row")
    start = lax.axis_index("row") * share
    own_total = lax.dynamic_slice_in_dim(total, start, share, 0)
    own_numer = lax.dynamic_slice_in_dim(numer, start, share, 1)
    proj_tgt = own_numer / own_total[None, :]

    def final(t):
        kern = kernel_rows(t[0], t[1], later_coordinate_entries, ynorm)
        den = jnp.dot(kern, later_dual_vector, precision=hi)
        cell_weights = (kern * later_dual_vector[None, :]).astype(jnp.bfloat16)
        num = lax.dot_general(
            later_coordinate_entries,
            cell_weights,
            (((1,), (1,)), ((), ())),
            preferred_element_type=jnp.float32,
        )
        return (den, num)

    dens, nums = lax.map(final, (earlier_coordinate_pieces, xn_blocks))
    den_local = dens.reshape(rows)
    num_local = nums.transpose(1, 0, 2).reshape(D, rows)
    den_all, num_all = lax.psum((den_local, num_local), "col")
    share = rows // lax.axis_size("col")
    start = lax.axis_index("col") * share
    own_den = lax.dynamic_slice_in_dim(den_all, start, share, 0)
    own_num = lax.dynamic_slice_in_dim(num_all, start, share, 1)
    proj_src = own_num / own_den[None, :]
    return (proj_src, proj_tgt)


def solution(mesh):
    return jax.shard_map(
        per_device,
        mesh=mesh,
        in_specs=(
            P(None, ("row", "col")),
            P(None, ("row", "col")),
            P(("row", "col")),
            P(("row", "col")),
        ),
        out_specs=(P(None, ("row", "col")), P(None, ("row", "col"))),
        check_vma=False,
    )
```

profile of v0, /device:TPU:0, one launch (start us, length us, event | category | flops | bytes accessed | tf_op | source)
XLA Modules:
  0.0 214.9 jit_solution(8043286846976220416)
XLA Ops:
  7.2 0.0 all-reduce.3.cloned.1.call-start
  7.2 11.4 %all_gather.13 = bf16[50,2048]{1,0:T(8,128)(2,1)S(1)} all-gather(bf16[50,256]{1,0:T(8,128)(2,1)} %param.5), channel_id=1, replica_groups=mesh['row'=8,'col'=4] {'row'}, dimensions={1}, use_global_device_ids=true | all-gather | bytes 230400 | tf_op jit(solution)/shard_map/all_gather | solution.py:26
  18.6 12.4 %all_gather.12 = bf16[50,512]{1,0:T(8,128)(2,1)S(1)} all-gather(bf16[50,128]{1,0:T(8,128)(2,1)} %param.4), channel_id=1, replica_groups=mesh['row'=8,'col'=4] {'col'}, dimensions={1}, use_global_device_ids=true | all-gather | bytes 64000 | tf_op jit(solution)/shard_map/all_gather | solution.py:22
  31.0 0.1 multiply_reduce_fusion
  31.1 0.7 reshape.30
  31.7 8.7 %all-gather = bf16[8,1,256]{2,1,0:T(2,128)(2,1)S(1)} all-gather(bf16[1,1,256]{2,1,0:T(2,128)(2,1)S(1)} %reshape.30), channel_id=1, replica_groups=mesh['row'=8,'col'=4] {'row'}, dimensions={0}, use_global_device_ids=true | all-gather | bytes 4608 | tf_op jit(solution)/shard_map/all_gather | solution.py:27
  40.4 10.0 %all-gather.1 = bf16[4,1,128]{2,1,0:T(2,128)(2,1)S(1)} all-gather(bf16[1,1,128]{2,1,0:T(2,128)(2,1)} %bitcast.42), channel_id=1, replica_groups=mesh['row'=8,'col'=4] {'col'}, dimensions={0}, use_global_device_ids=true | all-gather | bytes 1280 | tf_op jit(solution)/shard_map/all_gather | solution.py:23
  50.3 1.1 multiply_exponential_fusion
  51.5 0.0 copy-start
  51.5 1.9 copy-done
  53.4 3.6 %fusion.4 = f32[1,512]{1,0:T(1,128)S(1)} fusion(f32[512,2048]{1,0:T(8,128)S(1)} %multiply_exponential_fusion), kind=kOutput, calls=%fused_computation.12 | convolution fusion | flops 12582912 | bytes 4196352 | tf_op jit(solution)/shard_map/while/body/eval_jaxpr/dot_general | solution.py:42
  57.0 8.4 %psum.52 = f32[512]{0:T(512)S(1)} all-reduce(f32[512]{0:T(512)S(1)} %bitcast.41), channel_id=1, replica_groups=mesh['row'=8,'col'=4] {'col'}, use_global_device_ids=true, to_apply=%region_2.3 | all-reduce | flops 512 | bytes 4096 | tf_op jit(solution)/shard_map/psum | solution.py:49
  65.4 4.3 %fusion.7 = f32[1,2048]{1,0:T(1,128)S(1)} fusion(f32[512,1]{0,1:T(1,128)S(1)} %bitcast.38, f32[512,2048]{1,0:T(8,128)} %copy-done), kind=kOutput, calls=%fused_computation.15 | convolution fusion | flops 12582912 | bytes 4204544 | tf_op jit(solution)/shard_map/while/body/eval_jaxpr/dot_general | solution.py:58
  69.7 12.0 %psum.53 = f32[2048]{0:T(1024)S(1)} all-reduce(f32[2048]{0:T(1024)S(1)} %bitcast.33), channel_id=1, replica_groups=mesh['row'=8,'col'=4] {'row'}, use_global_device_ids=true, to_apply=%region_3.4 | all-reduce | flops 2048 | bytes 16384 | tf_op jit(solution)/shard_map/psum | solution.py:71
  81.7 5.8 %fusion.8 = f32[1,512]{1,0:T(1,128)S(1)} fusion(f32[512,2048]{1,0:T(8,128)} %copy-done, f32[2048,1]{0,1:T(1,128)S(1)} %bitcast.32), kind=kOutput, calls=%fused_computation.16 | convolution fusion | flops 12582912 | bytes 4204544 | tf_op jit(solution)/shard_map/while/body/eval_jaxpr/dot_general | solution.py:42
  87.5 10.5 %psum.54 = f32[512]{0:T(512)S(1)} all-reduce(f32[512]{0:T(512)S(1)} %bitcast.40), channel_id=1, replica_groups=mesh['row'=8,'col'=4] {'col'}, use_global_device_ids=true, to_apply=%region_4.5 | all-reduce | flops 512 | bytes 4096 | tf_op jit(solution)/shard_map/psum | solution.py:49
  98.0 4.3 %fusion.9 = f32[1,2048]{1,0:T(1,128)S(1)} fusion(f32[512,1]{0,1:T(1,128)S(1)} %bitcast.35, f32[512,2048]{1,0:T(8,128)} %copy-done), kind=kOutput, calls=%fused_computation.17 | convolution fusion | flops 12582912 | bytes 4204544 | tf_op jit(solution)/shard_map/while/body/eval_jaxpr/dot_general | solution.py:58
  102.3 12.1 %psum.55 = f32[2048]{0:T(1024)S(1)} all-reduce(f32[2048]{0:T(1024)S(1)} %bitcast.34), channel_id=1, replica_groups=mesh['row'=8,'col'=4] {'row'}, use_global_device_ids=true, to_apply=%region_5.6 | all-reduce | flops 2048 | bytes 16384 | tf_op jit(solution)/shard_map/psum | solution.py:71
  114.4 3.6 %fusion.3 = f32[50,512]{1,0:T(8,128)} fusion(bf16[50,2048]{1,0:T(8,128)(2,1)S(1)} %all_gather.13, f32[512,2048]{1,0:T(8,128)} %copy-done, f32[2048]{0:T(1024)S(1)} %div.46), kind=kOutput, calls=%fused_computation.7 | convolution fusion | flops 106954752 | bytes 4509696 | tf_op jit(solution)/shard_map/while/body/eval_jaxpr/dot_general | solution.py:94
  118.0 0.0 all-reduce.3.cloned.1.call-update
  118.1 0.0 all-reduce.5.cloned.1.call-start
  118.1 3.5 %convolution_bitcast_fusion = f32[50,2048]{1,0:T(8,128)} fusion(bf16[50,512]{1,0:T(8,128)(2,1)S(1)} %all_gather.12, f32[512,2048]{1,0:T(8,128)} %copy-done, f32[512]{0:T(512)S(1)} %div.45), kind=kOutput, calls=%fused_computation.3 | convolution fusion | flops 106954752 | bytes 4657152 | tf_op jit(solution)/shard_map/while/body/eval_jaxpr/dot_general | solution.py:61
  121.6 0.0 all-reduce.5.cloned.1.call-update
  121.7 5.8 %fusion.10 = f32[1,512]{1,0:T(1,128)S(1)} fusion(f32[512,2048]{1,0:T(8,128)} %copy-done, f32[2048,1]{0,1:T(1,128)S(1)} %bitcast.29), kind=kOutput, calls=%fused_computation.18 | convolution fusion | flops 12582912 | bytes 4204544 | tf_op jit(solution)/shard_map/while/body/eval_jaxpr/dot_general | solution.py:92
  127.4 8.4 %psum.57 = f32[512]{0:T(512)S(1)} all-reduce(f32[512]{0:T(512)S(1)} %bitcast.39), channel_id=1, replica_groups=mesh['row'=8,'col'=4] {'col'}, use_global_device_ids=true, to_apply=%region_7.8 | all-reduce | flops 512 | bytes 4096 | tf_op jit(solution)/shard_map/psum | solution.py:105
  135.8 0.1 dynamic_slice.47
  135.9 0.1 dynamic_slice.45
  136.0 12.9 %all-reduce.3.cloned.1.call-done = f32[50,512]{1,0:T(8,128)} async-done(((f32[50,512]{1,0:T(8,128)}), f32[50,512]{1,0:T(8,128)}) %all-reduce.3.cloned.1.call-update) | async-done | bytes 102416 | tf_op jit(solution)/shard_map/psum | solution.py:105
  148.8 1.4 dynamic-slice_divide_fusion.1
  150.2 56.5 %all-reduce.5.cloned.1.call-done = f32[50,2048]{1,0:T(8,128)} async-done(((f32[50,2048]{1,0:T(8,128)}), f32[50,2048]{1,0:T(8,128)}) %all-reduce.5.cloned.1.call-update) | async-done | bytes 409616 | tf_op jit(solution)/shard_map/psum | solution.py:83
  206.6 1.5 dynamic-slice_divide_fusion
  (7 shorter events, 0.1 us)
Async XLA Ops:
  7.2 141.6 %all-reduce.3.cloned.1.call-start = ((), (), s32[]{:S(2)}) async-start(), calls=%async_computation | async-start | bytes 229376 | tf_op jit(solution)/shard_map/psum | solution.py:105
  51.5 1.9 copy-start
  118.1 88.6 %all-reduce.5.cloned.1.call-start = ((), (), s32[]{:S(2)}) async-start(), calls=%async_computation.1 | async-start | bytes 917504 | tf_op jit(solution)/shard_map/psum | solution.py:83
Sparse Core Ops, SparseCore 0:
  118.2 30.5 all-reduce.2
  152.2 54.3 all-reduce.4
where the time goes:
time: 216 us; the launch traced here: 215 us
  blocking collectives  93.7 us (43%)
  waiting for transfers between devices  69.3 us (32%)
  matrix products  32 us (15%)
  between operations  14.1 us (7%)
  other arithmetic  2.95 us (1%)
  local copies, waits for them, and re-layouts  2.73 us (1%)
    psum x1, waiting for transfers between devices, per_device(): total, numer = lax.psum((total_again, numer_local), 'row')  56.5 us
    psum x2, blocking collectives, later_factor_vector(): total = lax.psum(partial_aggregate_amount, 'row')  24.1 us
    psum x2, blocking collectives, earlier_factor_vector(): total = lax.psum(local, 'col')  18.9 us
    psum x1, waiting for transfers between devices, per_device(): den_all, num_all = lax.psum((den_local, num_local), 'col')  12.9 us
    all_gather x1, blocking collectives, per_device(): lax.all_gather(x_src, 'col', axis=1, tiled=True)  12.4 us
    all_gather x1, blocking collectives, per_device(): lax.all_gather(y_tgt, 'row', axis=1, tiled=True)  11.4 us
    all_gather x1, blocking collectives, per_device(): lax.all_gather(a_src, 'col', axis=0, tiled=True)  9.95 us
    dot_general x2, matrix products, one(): jnp.dot(kernel_rows(t[0], t[1], later_coordinate_entries, ynorm), later_d...  9.38 us
  transfers between devices with their start and end apart: 2, of which 2 were waited for; matrix products, arithmetic and copies ran while one was open for 5% of the time, Pallas kernels for 0%

commit v1 on v0

v1 whole, which is shorter than its diff:
```python
import jax
import jax.numpy as jnp
import numpy as np
from jax import lax
from jax.experimental import pallas as pl
from jax.experimental.pallas import tpu as pltpu
from jax.sharding import PartitionSpec as P

D = 50
EPSILON_KERNEL = 0.05
SCALE = float(2.0 / (2.0 * D * EPSILON_KERNEL) / np.log(2.0))
EXT = 56
NORM_X, NORM_Y, B_ROW, A_ROW = D, D + 2, D + 4, D + 5

f32 = jnp.float32
bf16 = jnp.bfloat16
VM = pl.BlockSpec(memory_space=pltpu.VMEM)
SM = pl.BlockSpec(memory_space=pltpu.SMEM)


def params():
    return pltpu.CompilerParams(vmem_limit_bytes=40 * 2**20)


def ext_kernel(x_ref, y_ref, a_ref, b_ref, o_ref, sx, sy):
    nx = x_ref.shape[1]
    for src, w, s, norm, one, w_row in (
        (x_ref, a_ref, sx, NORM_X, NORM_Y, A_ROW),
        (y_ref, b_ref, sy, NORM_Y, NORM_X, B_ROW),
    ):
        c = src[...].astype(f32)
        n = -0.5 * jnp.sum(c * c, axis=0, keepdims=True)
        hi = n.astype(bf16).astype(f32)
        s[...] = jnp.zeros_like(s)
        s[0:D, :] = c
        s[norm : norm + 1, :] = hi
        s[norm + 1 : norm + 2, :] = n - hi
        s[one : one + 2, :] = jnp.ones((2, s.shape[1]), f32)
        s[w_row : w_row + 1, :] = w[...].astype(f32)
    o_ref[:, 0:nx] = sx[...].astype(bf16)
    o_ref[:, nx:] = sy[...].astype(bf16)


def kernel_block(xt, y):
    s = lax.dot_general(xt, y, (((1,), (0,)), ((), ())), preferred_element_type=f32)
    return jnp.exp2(s * SCALE)


def add_lanes(acc, e):
    for t in range(e.shape[1] // 128):
        acc = acc + e[:, t * 128 : (t + 1) * 128]
    return acc


def make_blocks(xt, ys, ks, acc):
    for i, y in enumerate(ys):
        e = kernel_block(xt, y[...])
        if ks:
            ks[i][...] = e
        acc = add_lanes(acc, e)
    return acc


def block(i, ks, xt_ref, ys, rows=slice(None), cols=slice(None)):
    if ks:
        return ks[i][rows, cols]
    return kernel_block(xt_ref[rows, :], ys[i][:, cols])


def first_kernel(n, xe_ref, *refs):
    ys, (xt_ref, acc_ref), ks = refs[:n], refs[n : n + 2], refs[n + 2 :]
    xt = jnp.transpose(xe_ref[...].astype(f32)).astype(bf16)
    xt_ref[...] = xt
    acc_ref[...] = make_blocks(xt, ys, ks, jnp.zeros(acc_ref.shape, f32))


def next_kernel(n, xt_ref, acc0_ref, *refs):
    ys, acc_ref, ks = refs[:n], refs[n], refs[n + 1 :]
    acc_ref[...] = make_blocks(xt_ref[...], ys, ks, acc0_ref[...])


def col_sums(rows, ks, xt_ref, ys, u, tot, r):
    for i in range(rows):
        e = block(i, ks, xt_ref, ys)
        tot[pl.ds(r ^ i, 1), :] = jnp.sum(e * u, axis=0, keepdims=True)


def last_kernel(n, rows, kept, r_ref, xt_ref, acc0_ref, *refs):
    n_y = n if kept else rows
    n_k = rows - n if kept else 0
    ys, old = refs[:n_y], refs[n_y : n_y + n_k]
    o_ref, new, tot = refs[n_y + n_k], refs[n_y + n_k + 1 : -1], refs[-1]
    late = range(3, rows, 2)
    acc = make_blocks(xt_ref[...], ys[-n:], new, acc0_ref[...])
    ks = [None] * rows if kept else ()
    if kept:
        for i, k in zip([0, 1, *range(2, rows, 2), *late], [*old, *new]):
            ks[i] = k
    else:
        ys = order(ys, rows)
    u = xt_ref[:, A_ROW : A_ROW + 1].astype(f32) / jnp.sum(acc, axis=1, keepdims=True)
    col_sums(rows, ks, xt_ref, ys, u, tot, r_ref[0])
    t = tot[...].astype(bf16)
    for e in range(rows):
        o_ref[e] = t


def order(blocks, rows):
    made = [0, 1, *range(2, rows, 2), *range(3, rows, 2)]
    return [blocks[made.index(i)] for i in range(rows)]


def second_kernel(rows, own, width, r_ref, got_ref, xt_ref, xe_ref, *refs):
    ys, ks = refs[:rows], refs[rows:-2]
    o_ref, tot = refs[-2:]
    r = r_ref[0]
    tot[...] = jnp.sum(got_ref[...].astype(f32), axis=0)
    acc = jnp.zeros((xt_ref.shape[0], 128), f32)
    for i in range(rows):
        v = ys[i][B_ROW : B_ROW + 1, :].astype(f32) / tot[pl.ds(r ^ i, 1), :]
        acc = add_lanes(acc, block(i, ks, xt_ref, ys) * v)
    u = xt_ref[:, A_ROW : A_ROW + 1].astype(f32) / jnp.sum(acc, axis=1, keepdims=True)
    col_sums(rows, ks, xt_ref, ys, u, tot, r)
    t = jnp.concatenate(
        [tot[:, g : g + width] for g in range(0, tot.shape[1], width)], axis=0
    ).astype(bf16)
    x = xe_ref[...]
    for i in range(rows):
        z = (block(i, ks, xt_ref, ys, cols=slice(0, own)) * u).astype(bf16)
        num = jnp.dot(x, z, preferred_element_type=f32)
        o_ref[r ^ i, 0 : t.shape[0], :] = t
        o_ref[r ^ i, t.shape[0] :, 0:own] = num.astype(bf16)


def final_kernel(rows, own_x, own, width, r_ref, got_ref, xt_ref, *refs):
    ys, ks = refs[:rows], refs[rows:-4]
    src_ref, tgt_ref, tot, num_s = refs[-4:]
    r = r_ref[0]
    s = jnp.sum(got_ref[...].astype(f32), axis=0)
    for g in range(tot.shape[1] // width):
        tot[:, g * width : (g + 1) * width] = s[g * rows : (g + 1) * rows, :]
    num_s[...] = s[rows * tot.shape[1] // width :, 0:own]
    tgt_ref[...] = num_s[0:D, :] / tot[pl.ds(r, 1), :][:, 0:own]
    num = jnp.zeros((EXT, own_x), f32)
    for i in range(rows):
        v = ys[i][B_ROW : B_ROW + 1, :].astype(f32) / tot[pl.ds(r ^ i, 1), :]
        w = (block(i, ks, xt_ref, ys, rows=slice(0, own_x)) * v).astype(bf16)
        num = num + lax.dot_general(
            ys[i][...], w, (((1,), (1,)), ((), ())), preferred_element_type=f32
        )
    src_ref[...] = num[0:D, :] / num[NORM_X : NORM_X + 1, :]


def xor_perm(n, m):
    return [(i, i ^ m) for i in range(n)]


def solution(mesh):
    rows, cols = mesh.shape["row"], mesh.shape["col"]

    def per_device(x_src, y_tgt, a_src, b_tgt):
        nx, ny = x_src.shape[1], y_tgt.shape[1]
        S, T = nx * cols, ny * cols
        kept = S * T * rows * 4 <= 24 * 2**20

        def held(shape, dtype):
            if kept:
                return pltpu.VMEM(shape, dtype)
            return jax.ShapeDtypeStruct(shape, dtype)

        def call(kernel, outs, n_in, scratch=(), smem=0, cost=None):
            return pl.pallas_call(
                kernel,
                out_shape=outs,
                in_specs=[SM] * smem + [VM] * n_in,
                out_specs=jax.tree.map(lambda _: VM, outs),
                scratch_shapes=scratch,
                compiler_params=params(),
                cost_estimate=cost,
            )

        r = lax.axis_index("row").astype(jnp.int32).reshape(1)
        p = call(
            ext_kernel,
            jax.ShapeDtypeStruct((EXT, nx + ny), bf16),
            4,
            [pltpu.VMEM((EXT, nx), f32), pltpu.VMEM((EXT, ny), f32)],
        )(x_src, y_tgt, a_src.reshape(1, nx), b_tgt.reshape(1, ny))
        ps = [p] + [
            lax.ppermute(p, "col", xor_perm(cols, m)) for m in range(1, cols)
        ]
        y = [None] * rows
        y[0] = jnp.concatenate([q[:, nx:] for q in ps], axis=1)
        for m in range(2, rows, 2):
            y[m] = lax.ppermute(y[0], "row", xor_perm(rows, m))
        for m in range(0, rows, 2):
            y[m + 1] = lax.ppermute(y[m], "row", xor_perm(rows, 1))
        xe = jnp.concatenate([q[:, :nx] for q in ps], axis=1)

        def cost(n):
            return pl.CostEstimate(
                flops=2 * EXT * S * T * n,
                bytes_accessed=S * T * n,
                transcendentals=S * T * n,
            )

        acc_t = held((S, 128), f32)
        k_t = held((S, T), f32)
        k_n = 1 if kept else 0
        n = rows // 2 - 1
        evens, odds = range(2, rows, 2), range(3, rows, 2)
        xt, acc, *made = call(
            lambda *refs: first_kernel(2, *refs),
            (held((S, EXT), bf16), acc_t) + (k_t,) * (2 * k_n),
            3,
            cost=cost(2),
        )(xe, y[0], y[1])
        acc, *new = call(
            lambda *refs: next_kernel(n, *refs),
            (acc_t,) + (k_t,) * (n * k_n),
            2 + n,
            cost=cost(n),
        )(xt, acc, *[y[m] for m in evens])
        made += new
        late = [y[m] for m in odds]
        if not kept:
            late = [y[0], y[1]] + [y[m] for m in evens] + late
        send, *new = call(
            lambda *refs: last_kernel(n, rows, kept, *refs),
            (jax.ShapeDtypeStruct((rows, rows, T), bf16),) + (k_t,) * (n * k_n),
            2 + len(late) + len(made),
            [pltpu.VMEM((rows, T), f32)],
            smem=1,
            cost=cost(n),
        )(r, xt, acc, *late, *made)
        ks = order(made + new, rows) if kept else []
        got = lax.all_to_all(send, "row", 0, 0)
        width = max(ny, 128)
        n_tot = rows * T // width
        send = call(
            lambda *refs: second_kernel(rows, ny, width, *refs),
            jax.ShapeDtypeStruct((rows, n_tot + EXT, width), bf16),
            3 + rows + len(ks),
            [pltpu.VMEM((rows, T), f32)],
            smem=1,
        )(r, got, xt, xe, *y, *ks)
        got = lax.all_to_all(send, "row", 0, 0)
        return tuple(
            call(
                lambda *refs: final_kernel(rows, nx, ny, width, *refs),
                (
                    jax.ShapeDtypeStruct((D, nx), f32),
                    jax.ShapeDtypeStruct((D, ny), f32),
                ),
                2 + rows + len(ks),
                [pltpu.VMEM((rows, T), f32), pltpu.VMEM((EXT, ny), f32)],
                smem=1,
            )(r, got, xt, *y, *ks)
        )

    spec = P(None, ("row", "col"))
    vec = P(("row", "col"))
    return jax.shard_map(
        per_device,
        mesh=mesh,
        in_specs=(spec, spec, vec, vec),
        out_specs=(spec, spec),
        check_vma=False,
    )
```

time: 216 us -> 61.8 us (0.29)
  blocking collectives: 93.7 us -> 18.3 us
  waiting for transfers between devices: 69.3 us -> 8.5 us
  matrix products: 32 us -> 0 us
  Pallas kernels: 0 us -> 17.3 us
  between operations: 14.1 us -> 0.79 us
  starting transfers between devices: 0.08 us -> 9.78 us
  local copies, waits for them, and re-layouts: 2.73 us -> 6.76 us
  other arithmetic: 2.95 us -> 0.02 us
    psum x2 -> x0, waiting for transfers between devices: 69.3 us -> none  [the longest x1 56.5 us: per_device(): total, numer = lax.psum((total_again, numer_local), 'row')]
    psum x5 -> x0, blocking collectives: 51.4 us -> none  [the longest x2 24.1 us: later_factor_vector(): total = lax.psum(partial_aggregate_amount, 'row')]
    all_gather x4 -> x0, blocking collectives: 42.3 us -> none  [the longest x1 12.4 us: per_device(): lax.all_gather(x_src, 'col', axis=1, tiled=True)]
    dot_general x8 -> x0, matrix products: 32 us -> none  [the longest x2 9.38 us: one(): jnp.dot(kernel_rows(t[0], t[1], later_coordinate_entries, ynorm), later_d...]
    all_to_all x0 -> x2, blocking collectives: none -> 18.3 us  [per_device(): got = lax.all_to_all(send, 'row', 0, 0)]
    pallas_call x0 -> x6, Pallas kernels: none -> 17.3 us  [the longest x1 6.47 us: per_device(): call(lambda *refs: second_kernel(rows, ny, width, *refs), jax.ShapeDtypeS...]
    ppermute x0 -> x10, starting transfers between devices: none -> 9.78 us  [the longest x3 5.75 us: per_device(): lax.ppermute(p, 'col', xor_perm(cols, m))]
    ppermute x0 -> x10, waiting for transfers between devices: none -> 8.5 us  [the longest x3 4.27 us: per_device(): lax.ppermute(p, 'col', xor_perm(cols, m))]
  transfers between devices with their start and end apart: 2 -> 10, of which waited for: 2 -> 4; matrix products, arithmetic and copies ran while one was open for 5% -> 0% of each run, Pallas kernels for 0% -> 3%
where the time goes in v1:
time: 61.8 us; the launch traced here: 61.5 us
  blocking collectives  18.3 us (30%)
  Pallas kernels  17.3 us (28%)
  starting transfers between devices  9.78 us (16%)
  waiting for transfers between devices  8.5 us (14%)
  local copies, waits for them, and re-layouts  6.76 us (11%)
  between operations  0.79 us (1%)
    all_to_all x2, blocking collectives, per_device(): got = lax.all_to_all(send, 'row', 0, 0)  18.3 us
    pallas_call x1, Pallas kernels, per_device(): call(lambda *refs: second_kernel(rows, ny, width, *refs), jax.ShapeDtypeS...  6.47 us
    unnamed x22, local copies, waits for them, and re-layouts  6.08 us
    ppermute x3, starting transfers between devices, per_device(): lax.ppermute(p, 'col', xor_perm(cols, m))  5.75 us
    pallas_call x1, Pallas kernels, per_device(): call(lambda *refs: last_kernel(n, rows, kept, *refs), (jax.ShapeDtypeStru...  5.35 us
    ppermute x3, waiting for transfers between devices, per_device(): lax.ppermute(p, 'col', xor_perm(cols, m))  4.27 us
    ppermute x3, waiting for transfers between devices, per_device(): y[m] = lax.ppermute(y[0], 'row', xor_perm(rows, m))  4.21 us
    pallas_call x1, Pallas kernels, per_device(): call(lambda *refs: final_kernel(rows, nx, ny, width, *refs), (jax.ShapeDt...  3.74 us
  transfers between devices with their start and end apart: 10, of which 4 were waited for; matrix products, arithmetic and copies ran while one was open for 0% of the time, Pallas kernels for 3%

profile of v1, /device:TPU:0, one launch (start us, length us, event | category | flops | bytes accessed | tf_op | source)
XLA Modules:
  0.0 61.5 jit_solution(8102870837057657393)
XLA Ops:
  0.6 0.7 %reshape.15.b_ref = bf16[1,256]{1,0:T(2,128)(2,1)S(1)} reshape(bf16[256]{0:T(256)(128)(2,1)} %param.7) | data formatting | bytes 1024 | tf_op jit(solution)/shard_map/reshape | solution.py:188
  1.3 0.7 %copy-done.8 = bf16[50,256]{1,0:T(8,128)(2,1)S(1)} copy-done((bf16[50,256]{1,0:T(8,128)(2,1)S(1)}, bf16[50,256]{1,0:T(8,128)(2,1)}, u32[]{:S(2)}) %copy-start.8) | copy-done | bytes 25624
  2.0 0.7 %copy-done.9 = bf16[50,128]{1,0:T(8,128)(2,1)S(1)} copy-done((bf16[50,128]{1,0:T(8,128)(2,1)S(1)}, bf16[50,128]{1,0:T(8,128)(2,1)}, u32[]{:S(2)}) %copy-start.9) | copy-done | bytes 12824
  2.8 0.7 %copy-done.10 = bf16[128]{0:T(256)(128)(2,1)S(1)} copy-done((bf16[128]{0:T(256)(128)(2,1)S(1)}, bf16[128]{0:T(256)(128)(2,1)}, u32[]{:S(2)}) %copy-start.10) | copy-done | bytes 280
  3.4 5.1 %collective-permute-start.2 = (bf16[56,384]{1,0:T(8,128)(2,1)S(1)}, bf16[56,384]{1,0:T(8,128)(2,1)S(1)}, u32[]{:S(2)}, u32[]{:S(2)}) collective-permute-start(bf16[56,384]{1,0:T(8,128)(2,1)S(1)} %shard_map.59), channel_id=1, source_target_pairs={{0,3},{1,2},{2,1},{3,0},{4,7},{5,6},{6,5},{7,4},{8,11},{9,10},{10,... | collective-permute-start | bytes 129032 | tf_op jit(solution)/shard_map/ppermute | solution.py:190
  8.6 0.0 collective-permute-start.1
  8.6 0.6 %collective-permute-start = (bf16[56,384]{1,0:T(8,128)(2,1)S(1)}, bf16[56,384]{1,0:T(8,128)(2,1)S(1)}, u32[]{:S(2)}, u32[]{:S(2)}) collective-permute-start(bf16[56,384]{1,0:T(8,128)(2,1)S(1)} %shard_map.59), channel_id=1, source_target_pairs={{0,1},{1,0},{2,3},{3,2},{4,5},{5,4},{6,7},{7,6},{8,9},{9,8},{10,11... | collective-permute-start | bytes 129032 | tf_op jit(solution)/shard_map/ppermute | solution.py:190
  9.2 1.4 %collective-permute-done.2 = bf16[56,384]{1,0:T(8,128)(2,1)S(1)} collective-permute-done((bf16[56,384]{1,0:T(8,128)(2,1)S(1)}, bf16[56,384]{1,0:T(8,128)(2,1)S(1)}, u32[]{:S(2)}, u32[]{:S(2)}) %collective-permute-start.2) | collective-permute-done | bytes 43040 | tf_op jit(solution)/shard_map/ppermute | solution.py:190
  10.6 2.9 %collective-permute-done.1 = bf16[56,384]{1,0:T(8,128)(2,1)S(1)} collective-permute-done((bf16[56,384]{1,0:T(8,128)(2,1)S(1)}, bf16[56,384]{1,0:T(8,128)(2,1)S(1)}, u32[]{:S(2)}, u32[]{:S(2)}) %collective-permute-start.1) | collective-permute-done | bytes 43040 | tf_op jit(solution)/shard_map/ppermute | solution.py:190
  13.5 0.0 collective-permute-done
  13.5 2.5 %collective-permute-start.6 = (bf16[56,1024]{1,0:T(8,128)(2,1)S(1)}, bf16[56,1024]{1,0:T(8,128)(2,1)S(1)}, u32[]{:S(2)}, u32[]{:S(2)}) collective-permute-start(bf16[56,1024]{1,0:T(8,128)(2,1)S(1)} %pad_maximum_fusion.refs_1_.refs_4_.refs_3_), channel_id=1, source_target_pairs={{0,24},{4,28},{8,16},{12,20},{16,8},{20,12},{24,0},{28,4},{1,25},{... | collective-permute-start | bytes 344072 | tf_op jit(solution)/shard_map/ppermute | solution.py:195
  16.0 0.5 collective-permute-start.5
  16.5 0.5 collective-permute-start.4
  17.1 0.0 collective-permute-start.3
  17.1 3.4 %collective-permute-done.6.refs_4_.refs_10_.refs_9_ = bf16[56,1024]{1,0:T(8,128)(2,1)S(1)} collective-permute-done((bf16[56,1024]{1,0:T(8,128)(2,1)S(1)}, bf16[56,1024]{1,0:T(8,128)(2,1)S(1)}, u32[]{:S(2)}, u32[]{:S(2)}) %collective-permute-start.6) | collective-permute-done | bytes 114720 | tf_op jit(solution)/shard_map/ppermute | solution.py:195
  20.5 0.0 collective-permute-start.9
  20.5 0.8 %collective-permute-done.5.refs_3_.refs_8_.refs_7_ = bf16[56,1024]{1,0:T(8,128)(2,1)S(1)} collective-permute-done((bf16[56,1024]{1,0:T(8,128)(2,1)S(1)}, bf16[56,1024]{1,0:T(8,128)(2,1)S(1)}, u32[]{:S(2)}, u32[]{:S(2)}) %collective-permute-start.5) | collective-permute-done | bytes 114720 | tf_op jit(solution)/shard_map/ppermute | solution.py:195
  21.3 0.0 collective-permute-done.4.refs_2_.refs_6_.refs_5_
  21.3 0.5 collective-permute-start.7
  21.8 0.8 %shard_map.60 = (bf16[512,56]{1,0:T(8,128)(2,1)S(1)}, f32[512,128]{1,0:T(8,128)S(1)}, f32[512,1024]{1,0:T(8,128)S(1)}, f32[512,1024]{1,0:T(8,128)S(1)}) custom-call(bf16[56,512]{1,0:T(8,128)(2,1)S(1)} %pad_maximum_fusion.1.refs_0_.refs_3_, bf16[56,1024]{1,0:T(8,128)(2,1)S(1)} %pad_maximum_fusion.refs_1_.refs_4_.refs_3_, ...), custom_call_target="tpu_custom_call" | custom-call | flops 117440512 | bytes 1048576 | tf_op jit(solution)/shard_map/pallas_call | solution.py:212
  22.6 1.0 %shard_map.61 = (f32[512,128]{1,0:T(8,128)S(1)}, f32[512,1024]{1,0:T(8,128)S(1)}, f32[512,1024]{1,0:T(8,128)S(1)}, f32[512,1024]{1,0:T(8,128)S(1)}) custom-call(bf16[512,56]{1,0:T(8,128)(2,1)S(1)} %get-tuple-element.14.refs_0_.refs_1_.refs_2_, f32[512,128]{1,0:T(8,128)S(1)} %get-tuple-element.15.refs_1_, ...), custom_call_target="tpu_custom_call" | custom-call | flops 176160768 | bytes 1572864 | tf_op jit(solution)/shard_map/pallas_call | solution.py:218
  23.6 1.3 %copy-done = f32[512,1024]{1,0:T(8,128)} copy-done((f32[512,1024]{1,0:T(8,128)}, f32[512,1024]{1,0:T(8,128)S(1)}, u32[]{:S(2)}) %copy-start) | copy-done | bytes 2097176
  24.9 1.3 %copy-done.2 = f32[512,1024]{1,0:T(8,128)} copy-done((f32[512,1024]{1,0:T(8,128)}, f32[512,1024]{1,0:T(8,128)S(1)}, u32[]{:S(2)}) %copy-start.2) | copy-done | bytes 2097176
  26.3 0.0 collective-permute-done.9.refs_5_.refs_11_.refs_10_
  26.3 0.0 collective-permute-done.8.refs_4_.refs_9_.refs_8_
  26.3 0.0 collective-permute-done.7.refs_3_.refs_7_.refs_6_
  26.3 5.4 %shard_map.62 = (bf16[8,8,1024]{2,1,0:T(8,128)(2,1)S(1)}, f32[512,1024]{1,0:T(8,128)S(1)}, f32[512,1024]{1,0:T(8,128)S(1)}, f32[512,1024]{1,0:T(8,128)S(1)}) custom-call(s32[1]{0:T(128)} %bitcast.refs_0_, bf16[512,56]{1,0:T(8,128)(2,1)S(1)} %get-tuple-element.14.refs_0_.refs_1_.refs_2_, f32[512,128]{1,0:T(8,128)S(1)} %get-tuple-element.16.refs_2_, ...), custom_call_target="tpu_custom_call" | custom-call | flops 176160768 | bytes 1572864 | tf_op jit(solution)/shard_map/pallas_call | solution.py:228
  31.7 1.3 %copy-done.3 = f32[512,1024]{1,0:T(8,128)} copy-done((f32[512,1024]{1,0:T(8,128)}, f32[512,1024]{1,0:T(8,128)S(1)}, u32[]{:S(2)}) %copy-start.3) | copy-done | bytes 2097176
  33.0 7.9 %all_to_all.10.refs_1_ = bf16[8,8,1024]{2,1,0:T(8,128)(2,1)S(1)} all-to-all(bf16[8,8,1024]{2,1,0:T(8,128)(2,1)S(1)} %get-tuple-element.22), channel_id=1, replica_groups=mesh['row'=8,'col'=4] {'row'}, dimensions={0} | all-to-all | bytes 262144 | tf_op jit(solution)/shard_map/all_to_all | solution.py:237
  40.9 6.5 %shard_map.63 = bf16[8,88,256]{2,1,0:T(8,128)(2,1)S(1)} custom-call(s32[1]{0:T(128)} %bitcast.refs_0_, bf16[8,8,1024]{2,1,0:T(8,128)(2,1)S(1)} %all_to_all.10.refs_1_, bf16[512,56]{1,0:T(8,128)(2,1)S(1)} %get-tuple-element.14.refs_0_.refs_1_.refs_2_, bf16[56,512]{1,0:T(8,128)(2,1)S(1)} %pad_maximum_fusion.1.refs_0_.refs_3_, ...), custom_call_target="tpu_custom_call" | custom-call | tf_op jit(solution)/shard_map/pallas_call | solution.py:240
  47.4 10.4 %all_to_all.11.refs_1_ = bf16[8,88,256]{2,1,0:T(8,128)(2,1)S(1)} all-to-all(bf16[8,88,256]{2,1,0:T(8,128)(2,1)S(1)} %shard_map.63), channel_id=1, replica_groups=mesh['row'=8,'col'=4] {'row'}, dimensions={0} | all-to-all | bytes 720896 | tf_op jit(solution)/shard_map/all_to_all | solution.py:247
  57.7 3.7 %shard_map.64 = (f32[50,128]{1,0:T(8,128)}, f32[50,256]{1,0:T(8,128)}) custom-call(s32[1]{0:T(128)} %bitcast.refs_0_, bf16[8,88,256]{2,1,0:T(8,128)(2,1)S(1)} %all_to_all.11.refs_1_, bf16[512,56]{1,0:T(8,128)(2,1)S(1)} %get-tuple-element.14.refs_0_.refs_1_.refs_2_, bf16[56,1024]{1,0:T(8,128)(2,1)S(1)} %pad_maximum_fusion.refs_1_.refs_4_.refs_3_, ...), custom_call_target="tpu_custom_call" | custom-call | tf_op jit(solution)/shard_map/pallas_call | solution.py:249
  (29 shorter events, 0.1 us)
Async XLA Ops:
  1.3 0.7 %copy-start.8 = (bf16[50,256]{1,0:T(8,128)(2,1)S(1)}, bf16[50,256]{1,0:T(8,128)(2,1)}, u32[]{:S(2)}) copy-start(bf16[50,256]{1,0:T(8,128)(2,1)} %y_ref.1) | copy-start | bytes 76804
  2.0 0.7 %copy-start.9 = (bf16[50,128]{1,0:T(8,128)(2,1)S(1)}, bf16[50,128]{1,0:T(8,128)(2,1)}, u32[]{:S(2)}) copy-start(bf16[50,128]{1,0:T(8,128)(2,1)} %x_ref.1) | copy-start | bytes 38404
  2.8 0.7 %copy-start.10 = (bf16[128]{0:T(256)(128)(2,1)S(1)}, bf16[128]{0:T(256)(128)(2,1)}, u32[]{:S(2)}) copy-start(bf16[128]{0:T(256)(128)(2,1)} %param.6) | copy-start | bytes 772
  3.4 7.2 %collective-permute-start.2 = (bf16[56,384]{1,0:T(8,128)(2,1)S(1)}, bf16[56,384]{1,0:T(8,128)(2,1)S(1)}, u32[]{:S(2)}, u32[]{:S(2)}) collective-permute-start(bf16[56,384]{1,0:T(8,128)(2,1)S(1)} %shard_map.59), channel_id=1, source_target_pairs={{0,3},{1,2},{2,1},{3,0},{4,7},{5,6},{6,5},{7,4},{8,11},{9,10},{10,... | collective-permute-start | bytes 129032 | tf_op jit(solution)/shard_map/ppermute | solution.py:190
  8.6 4.9 %collective-permute-start.1 = (bf16[56,384]{1,0:T(8,128)(2,1)S(1)}, bf16[56,384]{1,0:T(8,128)(2,1)S(1)}, u32[]{:S(2)}, u32[]{:S(2)}) collective-permute-start(bf16[56,384]{1,0:T(8,128)(2,1)S(1)} %shard_map.59), channel_id=1, source_target_pairs={{0,2},{1,3},{2,0},{3,1},{4,6},{5,7},{6,4},{7,5},{8,10},{9,11},{10,... | collective-permute-start | bytes 129032 | tf_op jit(solution)/shard_map/ppermute | solution.py:190
  8.6 4.9 %collective-permute-start = (bf16[56,384]{1,0:T(8,128)(2,1)S(1)}, bf16[56,384]{1,0:T(8,128)(2,1)S(1)}, u32[]{:S(2)}, u32[]{:S(2)}) collective-permute-start(bf16[56,384]{1,0:T(8,128)(2,1)S(1)} %shard_map.59), channel_id=1, source_target_pairs={{0,1},{1,0},{2,3},{3,2},{4,5},{5,4},{6,7},{7,6},{8,9},{9,8},{10,11... | collective-permute-start | bytes 129032 | tf_op jit(solution)/shard_map/ppermute | solution.py:190
  13.5 7.0 %collective-permute-start.6 = (bf16[56,1024]{1,0:T(8,128)(2,1)S(1)}, bf16[56,1024]{1,0:T(8,128)(2,1)S(1)}, u32[]{:S(2)}, u32[]{:S(2)}) collective-permute-start(bf16[56,1024]{1,0:T(8,128)(2,1)S(1)} %pad_maximum_fusion.refs_1_.refs_4_.refs_3_), channel_id=1, source_target_pairs={{0,24},{4,28},{8,16},{12,20},{16,8},{20,12},{24,0},{28,4},{1,25},{... | collective-permute-start | bytes 344072 | tf_op jit(solution)/shard_map/ppermute | solution.py:195
  16.0 5.2 %collective-permute-start.5 = (bf16[56,1024]{1,0:T(8,128)(2,1)S(1)}, bf16[56,1024]{1,0:T(8,128)(2,1)S(1)}, u32[]{:S(2)}, u32[]{:S(2)}) collective-permute-start(bf16[56,1024]{1,0:T(8,128)(2,1)S(1)} %pad_maximum_fusion.refs_1_.refs_4_.refs_3_), channel_id=1, source_target_pairs={{0,16},{4,20},{8,24},{12,28},{16,0},{20,4},{24,8},{28,12},{1,17},{... | collective-permute-start | bytes 344072 | tf_op jit(solution)/shard_map/ppermute | solution.py:195
  16.5 4.8 %collective-permute-start.4 = (bf16[56,1024]{1,0:T(8,128)(2,1)S(1)}, bf16[56,1024]{1,0:T(8,128)(2,1)S(1)}, u32[]{:S(2)}, u32[]{:S(2)}) collective-permute-start(bf16[56,1024]{1,0:T(8,128)(2,1)S(1)} %pad_maximum_fusion.refs_1_.refs_4_.refs_3_), channel_id=1, source_target_pairs={{0,8},{4,12},{8,0},{12,4},{16,24},{20,28},{24,16},{28,20},{1,9},{5... | collective-permute-start | bytes 344072 | tf_op jit(solution)/shard_map/ppermute | solution.py:195
  17.1 4.7 %collective-permute-start.3 = (bf16[56,1024]{1,0:T(8,128)(2,1)S(1)}, bf16[56,1024]{1,0:T(8,128)(2,1)S(1)}, u32[]{:S(2)}, u32[]{:S(2)}) collective-permute-start(bf16[56,1024]{1,0:T(8,128)(2,1)S(1)} %pad_maximum_fusion.refs_1_.refs_4_.refs_3_), channel_id=1, source_target_pairs={{0,4},{4,0},{8,12},{12,8},{16,20},{20,16},{24,28},{28,24},{1,5},{5... | collective-permute-start | bytes 344072 | tf_op jit(solution)/shard_map/ppermute | solution.py:197
  20.5 5.8 %collective-permute-start.9 = (bf16[56,1024]{1,0:T(8,128)(2,1)S(1)}, bf16[56,1024]{1,0:T(8,128)(2,1)S(1)}, u32[]{:S(2)}, u32[]{:S(2)}) collective-permute-start(bf16[56,1024]{1,0:T(8,128)(2,1)S(1)} %collective-permute-done.6.refs_4_.refs_10_.refs_9_), channel_id=1, source_target_pairs={{0,4},{4,0},{8,12},{12,8},{16,20},{20,16},{24,28},{28,24},{1,5},{5... | collective-permute-start | bytes 344072 | tf_op jit(solution)/shard_map/ppermute | solution.py:197
  21.3 5.0 %collective-permute-start.8 = (bf16[56,1024]{1,0:T(8,128)(2,1)S(1)}, bf16[56,1024]{1,0:T(8,128)(2,1)S(1)}, u32[]{:S(2)}, u32[]{:S(2)}) collective-permute-start(bf16[56,1024]{1,0:T(8,128)(2,1)S(1)} %collective-permute-done.5.refs_3_.refs_8_.refs_7_), channel_id=1, source_target_pairs={{0,4},{4,0},{8,12},{12,8},{16,20},{20,16},{24,28},{28,24},{1,5},{5... | collective-permute-start | bytes 344072 | tf_op jit(solution)/shard_map/ppermute | solution.py:197
  21.3 2.3 %copy-start.4 = (bf16[56,1024]{1,0:T(8,128)(2,1)}, bf16[56,1024]{1,0:T(8,128)(2,1)S(1)}, u32[]{:S(2)}) copy-start(bf16[56,1024]{1,0:T(8,128)(2,1)S(1)} %collective-permute-done.4.refs_2_.refs_6_.refs_5_) | copy-start | bytes 344068
  21.3 4.9 %collective-permute-start.7 = (bf16[56,1024]{1,0:T(8,128)(2,1)S(1)}, bf16[56,1024]{1,0:T(8,128)(2,1)S(1)}, u32[]{:S(2)}, u32[]{:S(2)}) collective-permute-start(bf16[56,1024]{1,0:T(8,128)(2,1)S(1)} %collective-permute-done.4.refs_2_.refs_6_.refs_5_), channel_id=1, source_target_pairs={{0,4},{4,0},{8,12},{12,8},{16,20},{20,16},{24,28},{28,24},{1,5},{5... | collective-permute-start | bytes 344072 | tf_op jit(solution)/shard_map/ppermute | solution.py:197
  21.8 1.8 %copy-start.6 = (bf16[56,1024]{1,0:T(8,128)(2,1)}, bf16[56,1024]{1,0:T(8,128)(2,1)S(1)}, u32[]{:S(2)}) copy-start(bf16[56,1024]{1,0:T(8,128)(2,1)S(1)} %collective-permute-done.3.refs_2_.refs_5_.refs_4_) | copy-start | bytes 344068
  23.6 1.3 %copy-start = (f32[512,1024]{1,0:T(8,128)}, f32[512,1024]{1,0:T(8,128)S(1)}, u32[]{:S(2)}) copy-start(f32[512,1024]{1,0:T(8,128)S(1)} %get-tuple-element.20.refs_9_.refs_16_.refs_15_) | copy-start | bytes 6291460
  24.9 1.3 %copy-start.2 = (f32[512,1024]{1,0:T(8,128)}, f32[512,1024]{1,0:T(8,128)S(1)}, u32[]{:S(2)}) copy-start(f32[512,1024]{1,0:T(8,128)S(1)} %get-tuple-element.21.refs_10_.refs_18_.refs_17_) | copy-start | bytes 6291460
  26.3 14.6 %copy-start.1 = (f32[512,1024]{1,0:T(8,128)S(1)}, f32[512,1024]{1,0:T(8,128)}, u32[]{:S(2)}) copy-start(f32[512,1024]{1,0:T(8,128)} %copy-done) | copy-start | bytes 6291460
  26.3 14.6 %copy-start.5 = (bf16[56,1024]{1,0:T(8,128)(2,1)S(1)}, bf16[56,1024]{1,0:T(8,128)(2,1)}, u32[]{:S(2)}) copy-start(bf16[56,1024]{1,0:T(8,128)(2,1)} %copy-done.4) | copy-start | bytes 344068
  26.3 14.6 %copy-start.7 = (bf16[56,1024]{1,0:T(8,128)(2,1)S(1)}, bf16[56,1024]{1,0:T(8,128)(2,1)}, u32[]{:S(2)}) copy-start(bf16[56,1024]{1,0:T(8,128)(2,1)} %copy-done.6) | copy-start | bytes 344068
  31.7 1.3 %copy-start.3 = (f32[512,1024]{1,0:T(8,128)}, f32[512,1024]{1,0:T(8,128)S(1)}, u32[]{:S(2)}) copy-start(f32[512,1024]{1,0:T(8,128)S(1)} %get-tuple-element.25.refs_19_.refs_18_) | copy-start | bytes 6291460

commit v2 on v0

v2 whole, which is shorter than its diff:
```python
import jax
import jax.numpy as jnp
import numpy as np
from jax import lax
from jax.experimental import pallas as pl
from jax.experimental.pallas import tpu as pltpu
from jax.sharding import PartitionSpec as P

D = 50
EPSILON_KERNEL = 0.05
SCALE = float(2.0 / (2.0 * D * EPSILON_KERNEL) / np.log(2.0))
EXT = 56
NORM_X, NORM_Y, B_ROW, A_ROW = D, D + 2, D + 4, D + 5
LANES, SUB = 128, 8
VMEM_BYTES = 16 * 2**20

f32 = jnp.float32
bf16 = jnp.bfloat16
VM = pl.BlockSpec(memory_space=pltpu.VMEM)
ANY = pl.BlockSpec(memory_space=pl.ANY)


def ext_kernel(x_hbm, y_hbm, a_hbm, b_hbm, o_ref, xv, yv, av, bv, sx, sy, sems):
    copies = [
        pltpu.make_async_copy(src, dst, sems.at[i])
        for i, (src, dst) in enumerate(
            ((x_hbm, xv), (y_hbm, yv), (a_hbm, av), (b_hbm, bv))
        )
    ]
    for c in copies:
        c.start()
    for c in copies:
        c.wait()
    ny = yv.shape[1]
    for src, w, s, norm, one, w_row in (
        (xv, av, sx, NORM_X, NORM_Y, A_ROW),
        (yv, bv, sy, NORM_Y, NORM_X, B_ROW),
    ):
        c = src[...].astype(f32)
        n = -0.5 * jnp.sum(c * c, axis=0, keepdims=True)
        hi = n.astype(bf16).astype(f32)
        s[...] = jnp.zeros_like(s)
        s[0:D, :] = c
        s[norm : norm + 1, :] = hi
        s[norm + 1 : norm + 2, :] = n - hi
        s[one : one + 2, :] = jnp.ones((2, s.shape[1]), f32)
        s[w_row : w_row + 1, :] = w[...].astype(f32).reshape(1, -1)
    o_ref[:, 0:ny] = sy[...].astype(bf16)
    o_ref[:, ny:] = sx[...].astype(bf16)


def kernel_block(xt, y):
    s = lax.dot_general(xt, y, (((1,), (0,)), ((), ())), preferred_element_type=f32)
    return jnp.exp2(s * SCALE)


def add_lanes(acc, e):
    for t in range(e.shape[1] // LANES):
        acc = acc + e[:, t * LANES : (t + 1) * LANES]
    return acc


def spread(v, width):
    return jnp.concatenate([v] * (width // LANES), axis=1)


def groups(rows, body, init=0):
    n = rows // SUB

    def step(i, carry):
        return body(pl.ds(pl.multiple_of(i * SUB, SUB), SUB), carry)

    return lax.fori_loop(0, n, step, init, unroll=min(8, n))


def row_pass(k, v, acc):
    vb = jnp.broadcast_to(v, (SUB, v.shape[1]))

    def body(rs, carry):
        acc[rs, :] = add_lanes(acc[rs, :], k[rs, :] * vb)
        return carry

    groups(k.shape[0], body)


def col_pass(k, u, init):
    def body(rs, carry):
        return carry + k[rs, :] * spread(u[rs, :], carry.shape[1])

    return groups(k.shape[0], body, init)


def scaling(weights, acc, u):
    u[...] = weights[...] / jnp.broadcast_to(
        jnp.sum(acc[...], axis=1, keepdims=True), u.shape
    )


class Refs:
    def __init__(self, refs):
        self.refs = list(refs)

    def take(self, *counts):
        out = []
        for n in counts:
            out.append(self.refs[:n] if isinstance(n, int) else self.refs[: n[0]][0])
            del self.refs[: n if isinstance(n, int) else n[0]]
        return out


ONE = (1,)


def xor_perm(n, m):
    return [(i, i ^ m) for i in range(n)]


def solution(mesh):
    rows, cols = mesh.shape["row"], mesh.shape["col"]

    def per_device(x_src, y_tgt, a_src, b_tgt):
        nx, ny = x_src.shape[1], y_tgt.shape[1]
        X, T = nx * cols, ny * cols
        def slab(split):
            return rows // split * X * T * rows * 4

        split = 4 if slab(4) <= 36 * 2**20 else rows
        kept = slab(split) <= 36 * 2**20
        parts = rows // split
        bits = split.bit_length() - 1
        width = max(ny, LANES)
        per_row = T // width

        def held(shape, dtype):
            return pltpu.VMEM(shape, dtype) if kept else jax.ShapeDtypeStruct(shape, dtype)

        def call(kernel, outs, args, scratch=(), cost=None, spec=VM):
            return pl.pallas_call(
                kernel,
                out_shape=outs,
                in_specs=[spec] * len(args),
                out_specs=jax.tree.map(lambda _: VM, outs),
                scratch_shapes=scratch,
                compiler_params=pltpu.CompilerParams(vmem_limit_bytes=VMEM_BYTES),
                cost_estimate=cost,
            )(*args)

        def cost(n):
            return pl.CostEstimate(
                flops=2 * EXT * X * T * n,
                bytes_accessed=X * T * n,
                transcendentals=X * T * n,
            )

        block_t = held((X, T), f32)
        lanes_t = held((X, LANES), f32)
        block_s = pltpu.VMEM((X, T), f32)
        lanes_s = pltpu.VMEM((X, LANES), f32)
        tot_t = jax.ShapeDtypeStruct((rows, T), f32)

        def blocks(ks, xts, ys, spare=None):
            def get(q, i):
                if kept:
                    return ks[q * rows + i]
                spare[...] = kernel_block(xts[q][...], ys[i][:, 0:T])
                return spare

            return get

        spare = [] if kept else [block_s]

        own = call(
            ext_kernel,
            jax.ShapeDtypeStruct((EXT, ny + nx), bf16),
            [
                pltpu.with_memory_space_constraint(t, pltpu.HBM)
                for t in (x_src, y_tgt, a_src, b_tgt)
            ],
            [
                pltpu.VMEM((D, nx), bf16),
                pltpu.VMEM((D, ny), bf16),
                pltpu.VMEM((nx,), bf16),
                pltpu.VMEM((ny,), bf16),
                pltpu.VMEM((EXT, nx), f32),
                pltpu.VMEM((EXT, ny), f32),
                pltpu.SemaphoreType.DMA((4,)),
            ],
            spec=ANY,
        )
        line = [own] + [
            lax.ppermute(own, "col", xor_perm(cols, m)) for m in range(1, cols)
        ]
        both = jnp.concatenate(
            [p[:, 0:ny] for p in line] + [p[:, ny:] for p in line], axis=1
        )
        y0 = both[:, 0:T]
        y, xe = [None] * rows, [None] * parts
        y[0], xe[0] = y0, both[:, T:]
        for m in range(2, rows, 2):
            if m % split == 0:
                w = lax.ppermute(both, "row", xor_perm(rows, m))
                y[m], xe[m // split] = w[:, 0:T], w[:, T:]
            else:
                y[m] = lax.ppermute(y0, "row", xor_perm(rows, m))
        for m in range(0, rows, 2):
            y[m + 1] = lax.ppermute(y[m], "row", xor_perm(rows, 1))

        k_all = [None] * (parts * rows)
        xts, abs_, accs = [None] * parts, [None] * parts, [None] * parts

        def make(new, todo, ys, extra):
            old = sorted({q for q, _ in todo} - set(new))

            def kernel(*refs):
                r = Refs(refs)
                xe_r, xt_r, acc_r, y_r = r.take(len(new), len(old), len(old), len(ys))
                xt_o, ab_o, acc_o, k_o = r.take(
                    len(new), len(new), len(new) + len(old), len(todo) if kept else 0
                )
                xt = dict(zip(old, xt_r))
                accs_in = {q: a[...] for q, a in zip(old, acc_r)}
                for q, e, t, ab in zip(new, xe_r, xt_o, ab_o):
                    t[...] = jnp.transpose(e[...].astype(f32)).astype(bf16)
                    xt[q] = t
                    ab[...] = jnp.broadcast_to(
                        t[:, A_ROW : A_ROW + 1].astype(f32), ab.shape
                    )
                    accs_in[q] = jnp.zeros((X, LANES), f32)
                y_of = dict(zip(ys, y_r))
                for n, (q, i) in enumerate(todo):
                    e = kernel_block(xt[q][...], y_of[i][...])
                    if kept:
                        k_o[n][...] = e
                    accs_in[q] = add_lanes(accs_in[q], e)
                for q, o in zip(new + old, acc_o):
                    o[...] = accs_in[q]

            outs = (
                [held((X, EXT), bf16)] * len(new)
                + [lanes_t] * (2 * len(new) + len(old))
                + ([block_t] * len(todo) if kept else [])
            )
            args = (
                [xe[q] for q in new]
                + [xts[q] for q in old]
                + [accs[q] for q in old]
                + [y[i] for i in ys]
            )
            got = Refs(call(kernel, outs, args, cost=cost(len(todo))))
            new_xt, new_ab, new_acc, new_k = got.take(
                len(new), len(new), len(new) + len(old), len(todo) if kept else 0
            )
            for q, t, ab in zip(new, new_xt, new_ab):
                xts[q], abs_[q] = t, ab
            for q, acc in zip(new + old, new_acc):
                accs[q] = acc
            for (q, i), k in zip(todo, new_k):
                k_all[q * rows + i] = k

        evens, odds = list(range(2, rows, 2)), list(range(3, rows, 2))
        rest = list(range(1, parts))
        make([0], [(0, 0), (0, 1)], [0, 1], None)
        make(
            rest,
            [(q, i) for q in range(parts) for i in ([] if q == 0 else [0, 1]) + evens],
            ([0, 1] if rest else []) + evens,
            None,
        )
        make([], [(q, i) for q in range(parts) for i in odds], odds, None)
        ks = k_all if kept else []
        matrix = [] if kept else [*xts, *y]

        def matrix_refs(r):
            if kept:
                return r.take(parts * rows)[0], (), ()
            xt, ys = r.take(parts, rows)
            return (), xt, ys

        def col_sums(get, us, tot):
            for i in range(rows):
                s = jnp.zeros((SUB, T), f32)
                for q in range(parts):
                    s = col_pass(get(q, i), us[q], s)
                tot[i : i + 1, :] = jnp.sum(s, axis=0, keepdims=True)

        def first_sums(*refs):
            r = Refs(refs)
            acc, ab = r.take(parts, parts)
            k, xt, ys = matrix_refs(r)
            tot, us = r.take(ONE, parts)
            get = blocks(k, xt, ys, *r.refs)
            for q in range(parts):
                scaling(ab[q], acc[q], us[q])
            col_sums(get, us, tot)

        tot = call(
            first_sums,
            tot_t,
            [*accs, *abs_, *ks, *matrix],
            [lanes_s] * parts + spare,
        )

        def add_swapped(t, g, m):
            return jnp.concatenate(
                [t[i : i + 1] + g[i ^ m : (i ^ m) + 1] for i in range(rows)], axis=0
            )

        def add_kernel(m):
            def kernel(t, g, o):
                o[...] = add_swapped(t[...], g[...], m)

            return kernel

        for b in range(bits):
            got = lax.ppermute(tot, "row", xor_perm(rows, 1 << b))
            if b < bits - 1:
                tot = call(add_kernel(1 << b), tot_t, [tot, got])

        n_tot = rows * per_row

        def pack_tot(t):
            return jnp.concatenate(
                [t[:, g * width : (g + 1) * width] for g in range(per_row)], axis=0
            ).astype(bf16)

        def unpack_tot(s):
            s = s.astype(f32)
            return jnp.concatenate(
                [s[g * rows : (g + 1) * rows, :] for g in range(per_row)], axis=1
            )

        def second(*refs):
            r = Refs(refs)
            t, g, ab, xes, bs = r.take(ONE, ONE, parts, parts, rows if kept else 0)
            k, xt, ys = matrix_refs(r)
            bs = bs or ys
            tot_o, keep_o, send_o, acc, us = r.take(ONE, ONE, ONE, ONE, parts)
            get = blocks(k, xt, ys, *r.refs)
            total = add_swapped(t[...], g[...], split // 2)
            v = [
                bs[i][B_ROW : B_ROW + 1, 0:T].astype(f32) / total[i : i + 1, :]
                for i in range(rows)
            ]
            for q in range(parts):
                acc[...] = jnp.zeros_like(acc)
                for i in range(rows):
                    row_pass(get(q, i), v[i], acc)
                scaling(ab[q], acc, us[q])
            col_sums(get, us, tot_o)
            send_o[0:n_tot, :] = pack_tot(tot_o[...])
            for i in range(split):
                num = jnp.zeros((EXT, ny), f32)
                for q in range(parts):
                    z = get(q, i)[:, 0:ny] * spread_to(us[q][...], ny)
                    num = num + jnp.dot(
                        xes[q][...], z.astype(bf16), preferred_element_type=f32
                    )
                if i % 2 == 0:
                    keep_o[i // 2, :, 0:ny] = num
                else:
                    at = n_tot + i // 2 * EXT
                    send_o[at : at + EXT, 0:ny] = num.astype(bf16)

        def spread_to(u, n):
            return u[:, 0:n] if n <= LANES else spread(u, n)

        half = split // 2
        tot, keep, send = call(
            second,
            (
                tot_t,
                jax.ShapeDtypeStruct((half, EXT, width), f32),
                jax.ShapeDtypeStruct((n_tot + half * EXT, width), bf16),
            ),
            [tot, got, *abs_, *xe, *(y if kept else []), *ks, *matrix],
            [lanes_s] * (1 + parts) + spare,
        )

        def halve(m):
            def kernel(t, kp, g, tot_o, keep_o, send_o):
                tot_o[...] = add_swapped(t[...], unpack_tot(g[0:n_tot, :]), m)
                send_o[0:n_tot, :] = pack_tot(tot_o[...])
                for j in range(kp.shape[0]):
                    s = kp[j] + g[n_tot + j * EXT : n_tot + (j + 1) * EXT, :].astype(f32)
                    if j % 2 == 0:
                        keep_o[j // 2] = s
                    else:
                        at = n_tot + j // 2 * EXT
                        send_o[at : at + EXT, :] = s.astype(bf16)

            return kernel

        for b in range(bits):
            got = lax.ppermute(send, "row", xor_perm(rows, 1 << b))
            if b < bits - 1:
                half //= 2
                tot, keep, send = call(
                    halve(1 << b),
                    (
                        tot_t,
                        jax.ShapeDtypeStruct((half, EXT, width), f32),
                        jax.ShapeDtypeStruct((n_tot + half * EXT, width), bf16),
                    ),
                    [tot, keep, got],
                )

        def final(*refs):
            r = Refs(refs)
            t, kp, g, xt, ys = r.take(ONE, ONE, ONE, ONE, rows)
            k = r.take(rows if kept else 0)[0]
            src_o, tgt_o = r.take(ONE, ONE)
            total = add_swapped(t[...], unpack_tot(g[0:n_tot, :]), split // 2)
            num = kp[0] + g[n_tot:, :].astype(f32)
            tgt_o[...] = num[0:D, 0:ny] / total[0:1, 0:ny]
            res = jnp.zeros((nx, EXT), f32)
            for i in range(rows):
                yi = ys[i][:, 0:T]
                v = yi[B_ROW : B_ROW + 1, :].astype(f32) / total[i : i + 1, :]
                e = k[i][0:nx, :] if kept else kernel_block(xt[0:nx, :], yi)
                res = res + lax.dot_general(
                    (e * v).astype(bf16),
                    yi,
                    (((1,), (1,)), ((), ())),
                    preferred_element_type=f32,
                )
            res = jnp.transpose(res)
            src_o[...] = res[0:D, :] / res[NORM_X : NORM_X + 1, :]

        return tuple(
            call(
                final,
                (
                    jax.ShapeDtypeStruct((D, nx), f32),
                    jax.ShapeDtypeStruct((D, ny), f32),
                ),
                [tot, keep, got, xts[0], *y, *(ks[0:rows] if kept else [])],
            )
        )

    spec = P(None, ("row", "col"))
    vec = P(("row", "col"))
    return jax.shard_map(
        per_device,
        mesh=mesh,
        in_specs=(spec, spec, vec, vec),
        out_specs=(spec, spec),
        check_vma=False,
    )
```

time: 216 us -> 47.6 us (0.22)
  blocking collectives: 93.7 us -> 0 us
  waiting for transfers between devices: 69.3 us -> 16.3 us
  matrix products: 32 us -> 0 us
  Pallas kernels: 0 us -> 17.3 us
  between operations: 14.1 us -> 0.78 us
  starting transfers between devices: 0.08 us -> 12.9 us
  other arithmetic: 2.95 us -> 0.02 us
  local copies, waits for them, and re-layouts: 2.73 us -> 0.08 us
    psum x2 -> x0, waiting for transfers between devices: 69.3 us -> none  [the longest x1 56.5 us: per_device(): total, numer = lax.psum((total_again, numer_local), 'row')]
    psum x5 -> x0, blocking collectives: 51.4 us -> none  [the longest x2 24.1 us: later_factor_vector(): total = lax.psum(partial_aggregate_amount, 'row')]
    all_gather x4 -> x0, blocking collectives: 42.3 us -> none  [the longest x1 12.4 us: per_device(): lax.all_gather(x_src, 'col', axis=1, tiled=True)]
    dot_general x8 -> x0, matrix products: 32 us -> none  [the longest x2 9.38 us: one(): jnp.dot(kernel_rows(t[0], t[1], later_coordinate_entries, ynorm), later_d...]
    pallas_call x0 -> x9, Pallas kernels: none -> 17.3 us  [call(): pl.pallas_call(kernel, out_shape=outs, in_specs=[spec] * len(args), out_s...]
    ppermute x0 -> x14, waiting for transfers between devices: none -> 16.3 us  [the longest x3 4.27 us: per_device(): lax.ppermute(own, 'col', xor_perm(cols, m))]
    ppermute x0 -> x14, starting transfers between devices: none -> 12.9 us  [the longest x3 5.76 us: per_device(): lax.ppermute(own, 'col', xor_perm(cols, m))]
    div x6 -> x0, other arithmetic: 2.84 us -> none  [the longest x1 1.45 us: per_device(): proj_tgt = own_numer / own_total[None, :]]
  transfers between devices with their start and end apart: 2 -> 14, of which waited for: 2 -> 8; matrix products, arithmetic and copies ran while one was open for 5% -> 0% of each run, Pallas kernels for 0% -> 7%
where the time goes in v2:
time: 47.6 us; the launch traced here: 47.3 us
  Pallas kernels  17.3 us (36%)
  waiting for transfers between devices  16.3 us (34%)
  starting transfers between devices  12.9 us (27%)
  between operations  0.78 us (2%)
    pallas_call x9, Pallas kernels, call(): pl.pallas_call(kernel, out_shape=outs, in_specs=[spec] * len(args), out_s...  17.3 us
    ppermute x3, starting transfers between devices, per_device(): lax.ppermute(own, 'col', xor_perm(cols, m))  5.76 us
    ppermute x3, waiting for transfers between devices, per_device(): lax.ppermute(own, 'col', xor_perm(cols, m))  4.27 us
    ppermute x2, waiting for transfers between devices, per_device(): y[m] = lax.ppermute(y0, 'row', xor_perm(rows, m))  4.25 us
    ppermute x2, waiting for transfers between devices, per_device(): got = lax.ppermute(send, 'row', xor_perm(rows, 1 << b))  4.02 us
    ppermute x2, waiting for transfers between devices, per_device(): got = lax.ppermute(tot, 'row', xor_perm(rows, 1 << b))  3.75 us
    ppermute x2, starting transfers between devices, per_device(): y[m] = lax.ppermute(y0, 'row', xor_perm(rows, m))  2.03 us
    ppermute x1, starting transfers between devices, per_device(): w = lax.ppermute(both, 'row', xor_perm(rows, m))  1.58 us
  transfers between devices with their start and end apart: 14, of which 8 were waited for; matrix products, arithmetic and copies ran while one was open for 0% of the time, Pallas kernels for 7%

profile of v2, /device:TPU:0, one launch (start us, length us, event | category | flops | bytes accessed | tf_op | source)
XLA Modules:
  0.0 47.3 jit_solution(558164140662047680)
XLA Ops:
  0.6 0.8 %shard_map.59 = bf16[56,384]{1,0:T(8,128)(2,1)S(1)} custom-call(bf16[50,128]{1,0:T(8,128)(2,1)} %x_hbm.1, bf16[50,256]{1,0:T(8,128)(2,1)} %y_hbm.1, bf16[128]{0:T(256)(128)(2,1)} %a_hbm.1, bf16[256]{0:T(256)(128)(2,1)} %b_hbm.1), custom_call_target="tpu_custom_call" | custom-call | tf_op jit(solution)/shard_map/pallas_call | solution.py:138
  1.5 5.1 %collective-permute-start.2 = (bf16[56,384]{1,0:T(8,128)(2,1)S(1)}, bf16[56,384]{1,0:T(8,128)(2,1)S(1)}, u32[]{:S(2)}, u32[]{:S(2)}) collective-permute-start(bf16[56,384]{1,0:T(8,128)(2,1)S(1)} %shard_map.59), channel_id=1, source_target_pairs={{0,3},{1,2},{2,1},{3,0},{4,7},{5,6},{6,5},{7,4},{8,11},{9,10},{10,... | collective-permute-start | bytes 129032 | tf_op jit(solution)/shard_map/ppermute | solution.py:191
  6.6 0.0 collective-permute-start.1
  6.6 0.6 %collective-permute-start = (bf16[56,384]{1,0:T(8,128)(2,1)S(1)}, bf16[56,384]{1,0:T(8,128)(2,1)S(1)}, u32[]{:S(2)}, u32[]{:S(2)}) collective-permute-start(bf16[56,384]{1,0:T(8,128)(2,1)S(1)} %shard_map.59), channel_id=1, source_target_pairs={{0,1},{1,0},{2,3},{3,2},{4,5},{5,4},{6,7},{7,6},{8,9},{9,8},{10,11... | collective-permute-start | bytes 129032 | tf_op jit(solution)/shard_map/ppermute | solution.py:191
  7.2 3.4 %collective-permute-done = bf16[56,384]{1,0:T(8,128)(2,1)S(1)} collective-permute-done((bf16[56,384]{1,0:T(8,128)(2,1)S(1)}, bf16[56,384]{1,0:T(8,128)(2,1)S(1)}, u32[]{:S(2)}, u32[]{:S(2)}) %collective-permute-start) | collective-permute-done | bytes 43040 | tf_op jit(solution)/shard_map/ppermute | solution.py:191
  10.6 0.9 %collective-permute-done.1 = bf16[56,384]{1,0:T(8,128)(2,1)S(1)} collective-permute-done((bf16[56,384]{1,0:T(8,128)(2,1)S(1)}, bf16[56,384]{1,0:T(8,128)(2,1)S(1)}, u32[]{:S(2)}, u32[]{:S(2)}) %collective-permute-start.1) | collective-permute-done | bytes 43040 | tf_op jit(solution)/shard_map/ppermute | solution.py:191
  11.6 1.6 %collective-permute-start.4 = (bf16[56,1536]{1,0:T(8,128)(2,1)S(1)}, bf16[56,1536]{1,0:T(8,128)(2,1)S(1)}, u32[]{:S(2)}, u32[]{:S(2)}) collective-permute-start(bf16[56,1536]{1,0:T(8,128)(2,1)S(1)} %get-tuple-element.64), channel_id=1, source_target_pairs={{0,16},{4,20},{8,24},{12,28},{16,0},{20,4},{24,8},{28,12},{1,17},{... | collective-permute-start | bytes 516104 | tf_op jit(solution)/shard_map/ppermute | solution.py:201
  13.2 1.5 %collective-permute-start.6 = (bf16[56,1024]{1,0:T(8,128)(2,1)S(1)}, bf16[56,1024]{1,0:T(8,128)(2,1)S(1)}, u32[]{:S(2)}, u32[]{:S(2)}) collective-permute-start(bf16[56,1024]{1,0:T(8,128)(2,1)S(1)} %pad_maximum_fusion.refs_1_.refs_3_.refs_6_.refs_4_), channel_id=1, source_target_pairs={{0,24},{4,28},{8,16},{12,20},{16,8},{20,12},{24,0},{28,4},{1,25},{... | collective-permute-start | bytes 344072 | tf_op jit(solution)/shard_map/ppermute | solution.py:204
  14.7 0.5 %collective-permute-start.5 = (bf16[56,1024]{1,0:T(8,128)(2,1)S(1)}, bf16[56,1024]{1,0:T(8,128)(2,1)S(1)}, u32[]{:S(2)}, u32[]{:S(2)}) collective-permute-start(bf16[56,1024]{1,0:T(8,128)(2,1)S(1)} %pad_maximum_fusion.refs_1_.refs_3_.refs_6_.refs_4_), channel_id=1, source_target_pairs={{0,8},{4,12},{8,0},{12,4},{16,24},{20,28},{24,16},{28,20},{1,9},{5... | collective-permute-start | bytes 344072 | tf_op jit(solution)/shard_map/ppermute | solution.py:204
  15.2 0.0 collective-permute-start.3
  15.2 3.8 %collective-permute-done.6.refs_7_.refs_12_.refs_10_ = bf16[56,1024]{1,0:T(8,128)(2,1)S(1)} collective-permute-done((bf16[56,1024]{1,0:T(8,128)(2,1)S(1)}, bf16[56,1024]{1,0:T(8,128)(2,1)S(1)}, u32[]{:S(2)}, u32[]{:S(2)}) %collective-permute-start.6) | collective-permute-done | bytes 114720 | tf_op jit(solution)/shard_map/ppermute | solution.py:204
  19.1 0.0 collective-permute-start.9
  19.1 0.4 collective-permute-done.5.refs_5_.refs_8_.refs_6_
  19.5 0.1 collective-permute-start.7
  19.6 0.5 %collective-permute-start.8 = (bf16[56,1024]{1,0:T(8,128)(2,1)S(1)}, bf16[56,1024]{1,0:T(8,128)(2,1)S(1)}, u32[]{:S(2)}, u32[]{:S(2)}) collective-permute-start(bf16[56,1024]{1,0:T(8,128)(2,1)S(1)} %slice.53.refs_6_.refs_10_.refs_8_), channel_id=1, source_target_pairs={{0,4},{4,0},{8,12},{12,8},{16,20},{20,16},{24,28},{28,24},{1,5},{5... | collective-permute-start | bytes 344072 | tf_op jit(solution)/shard_map/ppermute | solution.py:206
  20.1 0.0 collective-permute-done.3.refs_2_.refs_4_.refs_7_.refs_5_
  20.1 0.8 %shard_map.60 = (bf16[512,56]{1,0:T(8,128)(2,1)S(1)}, f32[512,128]{1,0:T(8,128)S(1)}, f32[512,128]{1,0:T(8,128)S(1)}, f32[512,1024]{1,0:T(8,128)S(1)}, f32[512,1024]{1,0:T(8,128)S(1)}) custom-call(bf16[56,512]{1,0:T(8,128)(2,1)S(1)} %pad_maximum_fusion.1.refs_0_.refs_4_, bf16[56,1024]{1,0:T(8,128)(2,1)S(1)} %pad_maximum_fusion.refs_1_.refs_3_.refs_6_.refs_4_, ...), custom_call_target="tpu_custom_call" | custom-call | flops 117440512 | bytes 1048576 | tf_op jit(solution)/shard_map/pallas_call | solution.py:138
  20.9 2.4 %shard_map.61 = (bf16[512,56]{1,0:T(8,128)(2,1)S(1)}, f32[512,128]{1,0:T(8,128)S(1)}, f32[512,128]{1,0:T(8,128)S(1)}, f32[512,128]{1,0:T(8,128)S(1)}, f32[512,10...) custom-call(bf16[56,512]{1,0:T(8,128)(2,1)S(1)} %slice.52.refs_0_.re, ...), custom_call_target="tpu_custom_call" | custom-call | flops 469762048 | bytes 4194304 | tf_op jit(solution)/shard_map/pallas_call | solution.py:138
  23.3 0.0 collective-permute-done.7.refs_4_.refs_9_.refs_7_
  23.3 0.0 collective-permute-done.8.refs_5_.refs_11_.refs_9_
  23.4 1.8 %shard_map.62 = (f32[512,128]{1,0:T(8,128)S(1)}, f32[512,128]{1,0:T(8,128)S(1)}, f32[512,1024]{1,0:T(8,128)S(1)}, f32[512,1024]{1,0:T(8,128)S(1)}, f32[512,1024]...) custom-call(bf16[512,56]{1,0:T(8,128)(2,1)S(1)} %get-tuple-element.33.refs_1_.refs_0_.r, ...), custom_call_target="tpu_custom_call" | custom-call | flops 352321536 | bytes 3145728 | tf_op jit(solution)/shard_map/pallas_call | solution.py:138
  25.1 3.1 %shard_map.63.t = f32[8,1024]{1,0:T(8,128)S(1)} custom-call(f32[512,128]{1,0:T(8,128)S(1)} %get-tuple-element.38.refs_0_, f32[512,128]{1,0:T(8,128)S(1)} %get-tuple-element.39.refs_1_, f32[512,128]{1,0:T(8,128)S(1)} %get-tuple-element.40.refs_2_, f32[512,128]{1,0:T(8,128)S(1)} %get-tuple-element.41.refs_3_, ...), custom_call_target="tpu_custom_call" | custom-call | tf_op jit(solution)/shard_map/pallas_call | solution.py:138
  28.2 0.2 collective-permute-start.10
  28.4 1.1 %collective-permute-done.10.g = f32[8,1024]{1,0:T(8,128)S(1)} collective-permute-done((f32[8,1024]{1,0:T(8,128)S(1)}, f32[8,1024]{1,0:T(8,128)S(1)}, u32[]{:S(2)}, u32[]{:S(2)}) %collective-permute-start.10) | collective-permute-done | bytes 32800 | tf_op jit(solution)/shard_map/ppermute | solution.py:315
  29.5 1.3 %collective-permute-start.11 = (f32[8,1024]{1,0:T(8,128)S(1)}, f32[8,1024]{1,0:T(8,128)S(1)}, u32[]{:S(2)}, u32[]{:S(2)}) collective-permute-start(f32[8,1024]{1,0:T(8,128)S(1)} %shard_map.64.refs_0_), channel_id=1, source_target_pairs={{0,8},{4,12},{8,0},{12,4},{16,24},{20,28},{24,16},{28,20},{1,9},{5... | collective-permute-start | bytes 98312 | tf_op jit(solution)/shard_map/ppermute | solution.py:315
  30.8 2.6 %collective-permute-done.11.refs_1_ = f32[8,1024]{1,0:T(8,128)S(1)} collective-permute-done((f32[8,1024]{1,0:T(8,128)S(1)}, f32[8,1024]{1,0:T(8,128)S(1)}, u32[]{:S(2)}, u32[]{:S(2)}) %collective-permute-start.11) | collective-permute-done | bytes 32800 | tf_op jit(solution)/shard_map/ppermute | solution.py:315
  33.5 7.0 %shard_map.65 = (f32[8,1024]{1,0:T(8,128)S(1)}, f32[2,56,256]{2,1,0:T(8,128)S(1)}, bf16[144,256]{1,0:T(8,128)(2,1)S(1)}) custom-call(f32[8,1024]{1,0:T(8,128)S(1)} %shard_map.64.refs_0_, f32[8,1024]{1,0:T(8,128)S(1)} %collective-permute-done.11.refs_1_, f32[512,128]{1,0:T(8,128)S(1)} %get-tuple-element.40.refs_2_, f32[512,128]{1,0:T(8,128)S(1)} %get-tuple-element.41.refs_3_, ...), custom_call_target="tpu_custom_call" | custom-call | tf_op jit(solution)/shard_map/pallas_call | solution.py:138
  40.5 0.1 collective-permute-start.12
  40.6 1.3 %collective-permute-done.12.g = bf16[144,256]{1,0:T(8,128)(2,1)S(1)} collective-permute-done((bf16[144,256]{1,0:T(8,128)(2,1)S(1)}, bf16[144,256]{1,0:T(8,128)(2,1)S(1)}, u32[]{:S(2)}, u32[]{:S(2)}) %collective-permute-start.12) | collective-permute-done | bytes 73760 | tf_op jit(solution)/shard_map/ppermute | solution.py:394
  41.8 1.3 %collective-permute-start.13 = (bf16[88,256]{1,0:T(8,128)(2,1)S(1)}, bf16[88,256]{1,0:T(8,128)(2,1)S(1)}, u32[]{:S(2)}, u32[]{:S(2)}) collective-permute-start(bf16[88,256]{1,0:T(8,128)(2,1)S(1)} %get-tuple-element.63), channel_id=1, source_target_pairs={{0,8},{4,12},{8,0},{12,4},{16,24},{20,28},{24,16},{28,20},{1,9},{5... | collective-permute-start | bytes 135176 | tf_op jit(solution)/shard_map/ppermute | solution.py:394
  43.2 2.8 %collective-permute-done.13.refs_2_ = bf16[88,256]{1,0:T(8,128)(2,1)S(1)} collective-permute-done((bf16[88,256]{1,0:T(8,128)(2,1)S(1)}, bf16[88,256]{1,0:T(8,128)(2,1)S(1)}, u32[]{:S(2)}, u32[]{:S(2)}) %collective-permute-start.13) | collective-permute-done | bytes 45088 | tf_op jit(solution)/shard_map/ppermute | solution.py:394
  45.9 1.4 %shard_map.67 = (f32[50,128]{1,0:T(8,128)}, f32[50,256]{1,0:T(8,128)}) custom-call(f32[8,1024]{1,0:T(8,128)S(1)} %get-tuple-element.61.refs_0_, f32[1,56,256]{2,1,0:T(8,128)S(1)} %get-tuple-element.62.refs_1_, bf16[88,256]{1,0:T(8,128)(2,1)S(1)} %collective-permute-done.13.refs_2_, bf16[512,56]{1,0:T(8,128)(2,1)S(1)} %get-tuple-element.33.refs_1_.refs_0_.refs_3_, ...), custom_call_target="tpu_custom_call" | custom-call | tf_op jit(solution)/shard_map/pallas_call | solution.py:138
  (17 shorter events, 0.1 us)
Async XLA Ops:
  1.5 10.0 %collective-permute-start.2 = (bf16[56,384]{1,0:T(8,128)(2,1)S(1)}, bf16[56,384]{1,0:T(8,128)(2,1)S(1)}, u32[]{:S(2)}, u32[]{:S(2)}) collective-permute-start(bf16[56,384]{1,0:T(8,128)(2,1)S(1)} %shard_map.59), channel_id=1, source_target_pairs={{0,3},{1,2},{2,1},{3,0},{4,7},{5,6},{6,5},{7,4},{8,11},{9,10},{10,... | collective-permute-start | bytes 129032 | tf_op jit(solution)/shard_map/ppermute | solution.py:191
  6.6 4.9 %collective-permute-start.1 = (bf16[56,384]{1,0:T(8,128)(2,1)S(1)}, bf16[56,384]{1,0:T(8,128)(2,1)S(1)}, u32[]{:S(2)}, u32[]{:S(2)}) collective-permute-start(bf16[56,384]{1,0:T(8,128)(2,1)S(1)} %shard_map.59), channel_id=1, source_target_pairs={{0,2},{1,3},{2,0},{3,1},{4,6},{5,7},{6,4},{7,5},{8,10},{9,11},{10,... | collective-permute-start | bytes 129032 | tf_op jit(solution)/shard_map/ppermute | solution.py:191
  6.6 4.0 %collective-permute-start = (bf16[56,384]{1,0:T(8,128)(2,1)S(1)}, bf16[56,384]{1,0:T(8,128)(2,1)S(1)}, u32[]{:S(2)}, u32[]{:S(2)}) collective-permute-start(bf16[56,384]{1,0:T(8,128)(2,1)S(1)} %shard_map.59), channel_id=1, source_target_pairs={{0,1},{1,0},{2,3},{3,2},{4,5},{5,4},{6,7},{7,6},{8,9},{9,8},{10,11... | collective-permute-start | bytes 129032 | tf_op jit(solution)/shard_map/ppermute | solution.py:191
  11.6 8.0 %collective-permute-start.4 = (bf16[56,1536]{1,0:T(8,128)(2,1)S(1)}, bf16[56,1536]{1,0:T(8,128)(2,1)S(1)}, u32[]{:S(2)}, u32[]{:S(2)}) collective-permute-start(bf16[56,1536]{1,0:T(8,128)(2,1)S(1)} %get-tuple-element.64), channel_id=1, source_target_pairs={{0,16},{4,20},{8,24},{12,28},{16,0},{20,4},{24,8},{28,12},{1,17},{... | collective-permute-start | bytes 516104 | tf_op jit(solution)/shard_map/ppermute | solution.py:201
  13.2 5.9 %collective-permute-start.6 = (bf16[56,1024]{1,0:T(8,128)(2,1)S(1)}, bf16[56,1024]{1,0:T(8,128)(2,1)S(1)}, u32[]{:S(2)}, u32[]{:S(2)}) collective-permute-start(bf16[56,1024]{1,0:T(8,128)(2,1)S(1)} %pad_maximum_fusion.refs_1_.refs_3_.refs_6_.refs_4_), channel_id=1, source_target_pairs={{0,24},{4,28},{8,16},{12,20},{16,8},{20,12},{24,0},{28,4},{1,25},{... | collective-permute-start | bytes 344072 | tf_op jit(solution)/shard_map/ppermute | solution.py:204
  14.7 4.8 %collective-permute-start.5 = (bf16[56,1024]{1,0:T(8,128)(2,1)S(1)}, bf16[56,1024]{1,0:T(8,128)(2,1)S(1)}, u32[]{:S(2)}, u32[]{:S(2)}) collective-permute-start(bf16[56,1024]{1,0:T(8,128)(2,1)S(1)} %pad_maximum_fusion.refs_1_.refs_3_.refs_6_.refs_4_), channel_id=1, source_target_pairs={{0,8},{4,12},{8,0},{12,4},{16,24},{20,28},{24,16},{28,20},{1,9},{5... | collective-permute-start | bytes 344072 | tf_op jit(solution)/shard_map/ppermute | solution.py:204
  15.2 4.9 %collective-permute-start.3 = (bf16[56,1024]{1,0:T(8,128)(2,1)S(1)}, bf16[56,1024]{1,0:T(8,128)(2,1)S(1)}, u32[]{:S(2)}, u32[]{:S(2)}) collective-permute-start(bf16[56,1024]{1,0:T(8,128)(2,1)S(1)} %pad_maximum_fusion.refs_1_.refs_3_.refs_6_.refs_4_), channel_id=1, source_target_pairs={{0,4},{4,0},{8,12},{12,8},{16,20},{20,16},{24,28},{28,24},{1,5},{5... | collective-permute-start | bytes 344072 | tf_op jit(solution)/shard_map/ppermute | solution.py:206
  19.1 4.3 %collective-permute-start.9 = (bf16[56,1024]{1,0:T(8,128)(2,1)S(1)}, bf16[56,1024]{1,0:T(8,128)(2,1)S(1)}, u32[]{:S(2)}, u32[]{:S(2)}) collective-permute-start(bf16[56,1024]{1,0:T(8,128)(2,1)S(1)} %collective-permute-done.6.refs_7_.refs_12_.refs_10_), channel_id=1, source_target_pairs={{0,4},{4,0},{8,12},{12,8},{16,20},{20,16},{24,28},{28,24},{1,5},{5... | collective-permute-start | bytes 344072 | tf_op jit(solution)/shard_map/ppermute | solution.py:206
  19.5 3.8 %collective-permute-start.7 = (bf16[56,1024]{1,0:T(8,128)(2,1)S(1)}, bf16[56,1024]{1,0:T(8,128)(2,1)S(1)}, u32[]{:S(2)}, u32[]{:S(2)}) collective-permute-start(bf16[56,1024]{1,0:T(8,128)(2,1)S(1)} %collective-permute-done.5.refs_5_.refs_8_.refs_6_), channel_id=1, source_target_pairs={{0,4},{4,0},{8,12},{12,8},{16,20},{20,16},{24,28},{28,24},{1,5},{5... | collective-permute-start | bytes 344072 | tf_op jit(solution)/shard_map/ppermute | solution.py:206
  19.6 3.8 %collective-permute-start.8 = (bf16[56,1024]{1,0:T(8,128)(2,1)S(1)}, bf16[56,1024]{1,0:T(8,128)(2,1)S(1)}, u32[]{:S(2)}, u32[]{:S(2)}) collective-permute-start(bf16[56,1024]{1,0:T(8,128)(2,1)S(1)} %slice.53.refs_6_.refs_10_.refs_8_), channel_id=1, source_target_pairs={{0,4},{4,0},{8,12},{12,8},{16,20},{20,16},{24,28},{28,24},{1,5},{5... | collective-permute-start | bytes 344072 | tf_op jit(solution)/shard_map/ppermute | solution.py:206
  28.2 1.3 %collective-permute-start.10 = (f32[8,1024]{1,0:T(8,128)S(1)}, f32[8,1024]{1,0:T(8,128)S(1)}, u32[]{:S(2)}, u32[]{:S(2)}) collective-permute-start(f32[8,1024]{1,0:T(8,128)S(1)} %shard_map.63.t), channel_id=1, source_target_pairs={{0,4},{4,0},{8,12},{12,8},{16,20},{20,16},{24,28},{28,24},{1,5},{5... | collective-permute-start | bytes 98312 | tf_op jit(solution)/shard_map/ppermute | solution.py:315
  29.5 4.0 %collective-permute-start.11 = (f32[8,1024]{1,0:T(8,128)S(1)}, f32[8,1024]{1,0:T(8,128)S(1)}, u32[]{:S(2)}, u32[]{:S(2)}) collective-permute-start(f32[8,1024]{1,0:T(8,128)S(1)} %shard_map.64.refs_0_), channel_id=1, source_target_pairs={{0,8},{4,12},{8,0},{12,4},{16,24},{20,28},{24,16},{28,20},{1,9},{5... | collective-permute-start | bytes 98312 | tf_op jit(solution)/shard_map/ppermute | solution.py:315
  40.5 1.3 %collective-permute-start.12 = (bf16[144,256]{1,0:T(8,128)(2,1)S(1)}, bf16[144,256]{1,0:T(8,128)(2,1)S(1)}, u32[]{:S(2)}, u32[]{:S(2)}) collective-permute-start(bf16[144,256]{1,0:T(8,128)(2,1)S(1)} %get-tuple-element.60), channel_id=1, source_target_pairs={{0,4},{4,0},{8,12},{12,8},{16,20},{20,16},{24,28},{28,24},{1,5},{5... | collective-permute-start | bytes 221192 | tf_op jit(solution)/shard_map/ppermute | solution.py:394
  41.8 4.1 %collective-permute-start.13 = (bf16[88,256]{1,0:T(8,128)(2,1)S(1)}, bf16[88,256]{1,0:T(8,128)(2,1)S(1)}, u32[]{:S(2)}, u32[]{:S(2)}) collective-permute-start(bf16[88,256]{1,0:T(8,128)(2,1)S(1)} %get-tuple-element.63), channel_id=1, source_target_pairs={{0,8},{4,12},{8,0},{12,4},{16,24},{20,28},{24,16},{28,20},{1,9},{5... | collective-permute-start | bytes 135176 | tf_op jit(solution)/shard_map/ppermute | solution.py:394

commit v3 on v2

v3 whole, which is shorter than its diff:
```python
import jax
import jax.numpy as jnp
import numpy as np
from jax import lax
from jax.experimental import pallas as pl
from jax.experimental.pallas import tpu as pltpu
from jax.sharding import PartitionSpec as P

D = 50
EPSILON_KERNEL = 0.05
SCALE = float(2.0 / (2.0 * D * EPSILON_KERNEL) / np.log(2.0))
EXT = 56
NORM_X, NORM_Y, B_ROW, A_ROW = D, D + 2, D + 4, D + 5
LANES, SUB = 128, 8


f32 = jnp.float32
bf16 = jnp.bfloat16
VM = pl.BlockSpec(memory_space=pltpu.VMEM)
ANY = pl.BlockSpec(memory_space=pl.ANY)


def ext_kernel(x_hbm, y_hbm, a_hbm, b_hbm, o_ref, xv, yv, av, bv, sx, sy, sems):
    copies = [
        pltpu.make_async_copy(src, dst, sems.at[i])
        for i, (src, dst) in enumerate(
            ((x_hbm, xv), (y_hbm, yv), (a_hbm, av), (b_hbm, bv))
        )
    ]
    for c in copies:
        c.start()
    for c in copies:
        c.wait()
    ny = yv.shape[1]
    for src, w, s, norm, one, w_row in (
        (xv, av, sx, NORM_X, NORM_Y, A_ROW),
        (yv, bv, sy, NORM_Y, NORM_X, B_ROW),
    ):
        c = src[...].astype(f32)
        n = -0.5 * jnp.sum(c * c, axis=0, keepdims=True)
        hi = n.astype(bf16).astype(f32)
        s[...] = jnp.zeros_like(s)
        s[0:D, :] = c
        s[norm : norm + 1, :] = hi
        s[norm + 1 : norm + 2, :] = n - hi
        s[one : one + 2, :] = jnp.ones((2, s.shape[1]), f32)
        s[w_row : w_row + 1, :] = w[...].astype(f32).reshape(1, -1)
    o_ref[:, 0:ny] = sy[...].astype(bf16)
    o_ref[:, ny:] = sx[...].astype(bf16)


def kernel_block(xt, y):
    s = lax.dot_general(xt, y, (((1,), (0,)), ((), ())), preferred_element_type=f32)
    return jnp.exp2(s * SCALE)


def add_lanes(acc, e):
    for t in range(e.shape[1] // LANES):
        acc = acc + e[:, t * LANES : (t + 1) * LANES]
    return acc


def make_blocks(xt, ys, ks, acc):
    for n, y in enumerate(ys):
        e = kernel_block(xt[...], y[...])
        if ks:
            ks[n][...] = e
        acc = add_lanes(acc, e)
    return acc


def spread(v, width):
    return jnp.concatenate([v] * (width // LANES), axis=1)


def groups(rows, body, init=0, unroll=8):
    n = rows // SUB

    def step(i, carry):
        return body(pl.ds(pl.multiple_of(i * SUB, SUB), SUB), carry)

    return lax.fori_loop(0, n, step, init, unroll=min(unroll, n))


def row_pass(k, v, acc, unroll):
    def body(rs, carry):
        acc[rs, :] = add_lanes(acc[rs, :], k[rs, :] * v)
        return carry

    groups(k.shape[0], body, unroll=unroll)


def col_pass(k, u, width, unroll):
    def body(rs, carry):
        return carry + k[rs, :] * spread(u[rs, :], width)

    return groups(k.shape[0], body, jnp.zeros((SUB, width), f32), unroll)


def scaling(weights, acc, u):
    u[...] = weights[...] / jnp.broadcast_to(
        jnp.sum(acc[...], axis=1, keepdims=True), u.shape
    )


class Refs:
    def __init__(self, refs):
        self.refs = list(refs)

    def take(self, *counts):
        out = []
        for n in counts:
            out.append(self.refs[:n] if isinstance(n, int) else self.refs[: n[0]][0])
            del self.refs[: n if isinstance(n, int) else n[0]]
        return out


ONE = (1,)


def xor_perm(n, m):
    return [(i, i ^ m) for i in range(n)]


def solution(mesh):
    rows, cols = mesh.shape["row"], mesh.shape["col"]

    def per_device(x_src, y_tgt, a_src, b_tgt):
        nx, ny = x_src.shape[1], y_tgt.shape[1]
        X, T = nx * cols, ny * cols
        kept = X * T * rows * 4 <= 24 * 2**20
        far = list(range(3, rows, 2))
        ends = [0] + far
        width = max(ny, LANES)
        per_row = T // width

        def held(shape, dtype):
            return pltpu.VMEM(shape, dtype) if kept else jax.ShapeDtypeStruct(shape, dtype)

        def call(kernel, outs, args, scratch=(), cost=None, spec=VM):
            return pl.pallas_call(
                kernel,
                out_shape=outs,
                in_specs=[spec] * len(args),
                out_specs=jax.tree.map(lambda _: VM, outs),
                scratch_shapes=scratch,
                compiler_params=pltpu.CompilerParams(vmem_limit_bytes=(4 if kept else 32) * 2**20),
                cost_estimate=cost,
            )(*args)

        def swap(t, m):
            return lax.ppermute(t, "row", xor_perm(rows, m))

        lanes_t = held((X, LANES), f32)
        lanes_s = pltpu.VMEM((X, LANES), f32)
        tot_t = jax.ShapeDtypeStruct((rows, T), f32)
        whole = X // SUB if kept else 8
        n_held = rows if kept else 1 + rows
        spare = [] if kept else [pltpu.VMEM((X, T), f32)]

        def blocks(held_refs, made):
            def get(i):
                if kept:
                    return held_refs[i]
                made[0][...] = kernel_block(held_refs[0][...], held_refs[1 + i][...])
                return made[0]

            return get

        own = call(
            ext_kernel,
            jax.ShapeDtypeStruct((EXT, ny + nx), bf16),
            [
                pltpu.with_memory_space_constraint(t, pltpu.HBM)
                for t in (x_src, y_tgt, a_src, b_tgt)
            ],
            [
                pltpu.VMEM((D, nx), bf16),
                pltpu.VMEM((D, ny), bf16),
                pltpu.VMEM((nx,), bf16),
                pltpu.VMEM((ny,), bf16),
                pltpu.VMEM((EXT, nx), f32),
                pltpu.VMEM((EXT, ny), f32),
                pltpu.SemaphoreType.DMA((4,)),
            ],
            spec=ANY,
        )
        line = [own] + [
            lax.ppermute(own, ("row", "col"), xor_perm(rows * cols, cols + m))
            for m in range(1, cols)
        ]
        both = jnp.concatenate(
            [p[:, 0:ny] for p in line] + [p[:, ny:] for p in line], axis=1
        )
        y0 = both[:, 0:T]
        y, ks = [None] * rows, [None] * rows
        y[0], xe = both[:, 0:T], both[:, T:]

        def start_kernel(e, y_ref, xt, ab, acc, *k):
            xt[...] = jnp.transpose(e[...].astype(f32)).astype(bf16)
            ab[...] = jnp.broadcast_to(xt[:, A_ROW : A_ROW + 1].astype(f32), ab.shape)
            acc[...] = make_blocks(xt, [y_ref], k, jnp.zeros(acc.shape, f32))

        def more_kernel(n, xt, acc, *refs):
            refs[n][...] = make_blocks(xt, refs[:n], refs[n + 1 :], acc[...])

        def more(new, acc):
            cost = pl.CostEstimate(flops=1, bytes_accessed=1, transcendentals=0)
            acc, *k = call(
                lambda *refs: more_kernel(len(new), *refs),
                [lanes_t] + [held((X, T), f32)] * (len(new) * kept),
                [xt, acc] + [y[i] for i in new],
                cost=cost,
            )
            if kept:
                for i, t in zip(new, k):
                    ks[i] = t
            return acc

        raw = {m: swap(y[0], m) for m in range(2, rows, 2)}
        y[1] = swap(y[0], 1)
        xt, ab, acc, *k = call(
            start_kernel,
            [held((X, EXT), bf16), lanes_t, lanes_t] + [held((X, T), f32)] * kept,
            [xe, y[0]],
            cost=pl.CostEstimate(flops=1, bytes_accessed=1, transcendentals=0),
        )
        if kept:
            ks[0] = k[0]
        acc = more([1], acc)
        evens, odds = list(range(2, rows, 2)), list(range(3, rows, 2))
        early, late = evens[:-1], evens[-1:]
        for some in (early, late):
            *lines, acc = lax.optimization_barrier((*[raw[m] for m in some], acc))
            for m, t in zip(some, lines):
                y[m] = t
                y[m + 1] = swap(t, 1)
            acc = more(some, acc)
        acc = more(odds[:-1], acc)
        acc = more(odds[-1:], acc)
        matrix = ks if kept else [xt, *y]

        def column_sums(k, u, tot, unroll):
            for i in range(rows):
                s = col_pass(k(i), u, T, unroll)
                tot[i : i + 1, :] = jnp.sum(s, axis=0, keepdims=True)

        def first_sums(*refs):
            r = Refs(refs)
            acc, ab, kr, tot, u = r.take(ONE, ONE, n_held, ONE, ONE)
            scaling(ab, acc, u)
            column_sums(blocks(kr, r.refs), u, tot, whole)

        tot = call(first_sums, tot_t, [acc, ab, *matrix], [lanes_s] + spare)

        def add_swapped(t, gs, masks):
            def row(i):
                return sum((g[i ^ m : (i ^ m) + 1] for g, m in zip(gs, masks)), t[i : i + 1])

            return jnp.concatenate([row(i) for i in range(rows)], axis=0)

        def add_kernel(t, g, o, send):
            o[...] = add_swapped(t[...], [g[...]], [1])
            send[...] = o[...].astype(bf16)

        tot, send = call(
            add_kernel,
            [tot_t, jax.ShapeDtypeStruct((rows, T), bf16)],
            [tot, swap(tot, 1)],
        )
        got = [swap(send, m) for m in far]

        n_tot = rows * per_row

        def pack_tot(t):
            return jnp.concatenate(
                [t[:, g * width : (g + 1) * width] for g in range(per_row)], axis=0
            ).astype(bf16)

        def unpack_tot(s):
            s = s.astype(f32)
            return jnp.concatenate(
                [s[g * rows : (g + 1) * rows, :] for g in range(per_row)], axis=1
            )

        def second(*refs):
            r = Refs(refs)
            t, gs, ab, x, bs, kr = r.take(ONE, len(far), ONE, ONE, rows, n_held)
            tot_o, keep_o, send_o, acc, u = r.take(ONE, ONE, ONE, ONE, ONE)
            k = blocks(kr, r.refs)
            total = add_swapped(t[...], [g[...].astype(f32) for g in gs], far)
            acc[...] = jnp.zeros_like(acc)
            for i in range(rows):
                v = bs[i][B_ROW : B_ROW + 1, :].astype(f32) / total[i : i + 1, :]
                row_pass(k(i), jnp.broadcast_to(v, (SUB, T)), acc, 32)
            scaling(ab, acc, u)
            column_sums(k, u, tot_o, 32)

            def weighted(mask):
                z = (k(mask)[:, 0:ny] * spread_to(u[...], ny)).astype(bf16)
                return jnp.dot(x[...], z, preferred_element_type=f32)

            send_o[0:n_tot, :] = pack_tot(tot_o[...])
            for n, mask in enumerate(ends):
                keep_o[n, :, 0:ny] = weighted(mask)
                at = n_tot + n * EXT
                send_o[at : at + EXT, 0:ny] = weighted(mask ^ 1).astype(bf16)

        def spread_to(u, n):
            return u[:, 0:n] if n <= LANES else spread(u, n)

        tot, keep, send = call(
            second,
            (
                tot_t,
                jax.ShapeDtypeStruct((len(ends), EXT, width), f32),
                jax.ShapeDtypeStruct((n_tot + len(ends) * EXT, width), bf16),
            ),
            [tot, *got, ab, xe, *y, *matrix],
            [lanes_s] * 2 + spare,
        )

        def join(t, kp, g, tot_o, keep_o, *sends):
            tot_o[...] = add_swapped(t[...], [unpack_tot(g[0:n_tot, :])], [1])
            packed = pack_tot(tot_o[...])
            for n in range(len(ends)):
                s = kp[n] + g[n_tot + n * EXT : n_tot + (n + 1) * EXT, :].astype(f32)
                if n == 0:
                    keep_o[...] = s
                else:
                    sends[n - 1][0:n_tot, :] = packed
                    sends[n - 1][n_tot:, :] = s.astype(bf16)

        tot, keep, *send = call(
            join,
            [tot_t, jax.ShapeDtypeStruct((EXT, width), f32)]
            + [jax.ShapeDtypeStruct((n_tot + EXT, width), bf16)] * len(far),
            [tot, keep, swap(send, 1)],
        )
        got = [swap(t, m) for t, m in zip(send, far)]

        def final(*refs):
            r = Refs(refs)
            t, kp, gs, xt, ys = r.take(ONE, ONE, len(far), ONE, rows)
            kr, src_o, tgt_o = r.take(rows * kept, ONE, ONE)
            total = add_swapped(t[...], [unpack_tot(g[0:n_tot, :]) for g in gs], far)
            num = sum((g[n_tot:, :].astype(f32) for g in gs), kp[...])
            tgt_o[...] = num[0:D, 0:ny] / total[0:1, 0:ny]
            res = jnp.zeros((nx, EXT), f32)
            for i in range(rows):
                yi = ys[i][...]
                v = yi[B_ROW : B_ROW + 1, :].astype(f32) / total[i : i + 1, :]
                e = kr[i][0:nx, :] if kept else kernel_block(xt[0:nx, :], yi)
                res = res + lax.dot_general(
                    (e * v).astype(bf16),
                    yi,
                    (((1,), (1,)), ((), ())),
                    preferred_element_type=f32,
                )
            res = jnp.transpose(res)
            src_o[...] = res[0:D, :] / res[NORM_X : NORM_X + 1, :]

        return tuple(
            call(
                final,
                (
                    jax.ShapeDtypeStruct((D, nx), f32),
                    jax.ShapeDtypeStruct((D, ny), f32),
                ),
                [tot, keep, *got, xt, *y, *(ks if kept else [])],
            )
        )

    spec = P(None, ("row", "col"))
    vec = P(("row", "col"))
    return jax.shard_map(
        per_device,
        mesh=mesh,
        in_specs=(spec, spec, vec, vec),
        out_specs=(spec, spec),
        check_vma=False,
    )
```

time: 47.6 us -> 43.1 us (0.905)
  Pallas kernels: 17.3 us -> 10.2 us
  starting transfers between devices: 12.9 us -> 17.1 us
  waiting for transfers between devices: 16.3 us -> 14.8 us
    pallas_call x9 -> x12, Pallas kernels: 17.3 us -> 10.2 us  [call(): pl.pallas_call(kernel, out_shape=outs, in_specs=[spec] * len(args), out_s...]
    ppermute x14 -> x18, starting transfers between devices: 12.9 us -> 17.1 us  [the longest x15 11.6 us: swap(): return lax.ppermute(t, 'row', xor_perm(rows, m))]
    ppermute x14 -> x18, waiting for transfers between devices: 16.3 us -> 14.8 us  [the longest x15 11 us: swap(): return lax.ppermute(t, 'row', xor_perm(rows, m))]
  transfers between devices with their start and end apart: 14 -> 18, of which waited for: 8 -> 14; matrix products, arithmetic and copies ran while one was open for 0% -> 0% of each run, Pallas kernels for 7% -> 6%
where the time goes in v3:
time: 43.1 us; the launch traced here: 42.8 us
  starting transfers between devices  17.1 us (40%)
  waiting for transfers between devices  14.8 us (34%)
  Pallas kernels  10.2 us (24%)
  between operations  0.77 us (2%)
    ppermute x15, starting transfers between devices, swap(): return lax.ppermute(t, 'row', xor_perm(rows, m))  11.6 us
    ppermute x15, waiting for transfers between devices, swap(): return lax.ppermute(t, 'row', xor_perm(rows, m))  11 us
    pallas_call x12, Pallas kernels, call(): pl.pallas_call(kernel, out_shape=outs, in_specs=[spec] * len(args), out_s...  10.2 us
    ppermute x3, starting transfers between devices, per_device(): lax.ppermute(own, ('row', 'col'), xor_perm(rows * cols, cols + m))  5.48 us
    ppermute x3, waiting for transfers between devices, per_device(): lax.ppermute(own, ('row', 'col'), xor_perm(rows * cols, cols + m))  3.83 us
  transfers between devices with their start and end apart: 18, of which 14 were waited for; matrix products, arithmetic and copies ran while one was open for 0% of the time, Pallas kernels for 6%

profile of v3, /device:TPU:0, one launch (start us, length us, event | category | flops | bytes accessed | tf_op | source)
XLA Modules:
  0.0 42.8 jit_solution(17745370762535784851)
XLA Ops:
  0.6 0.8 %shard_map.59 = bf16[56,384]{1,0:T(8,128)(2,1)S(1)} custom-call(bf16[50,128]{1,0:T(8,128)(2,1)} %x_hbm.1, bf16[50,256]{1,0:T(8,128)(2,1)} %y_hbm.1, bf16[128]{0:T(256)(128)(2,1)} %a_hbm.1, bf16[256]{0:T(256)(128)(2,1)} %b_hbm.1), custom_call_target="tpu_custom_call" | custom-call | tf_op jit(solution)/shard_map/pallas_call | solution.py:141
  1.5 4.6 %collective-permute-start.2 = (bf16[56,384]{1,0:T(8,128)(2,1)S(1)}, bf16[56,384]{1,0:T(8,128)(2,1)S(1)}, u32[]{:S(2)}, u32[]{:S(2)}) collective-permute-start(bf16[56,384]{1,0:T(8,128)(2,1)S(1)} %shard_map.59), channel_id=1, source_target_pairs={{0,7},{1,6},{2,5},{3,4},{4,3},{5,2},{6,1},{7,0},{8,15},{9,14},{10,... | collective-permute-start | bytes 129032 | tf_op jit(solution)/shard_map/ppermute | solution.py:189
  6.0 0.9 %collective-permute-start = (bf16[56,384]{1,0:T(8,128)(2,1)S(1)}, bf16[56,384]{1,0:T(8,128)(2,1)S(1)}, u32[]{:S(2)}, u32[]{:S(2)}) collective-permute-start(bf16[56,384]{1,0:T(8,128)(2,1)S(1)} %shard_map.59), channel_id=1, source_target_pairs={{0,5},{1,4},{2,7},{3,6},{4,1},{5,0},{6,3},{7,2},{8,13},{9,12},{10,... | collective-permute-start | bytes 129032 | tf_op jit(solution)/shard_map/ppermute | solution.py:189
  7.0 1.1 %collective-permute-done.2 = bf16[56,384]{1,0:T(8,128)(2,1)S(1)} collective-permute-done((bf16[56,384]{1,0:T(8,128)(2,1)S(1)}, bf16[56,384]{1,0:T(8,128)(2,1)S(1)}, u32[]{:S(2)}, u32[]{:S(2)}) %collective-permute-start.2) | collective-permute-done | bytes 43040 | tf_op jit(solution)/shard_map/ppermute | solution.py:189
  8.0 2.8 %collective-permute-done.1 = bf16[56,384]{1,0:T(8,128)(2,1)S(1)} collective-permute-done((bf16[56,384]{1,0:T(8,128)(2,1)S(1)}, bf16[56,384]{1,0:T(8,128)(2,1)S(1)}, u32[]{:S(2)}, u32[]{:S(2)}) %collective-permute-start.1) | collective-permute-done | bytes 43040 | tf_op jit(solution)/shard_map/ppermute | solution.py:189
  11.2 1.5 %collective-permute-start.5 = (bf16[56,1024]{1,0:T(8,128)(2,1)S(1)}, bf16[56,1024]{1,0:T(8,128)(2,1)S(1)}, u32[]{:S(2)}, u32[]{:S(2)}) collective-permute-start(bf16[56,1024]{1,0:T(8,128)(2,1)S(1)} %pad_maximum_fusion.y_ref.refs_6_), channel_id=1, source_target_pairs={{0,16},{4,20},{8,24},{12,28},{16,0},{20,4},{24,8},{28,12},{1,17},{... | collective-permute-start | bytes 344072 | tf_op jit(solution)/shard_map/ppermute | solution.py:152
  12.7 1.5 %collective-permute-start.4 = (bf16[56,1024]{1,0:T(8,128)(2,1)S(1)}, bf16[56,1024]{1,0:T(8,128)(2,1)S(1)}, u32[]{:S(2)}, u32[]{:S(2)}) collective-permute-start(bf16[56,1024]{1,0:T(8,128)(2,1)S(1)} %pad_maximum_fusion.y_ref.refs_6_), channel_id=1, source_target_pairs={{0,8},{4,12},{8,0},{12,4},{16,24},{20,28},{24,16},{28,20},{1,9},{5... | collective-permute-start | bytes 344072 | tf_op jit(solution)/shard_map/ppermute | solution.py:152
  14.2 0.5 %collective-permute-start.3 = (bf16[56,1024]{1,0:T(8,128)(2,1)S(1)}, bf16[56,1024]{1,0:T(8,128)(2,1)S(1)}, u32[]{:S(2)}, u32[]{:S(2)}) collective-permute-start(bf16[56,1024]{1,0:T(8,128)(2,1)S(1)} %pad_maximum_fusion.y_ref.refs_6_), channel_id=1, source_target_pairs={{0,24},{4,28},{8,16},{12,20},{16,8},{20,12},{24,0},{28,4},{1,25},{... | collective-permute-start | bytes 344072 | tf_op jit(solution)/shard_map/ppermute | solution.py:152
  14.7 0.5 %shard_map.60 = (bf16[512,56]{1,0:T(8,128)(2,1)S(1)}, f32[512,128]{1,0:T(8,128)S(1)}, f32[512,128]{1,0:T(8,128)S(1)}, f32[512,1024]{1,0:T(8,128)S(1)}) custom-call(bf16[56,512]{1,0:T(8,128)(2,1)S(1)} %pad_maximum_fusion.1.e.refs_5_, bf16[56,1024]{1,0:T(8,128)(2,1)S(1)} %pad_maximum_fusion.y_ref.refs_6_), custom_call_target="tpu_custom_call" | custom-call | flops 1 | bytes 1 | tf_op jit(solution)/shard_map/pallas_call | solution.py:141
  15.3 0.4 shard_map.61
  15.7 0.8 %collective-permute-done.5.refs_3_.refs_10_ = bf16[56,1024]{1,0:T(8,128)(2,1)S(1)} collective-permute-done((bf16[56,1024]{1,0:T(8,128)(2,1)S(1)}, bf16[56,1024]{1,0:T(8,128)(2,1)S(1)}, u32[]{:S(2)}, u32[]{:S(2)}) %collective-permute-start.5) | collective-permute-done | bytes 114720 | tf_op jit(solution)/shard_map/ppermute | solution.py:152
  16.4 2.3 %collective-permute-done.4.refs_2_.refs_8_ = bf16[56,1024]{1,0:T(8,128)(2,1)S(1)} collective-permute-done((bf16[56,1024]{1,0:T(8,128)(2,1)S(1)}, bf16[56,1024]{1,0:T(8,128)(2,1)S(1)}, u32[]{:S(2)}, u32[]{:S(2)}) %collective-permute-start.4) | collective-permute-done | bytes 114720 | tf_op jit(solution)/shard_map/ppermute | solution.py:152
  18.7 0.5 %collective-permute-start.8 = (bf16[56,1024]{1,0:T(8,128)(2,1)S(1)}, bf16[56,1024]{1,0:T(8,128)(2,1)S(1)}, u32[]{:S(2)}, u32[]{:S(2)}) collective-permute-start(bf16[56,1024]{1,0:T(8,128)(2,1)S(1)} %collective-permute-done.5.refs_3_.refs_10_), channel_id=1, source_target_pairs={{0,4},{4,0},{8,12},{12,8},{16,20},{20,16},{24,28},{28,24},{1,5},{5... | collective-permute-start | bytes 344072 | tf_op jit(solution)/shard_map/ppermute | solution.py:152
  19.2 0.7 %shard_map.62 = (f32[512,128]{1,0:T(8,128)S(1)}, f32[512,1024]{1,0:T(8,128)S(1)}, f32[512,1024]{1,0:T(8,128)S(1)}) custom-call(bf16[512,56]{1,0:T(8,128)(2,1)S(1)} %get-tuple-element.33.refs_0_.refs_5_, f32[512,128]{1,0:T(8,128)S(1)} %get-tuple-element.36.refs_1_, bf16[56,1024]{1,0:T(8,128)(2,1)S(1)} %collective-permute-done.4.refs_2_.refs_8_, ...), custom_call_target="tpu_custom_call" | custom-call | flops 1 | bytes 1 | tf_op jit(solution)/shard_map/pallas_call | solution.py:141
  20.1 0.4 shard_map.63
  20.5 0.7 %shard_map.64 = (f32[512,128]{1,0:T(8,128)S(1)}, f32[512,1024]{1,0:T(8,128)S(1)}, f32[512,1024]{1,0:T(8,128)S(1)}) custom-call(bf16[512,56]{1,0:T(8,128)(2,1)S(1)} %get-tuple-element.33.refs_0_.refs_5_, f32[512,128]{1,0:T(8,128)S(1)} %get-tuple-element.42.refs_1_, bf16[56,1024]{1,0:T(8,128)(2,1)S(1)} %collective-permute-done.7.refs_2_.refs_9_, ...), custom_call_target="tpu_custom_call" | custom-call | flops 1 | bytes 1 | tf_op jit(solution)/shard_map/pallas_call | solution.py:141
  21.4 0.4 shard_map.65
  21.8 1.3 %shard_map.66.t = f32[8,1024]{1,0:T(8,128)S(1)} custom-call(f32[512,128]{1,0:T(8,128)S(1)} %get-tuple-element.44.refs_0_, f32[512,128]{1,0:T(8,128)S(1)} %get-tuple-element.45.refs_1_.refs_4_, f32[512,1024]{1,0:T(8,128)S(1)} %get-tuple-element.46.refs_2_.refs_14_, f32[512,1024]{1,0:T(8,128)S(1)} %get-tuple-element.47.refs_3_.refs_15_, ...), custom_call_target="tpu_custom_call" | custom-call | tf_op jit(solution)/shard_map/pallas_call | solution.py:141
  23.1 0.4 collective-permute-start.10
  23.6 0.9 %collective-permute-done.10.g = f32[8,1024]{1,0:T(8,128)S(1)} collective-permute-done((f32[8,1024]{1,0:T(8,128)S(1)}, f32[8,1024]{1,0:T(8,128)S(1)}, u32[]{:S(2)}, u32[]{:S(2)}) %collective-permute-start.10) | collective-permute-done | bytes 32800 | tf_op jit(solution)/shard_map/ppermute | solution.py:152
  24.4 2.5 %collective-permute-start.13 = (bf16[8,1024]{1,0:T(8,128)(2,1)S(1)}, bf16[8,1024]{1,0:T(8,128)(2,1)S(1)}, u32[]{:S(2)}, u32[]{:S(2)}) collective-permute-start(bf16[8,1024]{1,0:T(8,128)(2,1)S(1)} %get-tuple-element.55), channel_id=1, source_target_pairs={{0,28},{4,24},{8,20},{12,16},{16,12},{20,8},{24,4},{28,0},{1,29},{... | collective-permute-start | bytes 49160 | tf_op jit(solution)/shard_map/ppermute | solution.py:152
  27.2 0.5 %collective-permute-start.11 = (bf16[8,1024]{1,0:T(8,128)(2,1)S(1)}, bf16[8,1024]{1,0:T(8,128)(2,1)S(1)}, u32[]{:S(2)}, u32[]{:S(2)}) collective-permute-start(bf16[8,1024]{1,0:T(8,128)(2,1)S(1)} %get-tuple-element.55), channel_id=1, source_target_pairs={{0,12},{4,8},{8,4},{12,0},{16,28},{20,24},{24,20},{28,16},{1,13},{... | collective-permute-start | bytes 49160 | tf_op jit(solution)/shard_map/ppermute | solution.py:152
  27.7 0.9 %collective-permute-done.13.refs_3_ = bf16[8,1024]{1,0:T(8,128)(2,1)S(1)} collective-permute-done((bf16[8,1024]{1,0:T(8,128)(2,1)S(1)}, bf16[8,1024]{1,0:T(8,128)(2,1)S(1)}, u32[]{:S(2)}, u32[]{:S(2)}) %collective-permute-start.13) | collective-permute-done | bytes 16416 | tf_op jit(solution)/shard_map/ppermute | solution.py:152
  28.6 1.5 %collective-permute-done.12.refs_2_ = bf16[8,1024]{1,0:T(8,128)(2,1)S(1)} collective-permute-done((bf16[8,1024]{1,0:T(8,128)(2,1)S(1)}, bf16[8,1024]{1,0:T(8,128)(2,1)S(1)}, u32[]{:S(2)}, u32[]{:S(2)}) %collective-permute-start.12) | collective-permute-done | bytes 16416 | tf_op jit(solution)/shard_map/ppermute | solution.py:152
  30.4 3.4 %shard_map.68 = (f32[8,1024]{1,0:T(8,128)S(1)}, f32[4,56,256]{2,1,0:T(8,128)S(1)}, bf16[256,256]{1,0:T(8,128)(2,1)S(1)}) custom-call(f32[8,1024]{1,0:T(8,128)S(1)} %get-tuple-element.54.refs_0_, bf16[8,1024]{1,0:T(8,128)(2,1)S(1)} %collective-permute-done.11.refs_1_, bf16[8,1024]{1,0:T(8,128)(2,1)S(1)} %collective-permute-done.12.refs_2_, ...), custom_call_target="tpu_custom_call" | custom-call | tf_op jit(solution)/shard_map/pallas_call | solution.py:141
  34.2 1.0 %collective-permute-done.14.g = bf16[256,256]{1,0:T(8,128)(2,1)S(1)} collective-permute-done((bf16[256,256]{1,0:T(8,128)(2,1)S(1)}, bf16[256,256]{1,0:T(8,128)(2,1)S(1)}, u32[]{:S(2)}, u32[]{:S(2)}) %collective-permute-start.14) | collective-permute-done | bytes 131104 | tf_op jit(solution)/shard_map/ppermute | solution.py:152
  35.2 0.5 %collective-permute-start.15 = (bf16[88,256]{1,0:T(8,128)(2,1)S(1)}, bf16[88,256]{1,0:T(8,128)(2,1)S(1)}, u32[]{:S(2)}, u32[]{:S(2)}) collective-permute-start(bf16[88,256]{1,0:T(8,128)(2,1)S(1)} %get-tuple-element.61), channel_id=1, source_target_pairs={{0,12},{4,8},{8,4},{12,0},{16,28},{20,24},{24,20},{28,16},{1,13},{... | collective-permute-start | bytes 135176 | tf_op jit(solution)/shard_map/ppermute | solution.py:152
  35.8 1.3 %collective-permute-start.16 = (bf16[88,256]{1,0:T(8,128)(2,1)S(1)}, bf16[88,256]{1,0:T(8,128)(2,1)S(1)}, u32[]{:S(2)}, u32[]{:S(2)}) collective-permute-start(bf16[88,256]{1,0:T(8,128)(2,1)S(1)} %get-tuple-element.62), channel_id=1, source_target_pairs={{0,20},{4,16},{8,28},{12,24},{16,4},{20,0},{24,12},{28,8},{1,21},{... | collective-permute-start | bytes 135176 | tf_op jit(solution)/shard_map/ppermute | solution.py:152
  37.1 1.4 %collective-permute-start.17 = (bf16[88,256]{1,0:T(8,128)(2,1)S(1)}, bf16[88,256]{1,0:T(8,128)(2,1)S(1)}, u32[]{:S(2)}, u32[]{:S(2)}) collective-permute-start(bf16[88,256]{1,0:T(8,128)(2,1)S(1)} %get-tuple-element.63), channel_id=1, source_target_pairs={{0,28},{4,24},{8,20},{12,16},{16,12},{20,8},{24,4},{28,0},{1,29},{... | collective-permute-start | bytes 135176 | tf_op jit(solution)/shard_map/ppermute | solution.py:152
  38.8 0.7 %collective-permute-done.16.refs_3_ = bf16[88,256]{1,0:T(8,128)(2,1)S(1)} collective-permute-done((bf16[88,256]{1,0:T(8,128)(2,1)S(1)}, bf16[88,256]{1,0:T(8,128)(2,1)S(1)}, u32[]{:S(2)}, u32[]{:S(2)}) %collective-permute-start.16) | collective-permute-done | bytes 45088 | tf_op jit(solution)/shard_map/ppermute | solution.py:152
  39.4 2.0 %collective-permute-done.17.refs_4_ = bf16[88,256]{1,0:T(8,128)(2,1)S(1)} collective-permute-done((bf16[88,256]{1,0:T(8,128)(2,1)S(1)}, bf16[88,256]{1,0:T(8,128)(2,1)S(1)}, u32[]{:S(2)}, u32[]{:S(2)}) %collective-permute-start.17) | collective-permute-done | bytes 45088 | tf_op jit(solution)/shard_map/ppermute | solution.py:152
  41.4 1.4 %shard_map.70 = (f32[50,128]{1,0:T(8,128)}, f32[50,256]{1,0:T(8,128)}) custom-call(f32[8,1024]{1,0:T(8,128)S(1)} %get-tuple-element.59.refs_0_, f32[56,256]{1,0:T(8,128)S(1)} %get-tuple-element.60.refs_1_, bf16[88,256]{1,0:T(8,128)(2,1)S(1)} %collective-permute-done.15.refs_2_, bf16[88,256]{1,0:T(8,128)(2,1)S(1)} %collective-permute-done.16.refs_3_, ...), custom_call_target="tpu_custom_call" | custom-call | tf_op jit(solution)/shard_map/pallas_call | solution.py:141
  (26 shorter events, 2.1 us)
Async XLA Ops:
  1.5 6.6 %collective-permute-start.2 = (bf16[56,384]{1,0:T(8,128)(2,1)S(1)}, bf16[56,384]{1,0:T(8,128)(2,1)S(1)}, u32[]{:S(2)}, u32[]{:S(2)}) collective-permute-start(bf16[56,384]{1,0:T(8,128)(2,1)S(1)} %shard_map.59), channel_id=1, source_target_pairs={{0,7},{1,6},{2,5},{3,4},{4,3},{5,2},{6,1},{7,0},{8,15},{9,14},{10,... | collective-permute-start | bytes 129032 | tf_op jit(solution)/shard_map/ppermute | solution.py:189
  6.0 4.8 %collective-permute-start.1 = (bf16[56,384]{1,0:T(8,128)(2,1)S(1)}, bf16[56,384]{1,0:T(8,128)(2,1)S(1)}, u32[]{:S(2)}, u32[]{:S(2)}) collective-permute-start(bf16[56,384]{1,0:T(8,128)(2,1)S(1)} %shard_map.59), channel_id=1, source_target_pairs={{0,6},{1,7},{2,4},{3,5},{4,2},{5,3},{6,0},{7,1},{8,14},{9,15},{10,... | collective-permute-start | bytes 129032 | tf_op jit(solution)/shard_map/ppermute | solution.py:189
  6.0 4.8 %collective-permute-start = (bf16[56,384]{1,0:T(8,128)(2,1)S(1)}, bf16[56,384]{1,0:T(8,128)(2,1)S(1)}, u32[]{:S(2)}, u32[]{:S(2)}) collective-permute-start(bf16[56,384]{1,0:T(8,128)(2,1)S(1)} %shard_map.59), channel_id=1, source_target_pairs={{0,5},{1,4},{2,7},{3,6},{4,1},{5,0},{6,3},{7,2},{8,13},{9,12},{10,... | collective-permute-start | bytes 129032 | tf_op jit(solution)/shard_map/ppermute | solution.py:189
  10.8 4.4 %collective-permute-start.6 = (bf16[56,1024]{1,0:T(8,128)(2,1)S(1)}, bf16[56,1024]{1,0:T(8,128)(2,1)S(1)}, u32[]{:S(2)}, u32[]{:S(2)}) collective-permute-start(bf16[56,1024]{1,0:T(8,128)(2,1)S(1)} %pad_maximum_fusion.y_ref.refs_6_), channel_id=1, source_target_pairs={{0,4},{4,0},{8,12},{12,8},{16,20},{20,16},{24,28},{28,24},{1,5},{5... | collective-permute-start | bytes 344072 | tf_op jit(solution)/shard_map/ppermute | solution.py:152
  11.2 5.3 %collective-permute-start.5 = (bf16[56,1024]{1,0:T(8,128)(2,1)S(1)}, bf16[56,1024]{1,0:T(8,128)(2,1)S(1)}, u32[]{:S(2)}, u32[]{:S(2)}) collective-permute-start(bf16[56,1024]{1,0:T(8,128)(2,1)S(1)} %pad_maximum_fusion.y_ref.refs_6_), channel_id=1, source_target_pairs={{0,16},{4,20},{8,24},{12,28},{16,0},{20,4},{24,8},{28,12},{1,17},{... | collective-permute-start | bytes 344072 | tf_op jit(solution)/shard_map/ppermute | solution.py:152
  12.7 6.0 %collective-permute-start.4 = (bf16[56,1024]{1,0:T(8,128)(2,1)S(1)}, bf16[56,1024]{1,0:T(8,128)(2,1)S(1)}, u32[]{:S(2)}, u32[]{:S(2)}) collective-permute-start(bf16[56,1024]{1,0:T(8,128)(2,1)S(1)} %pad_maximum_fusion.y_ref.refs_6_), channel_id=1, source_target_pairs={{0,8},{4,12},{8,0},{12,4},{16,24},{20,28},{24,16},{28,20},{1,9},{5... | collective-permute-start | bytes 344072 | tf_op jit(solution)/shard_map/ppermute | solution.py:152
  14.2 5.9 %collective-permute-start.3 = (bf16[56,1024]{1,0:T(8,128)(2,1)S(1)}, bf16[56,1024]{1,0:T(8,128)(2,1)S(1)}, u32[]{:S(2)}, u32[]{:S(2)}) collective-permute-start(bf16[56,1024]{1,0:T(8,128)(2,1)S(1)} %pad_maximum_fusion.y_ref.refs_6_), channel_id=1, source_target_pairs={{0,24},{4,28},{8,16},{12,20},{16,8},{20,12},{24,0},{28,4},{1,25},{... | collective-permute-start | bytes 344072 | tf_op jit(solution)/shard_map/ppermute | solution.py:152
  18.7 1.8 %collective-permute-start.7 = (bf16[56,1024]{1,0:T(8,128)(2,1)S(1)}, bf16[56,1024]{1,0:T(8,128)(2,1)S(1)}, u32[]{:S(2)}, u32[]{:S(2)}) collective-permute-start(bf16[56,1024]{1,0:T(8,128)(2,1)S(1)} %collective-permute-done.4.refs_2_.refs_8_), channel_id=1, source_target_pairs={{0,4},{4,0},{8,12},{12,8},{16,20},{20,16},{24,28},{28,24},{1,5},{5... | collective-permute-start | bytes 344072 | tf_op jit(solution)/shard_map/ppermute | solution.py:152
  18.7 1.8 %collective-permute-start.8 = (bf16[56,1024]{1,0:T(8,128)(2,1)S(1)}, bf16[56,1024]{1,0:T(8,128)(2,1)S(1)}, u32[]{:S(2)}, u32[]{:S(2)}) collective-permute-start(bf16[56,1024]{1,0:T(8,128)(2,1)S(1)} %collective-permute-done.5.refs_3_.refs_10_), channel_id=1, source_target_pairs={{0,4},{4,0},{8,12},{12,8},{16,20},{20,16},{24,28},{28,24},{1,5},{5... | collective-permute-start | bytes 344072 | tf_op jit(solution)/shard_map/ppermute | solution.py:152
  20.1 1.3 %collective-permute-start.9 = (bf16[56,1024]{1,0:T(8,128)(2,1)S(1)}, bf16[56,1024]{1,0:T(8,128)(2,1)S(1)}, u32[]{:S(2)}, u32[]{:S(2)}) collective-permute-start(bf16[56,1024]{1,0:T(8,128)(2,1)S(1)} %collective-permute-done.3.refs_2_.refs_12_), channel_id=1, source_target_pairs={{0,4},{4,0},{8,12},{12,8},{16,20},{20,16},{24,28},{28,24},{1,5},{5... | collective-permute-start | bytes 344072 | tf_op jit(solution)/shard_map/ppermute | solution.py:152
  23.1 1.3 %collective-permute-start.10 = (f32[8,1024]{1,0:T(8,128)S(1)}, f32[8,1024]{1,0:T(8,128)S(1)}, u32[]{:S(2)}, u32[]{:S(2)}) collective-permute-start(f32[8,1024]{1,0:T(8,128)S(1)} %shard_map.66.t), channel_id=1, source_target_pairs={{0,4},{4,0},{8,12},{12,8},{16,20},{20,16},{24,28},{28,24},{1,5},{5... | collective-permute-start | bytes 98312 | tf_op jit(solution)/shard_map/ppermute | solution.py:152
  24.4 4.1 %collective-permute-start.13 = (bf16[8,1024]{1,0:T(8,128)(2,1)S(1)}, bf16[8,1024]{1,0:T(8,128)(2,1)S(1)}, u32[]{:S(2)}, u32[]{:S(2)}) collective-permute-start(bf16[8,1024]{1,0:T(8,128)(2,1)S(1)} %get-tuple-element.55), channel_id=1, source_target_pairs={{0,28},{4,24},{8,20},{12,16},{16,12},{20,8},{24,4},{28,0},{1,29},{... | collective-permute-start | bytes 49160 | tf_op jit(solution)/shard_map/ppermute | solution.py:152
  26.9 3.2 %collective-permute-start.12 = (bf16[8,1024]{1,0:T(8,128)(2,1)S(1)}, bf16[8,1024]{1,0:T(8,128)(2,1)S(1)}, u32[]{:S(2)}, u32[]{:S(2)}) collective-permute-start(bf16[8,1024]{1,0:T(8,128)(2,1)S(1)} %get-tuple-element.55), channel_id=1, source_target_pairs={{0,20},{4,16},{8,28},{12,24},{16,4},{20,0},{24,12},{28,8},{1,21},{... | collective-permute-start | bytes 49160 | tf_op jit(solution)/shard_map/ppermute | solution.py:152
  27.2 3.2 %collective-permute-start.11 = (bf16[8,1024]{1,0:T(8,128)(2,1)S(1)}, bf16[8,1024]{1,0:T(8,128)(2,1)S(1)}, u32[]{:S(2)}, u32[]{:S(2)}) collective-permute-start(bf16[8,1024]{1,0:T(8,128)(2,1)S(1)} %get-tuple-element.55), channel_id=1, source_target_pairs={{0,12},{4,8},{8,4},{12,0},{16,28},{20,24},{24,20},{28,16},{1,13},{... | collective-permute-start | bytes 49160 | tf_op jit(solution)/shard_map/ppermute | solution.py:152
  33.8 1.4 %collective-permute-start.14 = (bf16[256,256]{1,0:T(8,128)(2,1)S(1)}, bf16[256,256]{1,0:T(8,128)(2,1)S(1)}, u32[]{:S(2)}, u32[]{:S(2)}) collective-permute-start(bf16[256,256]{1,0:T(8,128)(2,1)S(1)} %get-tuple-element.58), channel_id=1, source_target_pairs={{0,4},{4,0},{8,12},{12,8},{16,20},{20,16},{24,28},{28,24},{1,5},{5... | collective-permute-start | bytes 393224 | tf_op jit(solution)/shard_map/ppermute | solution.py:152
  35.2 3.5 %collective-permute-start.15 = (bf16[88,256]{1,0:T(8,128)(2,1)S(1)}, bf16[88,256]{1,0:T(8,128)(2,1)S(1)}, u32[]{:S(2)}, u32[]{:S(2)}) collective-permute-start(bf16[88,256]{1,0:T(8,128)(2,1)S(1)} %get-tuple-element.61), channel_id=1, source_target_pairs={{0,12},{4,8},{8,4},{12,0},{16,28},{20,24},{24,20},{28,16},{1,13},{... | collective-permute-start | bytes 135176 | tf_op jit(solution)/shard_map/ppermute | solution.py:152
  35.8 3.7 %collective-permute-start.16 = (bf16[88,256]{1,0:T(8,128)(2,1)S(1)}, bf16[88,256]{1,0:T(8,128)(2,1)S(1)}, u32[]{:S(2)}, u32[]{:S(2)}) collective-permute-start(bf16[88,256]{1,0:T(8,128)(2,1)S(1)} %get-tuple-element.62), channel_id=1, source_target_pairs={{0,20},{4,16},{8,28},{12,24},{16,4},{20,0},{24,12},{28,8},{1,21},{... | collective-permute-start | bytes 135176 | tf_op jit(solution)/shard_map/ppermute | solution.py:152
  37.1 4.4 %collective-permute-start.17 = (bf16[88,256]{1,0:T(8,128)(2,1)S(1)}, bf16[88,256]{1,0:T(8,128)(2,1)S(1)}, u32[]{:S(2)}, u32[]{:S(2)}) collective-permute-start(bf16[88,256]{1,0:T(8,128)(2,1)S(1)} %get-tuple-element.63), channel_id=1, source_target_pairs={{0,28},{4,24},{8,20},{12,16},{16,12},{20,8},{24,4},{28,0},{1,29},{... | collective-permute-start | bytes 135176 | tf_op jit(solution)/shard_map/ppermute | solution.py:152

commit v4 on v3

--- a/solution.py
+++ b/solution.py
@@ -283,18 +283,31 @@
                 [s[g * rows : (g + 1) * rows, :] for g in range(per_row)], axis=1
             )
 
-        def second(*refs):
+        def second_rows(*refs):
             r = Refs(refs)
-            t, gs, ab, x, bs, kr = r.take(ONE, len(far), ONE, ONE, rows, n_held)
-            tot_o, keep_o, send_o, acc, u = r.take(ONE, ONE, ONE, ONE, ONE)
+            t, gs, ab, bs, kr = r.take(ONE, len(far), ONE, rows, n_held)
+            u, acc = r.take(ONE, ONE)
             k = blocks(kr, r.refs)
             total = add_swapped(t[...], [g[...].astype(f32) for g in gs], far)
             acc[...] = jnp.zeros_like(acc)
             for i in range(rows):
                 v = bs[i][B_ROW : B_ROW + 1, :].astype(f32) / total[i : i + 1, :]
-                row_pass(k(i), jnp.broadcast_to(v, (SUB, T)), acc, 32)
+                row_pass(k(i), jnp.broadcast_to(v, (SUB, T)), acc, 64)
             scaling(ab, acc, u)
-            column_sums(k, u, tot_o, 32)
+
+        u = call(
+            second_rows,
+            lanes_t,
+            [tot, *got, ab, *y, *matrix],
+            [lanes_s] + spare,
+        )
+
+        def second_cols(*refs):
+            r = Refs(refs)
+            u, x, kr = r.take(ONE, ONE, n_held)
+            tot_o, keep_o, send_o = r.take(ONE, ONE, ONE)
+            k = blocks(kr, r.refs)
+            column_sums(k, u, tot_o, 64)
 
             def weighted(mask):
                 z = (k(mask)[:, 0:ny] * spread_to(u[...], ny)).astype(bf16)
@@ -310,14 +323,14 @@
             return u[:, 0:n] if n <= LANES else spread(u, n)
 
         tot, keep, send = call(
-            second,
+            second_cols,
             (
                 tot_t,
                 jax.ShapeDtypeStruct((len(ends), EXT, width), f32),
                 jax.ShapeDtypeStruct((n_tot + len(ends) * EXT, width), bf16),
             ),
-            [tot, *got, ab, xe, *y, *matrix],
-            [lanes_s] * 2 + spare,
+            [u, xe, *matrix],
+            spare,
         )
 
         def join(t, kp, g, tot_o, keep_o, *sends):

time: 43.1 us -> 42.6 us (0.988)
  Pallas kernels: 10.2 us -> 9.7 us
    pallas_call x12 -> x13, Pallas kernels: 10.2 us -> 9.7 us  [call(): pl.pallas_call(kernel, out_shape=outs, in_specs=[spec] * len(args), out_s...]
where the time goes in v4:
time: 42.6 us; the launch traced here: 42.4 us
  starting transfers between devices  17.1 us (40%)
  waiting for transfers between devices  14.8 us (35%)
  Pallas kernels  9.7 us (23%)
  between operations  0.77 us (2%)
    ppermute x15, starting transfers between devices, swap(): return lax.ppermute(t, 'row', xor_perm(rows, m))  11.6 us
    ppermute x15, waiting for transfers between devices, swap(): return lax.ppermute(t, 'row', xor_perm(rows, m))  10.9 us
    pallas_call x13, Pallas kernels, call(): pl.pallas_call(kernel, out_shape=outs, in_specs=[spec] * len(args), out_s...  9.7 us
    ppermute x3, starting transfers between devices, per_device(): lax.ppermute(own, ('row', 'col'), xor_perm(rows * cols, cols + m))  5.48 us
    ppermute x3, waiting for transfers between devices, per_device(): lax.ppermute(own, ('row', 'col'), xor_perm(rows * cols, cols + m))  3.83 us
  transfers between devices with their start and end apart: 18, of which 14 were waited for; matrix products, arithmetic and copies ran while one was open for 0% of the time, Pallas kernels for 6%

profile of v4, /device:TPU:0, one launch (start us, length us, event | category | flops | bytes accessed | tf_op | source)
XLA Modules:
  0.0 42.4 jit_solution(15543328643743699361)
XLA Ops:
  0.6 0.8 %shard_map.59 = bf16[56,384]{1,0:T(8,128)(2,1)S(1)} custom-call(bf16[50,128]{1,0:T(8,128)(2,1)} %x_hbm.1, bf16[50,256]{1,0:T(8,128)(2,1)} %y_hbm.1, bf16[128]{0:T(256)(128)(2,1)} %a_hbm.1, bf16[256]{0:T(256)(128)(2,1)} %b_hbm.1), custom_call_target="tpu_custom_call" | custom-call | tf_op jit(solution)/shard_map/pallas_call | solution.py:141
  1.5 4.6 %collective-permute-start.2 = (bf16[56,384]{1,0:T(8,128)(2,1)S(1)}, bf16[56,384]{1,0:T(8,128)(2,1)S(1)}, u32[]{:S(2)}, u32[]{:S(2)}) collective-permute-start(bf16[56,384]{1,0:T(8,128)(2,1)S(1)} %shard_map.59), channel_id=1, source_target_pairs={{0,7},{1,6},{2,5},{3,4},{4,3},{5,2},{6,1},{7,0},{8,15},{9,14},{10,... | collective-permute-start | bytes 129032 | tf_op jit(solution)/shard_map/ppermute | solution.py:189
  6.0 0.9 %collective-permute-start = (bf16[56,384]{1,0:T(8,128)(2,1)S(1)}, bf16[56,384]{1,0:T(8,128)(2,1)S(1)}, u32[]{:S(2)}, u32[]{:S(2)}) collective-permute-start(bf16[56,384]{1,0:T(8,128)(2,1)S(1)} %shard_map.59), channel_id=1, source_target_pairs={{0,5},{1,4},{2,7},{3,6},{4,1},{5,0},{6,3},{7,2},{8,13},{9,12},{10,... | collective-permute-start | bytes 129032 | tf_op jit(solution)/shard_map/ppermute | solution.py:189
  7.0 1.1 %collective-permute-done.2 = bf16[56,384]{1,0:T(8,128)(2,1)S(1)} collective-permute-done((bf16[56,384]{1,0:T(8,128)(2,1)S(1)}, bf16[56,384]{1,0:T(8,128)(2,1)S(1)}, u32[]{:S(2)}, u32[]{:S(2)}) %collective-permute-start.2) | collective-permute-done | bytes 43040 | tf_op jit(solution)/shard_map/ppermute | solution.py:189
  8.0 2.8 %collective-permute-done.1 = bf16[56,384]{1,0:T(8,128)(2,1)S(1)} collective-permute-done((bf16[56,384]{1,0:T(8,128)(2,1)S(1)}, bf16[56,384]{1,0:T(8,128)(2,1)S(1)}, u32[]{:S(2)}, u32[]{:S(2)}) %collective-permute-start.1) | collective-permute-done | bytes 43040 | tf_op jit(solution)/shard_map/ppermute | solution.py:189
  11.2 1.5 %collective-permute-start.5 = (bf16[56,1024]{1,0:T(8,128)(2,1)S(1)}, bf16[56,1024]{1,0:T(8,128)(2,1)S(1)}, u32[]{:S(2)}, u32[]{:S(2)}) collective-permute-start(bf16[56,1024]{1,0:T(8,128)(2,1)S(1)} %pad_maximum_fusion.y_ref.refs_5_.refs_6_), channel_id=1, source_target_pairs={{0,16},{4,20},{8,24},{12,28},{16,0},{20,4},{24,8},{28,12},{1,17},{... | collective-permute-start | bytes 344072 | tf_op jit(solution)/shard_map/ppermute | solution.py:152
  12.7 1.5 %collective-permute-start.4 = (bf16[56,1024]{1,0:T(8,128)(2,1)S(1)}, bf16[56,1024]{1,0:T(8,128)(2,1)S(1)}, u32[]{:S(2)}, u32[]{:S(2)}) collective-permute-start(bf16[56,1024]{1,0:T(8,128)(2,1)S(1)} %pad_maximum_fusion.y_ref.refs_5_.refs_6_), channel_id=1, source_target_pairs={{0,8},{4,12},{8,0},{12,4},{16,24},{20,28},{24,16},{28,20},{1,9},{5... | collective-permute-start | bytes 344072 | tf_op jit(solution)/shard_map/ppermute | solution.py:152
  14.2 0.5 %collective-permute-start.3 = (bf16[56,1024]{1,0:T(8,128)(2,1)S(1)}, bf16[56,1024]{1,0:T(8,128)(2,1)S(1)}, u32[]{:S(2)}, u32[]{:S(2)}) collective-permute-start(bf16[56,1024]{1,0:T(8,128)(2,1)S(1)} %pad_maximum_fusion.y_ref.refs_5_.refs_6_), channel_id=1, source_target_pairs={{0,24},{4,28},{8,16},{12,20},{16,8},{20,12},{24,0},{28,4},{1,25},{... | collective-permute-start | bytes 344072 | tf_op jit(solution)/shard_map/ppermute | solution.py:152
  14.7 0.5 %shard_map.60 = (bf16[512,56]{1,0:T(8,128)(2,1)S(1)}, f32[512,128]{1,0:T(8,128)S(1)}, f32[512,128]{1,0:T(8,128)S(1)}, f32[512,1024]{1,0:T(8,128)S(1)}) custom-call(bf16[56,512]{1,0:T(8,128)(2,1)S(1)} %pad_maximum_fusion.1.e.refs_1_, bf16[56,1024]{1,0:T(8,128)(2,1)S(1)} %pad_maximum_fusion.y_ref.refs_5_.refs_6_), custom_call_target="tpu_custom_call" | custom-call | flops 1 | bytes 1 | tf_op jit(solution)/shard_map/pallas_call | solution.py:141
  15.3 0.4 shard_map.61
  15.7 0.8 %collective-permute-done.5.refs_3_.refs_9_.refs_10_ = bf16[56,1024]{1,0:T(8,128)(2,1)S(1)} collective-permute-done((bf16[56,1024]{1,0:T(8,128)(2,1)S(1)}, bf16[56,1024]{1,0:T(8,128)(2,1)S(1)}, u32[]{:S(2)}, u32[]{:S(2)}) %collective-permute-start.5) | collective-permute-done | bytes 114720 | tf_op jit(solution)/shard_map/ppermute | solution.py:152
  16.4 2.3 %collective-permute-done.4.refs_2_.refs_7_.refs_8_ = bf16[56,1024]{1,0:T(8,128)(2,1)S(1)} collective-permute-done((bf16[56,1024]{1,0:T(8,128)(2,1)S(1)}, bf16[56,1024]{1,0:T(8,128)(2,1)S(1)}, u32[]{:S(2)}, u32[]{:S(2)}) %collective-permute-start.4) | collective-permute-done | bytes 114720 | tf_op jit(solution)/shard_map/ppermute | solution.py:152
  18.7 0.5 %collective-permute-start.8 = (bf16[56,1024]{1,0:T(8,128)(2,1)S(1)}, bf16[56,1024]{1,0:T(8,128)(2,1)S(1)}, u32[]{:S(2)}, u32[]{:S(2)}) collective-permute-start(bf16[56,1024]{1,0:T(8,128)(2,1)S(1)} %collective-permute-done.5.refs_3_.refs_9_.refs_10_), channel_id=1, source_target_pairs={{0,4},{4,0},{8,12},{12,8},{16,20},{20,16},{24,28},{28,24},{1,5},{5... | collective-permute-start | bytes 344072 | tf_op jit(solution)/shard_map/ppermute | solution.py:152
  19.2 0.7 %shard_map.62 = (f32[512,128]{1,0:T(8,128)S(1)}, f32[512,1024]{1,0:T(8,128)S(1)}, f32[512,1024]{1,0:T(8,128)S(1)}) custom-call(bf16[512,56]{1,0:T(8,128)(2,1)S(1)} %get-tuple-element.33.refs_0_.refs_5_, f32[512,128]{1,0:T(8,128)S(1)} %get-tuple-element.36.refs_1_, bf16[56,1024]{1,0:T(8,128)(2,1)S(1)} %collective-permute-done.4.refs_2_.refs_7_.refs_8_, ...), custom_call_target="tpu_custom_call" | custom-call | flops 1 | bytes 1 | tf_op jit(solution)/shard_map/pallas_call | solution.py:141
  20.1 0.4 shard_map.63
  20.5 0.7 %shard_map.64 = (f32[512,128]{1,0:T(8,128)S(1)}, f32[512,1024]{1,0:T(8,128)S(1)}, f32[512,1024]{1,0:T(8,128)S(1)}) custom-call(bf16[512,56]{1,0:T(8,128)(2,1)S(1)} %get-tuple-element.33.refs_0_.refs_5_, f32[512,128]{1,0:T(8,128)S(1)} %get-tuple-element.42.refs_1_, bf16[56,1024]{1,0:T(8,128)(2,1)S(1)} %collective-permute-done.7.refs_2_.refs_8_.refs_9_, ...), custom_call_target="tpu_custom_call" | custom-call | flops 1 | bytes 1 | tf_op jit(solution)/shard_map/pallas_call | solution.py:141
  21.4 0.4 shard_map.65
  21.8 1.2 %shard_map.66.t = f32[8,1024]{1,0:T(8,128)S(1)} custom-call(f32[512,128]{1,0:T(8,128)S(1)} %get-tuple-element.44.refs_0_, f32[512,128]{1,0:T(8,128)S(1)} %get-tuple-element.45.refs_1_.refs_4_, f32[512,1024]{1,0:T(8,128)S(1)} %get-tuple-element.46.refs_2_.refs_13_.refs_14_, f32[512,1024]{1,0:T(8,128)S(1)} %get-tuple-element.47.refs_3_.refs_14_.refs_15_, ...), custom_call_target="tpu_custom_call" | custom-call | tf_op jit(solution)/shard_map/pallas_call | solution.py:141
  23.5 0.9 %collective-permute-done.10.g = f32[8,1024]{1,0:T(8,128)S(1)} collective-permute-done((f32[8,1024]{1,0:T(8,128)S(1)}, f32[8,1024]{1,0:T(8,128)S(1)}, u32[]{:S(2)}, u32[]{:S(2)}) %collective-permute-start.10) | collective-permute-done | bytes 32800 | tf_op jit(solution)/shard_map/ppermute | solution.py:152
  24.4 2.5 %collective-permute-start.13 = (bf16[8,1024]{1,0:T(8,128)(2,1)S(1)}, bf16[8,1024]{1,0:T(8,128)(2,1)S(1)}, u32[]{:S(2)}, u32[]{:S(2)}) collective-permute-start(bf16[8,1024]{1,0:T(8,128)(2,1)S(1)} %get-tuple-element.55), channel_id=1, source_target_pairs={{0,28},{4,24},{8,20},{12,16},{16,12},{20,8},{24,4},{28,0},{1,29},{... | collective-permute-start | bytes 49160 | tf_op jit(solution)/shard_map/ppermute | solution.py:152
  27.1 0.5 %collective-permute-start.11 = (bf16[8,1024]{1,0:T(8,128)(2,1)S(1)}, bf16[8,1024]{1,0:T(8,128)(2,1)S(1)}, u32[]{:S(2)}, u32[]{:S(2)}) collective-permute-start(bf16[8,1024]{1,0:T(8,128)(2,1)S(1)} %get-tuple-element.55), channel_id=1, source_target_pairs={{0,12},{4,8},{8,4},{12,0},{16,28},{20,24},{24,20},{28,16},{1,13},{... | collective-permute-start | bytes 49160 | tf_op jit(solution)/shard_map/ppermute | solution.py:152
  27.6 0.9 %collective-permute-done.13.refs_3_ = bf16[8,1024]{1,0:T(8,128)(2,1)S(1)} collective-permute-done((bf16[8,1024]{1,0:T(8,128)(2,1)S(1)}, bf16[8,1024]{1,0:T(8,128)(2,1)S(1)}, u32[]{:S(2)}, u32[]{:S(2)}) %collective-permute-start.13) | collective-permute-done | bytes 16416 | tf_op jit(solution)/shard_map/ppermute | solution.py:152
  28.5 1.5 %collective-permute-done.12.refs_2_ = bf16[8,1024]{1,0:T(8,128)(2,1)S(1)} collective-permute-done((bf16[8,1024]{1,0:T(8,128)(2,1)S(1)}, bf16[8,1024]{1,0:T(8,128)(2,1)S(1)}, u32[]{:S(2)}, u32[]{:S(2)}) %collective-permute-start.12) | collective-permute-done | bytes 16416 | tf_op jit(solution)/shard_map/ppermute | solution.py:152
  30.3 1.3 %shard_map.68.refs_0_ = f32[512,128]{1,0:T(8,128)S(1)} custom-call(f32[8,1024]{1,0:T(8,128)S(1)} %get-tuple-element.54.refs_0_, bf16[8,1024]{1,0:T(8,128)(2,1)S(1)} %collective-permute-done.11.refs_1_, bf16[8,1024]{1,0:T(8,128)(2,1)S(1)} %collective-permute-done.12.refs_2_, bf16[8,1024]{1,0:T(8,128)(2,1)S(1)} %collective-permute-done.13.refs_3_, ...), custom_call_target="tpu_custom_call" | custom-call | tf_op jit(solution)/shard_map/pallas_call | solution.py:141
  31.6 1.7 %shard_map.69 = (f32[8,1024]{1,0:T(8,128)S(1)}, f32[4,56,256]{2,1,0:T(8,128)S(1)}, bf16[256,256]{1,0:T(8,128)(2,1)S(1)}) custom-call(f32[512,128]{1,0:T(8,128)S(1)} %shard_map.68.refs_0_, bf16[56,512]{1,0:T(8,128)(2,1)S(1)} %pad_maximum_fusion.1.e.refs_1_, f32[512,1024]{1,0:T(8,128)S(1)} %get-tuple-element.46.refs_2_.refs_13_.refs_14_, ...), custom_call_target="tpu_custom_call" | custom-call | tf_op jit(solution)/shard_map/pallas_call | solution.py:141
  33.7 1.0 %collective-permute-done.14.g = bf16[256,256]{1,0:T(8,128)(2,1)S(1)} collective-permute-done((bf16[256,256]{1,0:T(8,128)(2,1)S(1)}, bf16[256,256]{1,0:T(8,128)(2,1)S(1)}, u32[]{:S(2)}, u32[]{:S(2)}) %collective-permute-start.14) | collective-permute-done | bytes 131104 | tf_op jit(solution)/shard_map/ppermute | solution.py:152
  34.8 0.5 %collective-permute-start.15 = (bf16[88,256]{1,0:T(8,128)(2,1)S(1)}, bf16[88,256]{1,0:T(8,128)(2,1)S(1)}, u32[]{:S(2)}, u32[]{:S(2)}) collective-permute-start(bf16[88,256]{1,0:T(8,128)(2,1)S(1)} %get-tuple-element.61), channel_id=1, source_target_pairs={{0,12},{4,8},{8,4},{12,0},{16,28},{20,24},{24,20},{28,16},{1,13},{... | collective-permute-start | bytes 135176 | tf_op jit(solution)/shard_map/ppermute | solution.py:152
  35.3 1.3 %collective-permute-start.16 = (bf16[88,256]{1,0:T(8,128)(2,1)S(1)}, bf16[88,256]{1,0:T(8,128)(2,1)S(1)}, u32[]{:S(2)}, u32[]{:S(2)}) collective-permute-start(bf16[88,256]{1,0:T(8,128)(2,1)S(1)} %get-tuple-element.62), channel_id=1, source_target_pairs={{0,20},{4,16},{8,28},{12,24},{16,4},{20,0},{24,12},{28,8},{1,21},{... | collective-permute-start | bytes 135176 | tf_op jit(solution)/shard_map/ppermute | solution.py:152
  36.6 1.4 %collective-permute-start.17 = (bf16[88,256]{1,0:T(8,128)(2,1)S(1)}, bf16[88,256]{1,0:T(8,128)(2,1)S(1)}, u32[]{:S(2)}, u32[]{:S(2)}) collective-permute-start(bf16[88,256]{1,0:T(8,128)(2,1)S(1)} %get-tuple-element.63), channel_id=1, source_target_pairs={{0,28},{4,24},{8,20},{12,16},{16,12},{20,8},{24,4},{28,0},{1,29},{... | collective-permute-start | bytes 135176 | tf_op jit(solution)/shard_map/ppermute | solution.py:152
  38.3 0.7 %collective-permute-done.16.refs_3_ = bf16[88,256]{1,0:T(8,128)(2,1)S(1)} collective-permute-done((bf16[88,256]{1,0:T(8,128)(2,1)S(1)}, bf16[88,256]{1,0:T(8,128)(2,1)S(1)}, u32[]{:S(2)}, u32[]{:S(2)}) %collective-permute-start.16) | collective-permute-done | bytes 45088 | tf_op jit(solution)/shard_map/ppermute | solution.py:152
  39.0 2.0 %collective-permute-done.17.refs_4_ = bf16[88,256]{1,0:T(8,128)(2,1)S(1)} collective-permute-done((bf16[88,256]{1,0:T(8,128)(2,1)S(1)}, bf16[88,256]{1,0:T(8,128)(2,1)S(1)}, u32[]{:S(2)}, u32[]{:S(2)}) %collective-permute-start.17) | collective-permute-done | bytes 45088 | tf_op jit(solution)/shard_map/ppermute | solution.py:152
  41.0 1.4 %shard_map.71 = (f32[50,128]{1,0:T(8,128)}, f32[50,256]{1,0:T(8,128)}) custom-call(f32[8,1024]{1,0:T(8,128)S(1)} %get-tuple-element.59.refs_0_, f32[56,256]{1,0:T(8,128)S(1)} %get-tuple-element.60.refs_1_, bf16[88,256]{1,0:T(8,128)(2,1)S(1)} %collective-permute-done.15.refs_2_, bf16[88,256]{1,0:T(8,128)(2,1)S(1)} %collective-permute-done.16.refs_3_, ...), custom_call_target="tpu_custom_call" | custom-call | tf_op jit(solution)/shard_map/pallas_call | solution.py:141
  (27 shorter events, 2.5 us)
Async XLA Ops:
  1.5 6.6 %collective-permute-start.2 = (bf16[56,384]{1,0:T(8,128)(2,1)S(1)}, bf16[56,384]{1,0:T(8,128)(2,1)S(1)}, u32[]{:S(2)}, u32[]{:S(2)}) collective-permute-start(bf16[56,384]{1,0:T(8,128)(2,1)S(1)} %shard_map.59), channel_id=1, source_target_pairs={{0,7},{1,6},{2,5},{3,4},{4,3},{5,2},{6,1},{7,0},{8,15},{9,14},{10,... | collective-permute-start | bytes 129032 | tf_op jit(solution)/shard_map/ppermute | solution.py:189
  6.0 4.8 %collective-permute-start.1 = (bf16[56,384]{1,0:T(8,128)(2,1)S(1)}, bf16[56,384]{1,0:T(8,128)(2,1)S(1)}, u32[]{:S(2)}, u32[]{:S(2)}) collective-permute-start(bf16[56,384]{1,0:T(8,128)(2,1)S(1)} %shard_map.59), channel_id=1, source_target_pairs={{0,6},{1,7},{2,4},{3,5},{4,2},{5,3},{6,0},{7,1},{8,14},{9,15},{10,... | collective-permute-start | bytes 129032 | tf_op jit(solution)/shard_map/ppermute | solution.py:189
  6.0 4.8 %collective-permute-start = (bf16[56,384]{1,0:T(8,128)(2,1)S(1)}, bf16[56,384]{1,0:T(8,128)(2,1)S(1)}, u32[]{:S(2)}, u32[]{:S(2)}) collective-permute-start(bf16[56,384]{1,0:T(8,128)(2,1)S(1)} %shard_map.59), channel_id=1, source_target_pairs={{0,5},{1,4},{2,7},{3,6},{4,1},{5,0},{6,3},{7,2},{8,13},{9,12},{10,... | collective-permute-start | bytes 129032 | tf_op jit(solution)/shard_map/ppermute | solution.py:189
  10.8 4.4 %collective-permute-start.6 = (bf16[56,1024]{1,0:T(8,128)(2,1)S(1)}, bf16[56,1024]{1,0:T(8,128)(2,1)S(1)}, u32[]{:S(2)}, u32[]{:S(2)}) collective-permute-start(bf16[56,1024]{1,0:T(8,128)(2,1)S(1)} %pad_maximum_fusion.y_ref.refs_5_.refs_6_), channel_id=1, source_target_pairs={{0,4},{4,0},{8,12},{12,8},{16,20},{20,16},{24,28},{28,24},{1,5},{5... | collective-permute-start | bytes 344072 | tf_op jit(solution)/shard_map/ppermute | solution.py:152
  11.2 5.3 %collective-permute-start.5 = (bf16[56,1024]{1,0:T(8,128)(2,1)S(1)}, bf16[56,1024]{1,0:T(8,128)(2,1)S(1)}, u32[]{:S(2)}, u32[]{:S(2)}) collective-permute-start(bf16[56,1024]{1,0:T(8,128)(2,1)S(1)} %pad_maximum_fusion.y_ref.refs_5_.refs_6_), channel_id=1, source_target_pairs={{0,16},{4,20},{8,24},{12,28},{16,0},{20,4},{24,8},{28,12},{1,17},{... | collective-permute-start | bytes 344072 | tf_op jit(solution)/shard_map/ppermute | solution.py:152
  12.7 6.0 %collective-permute-start.4 = (bf16[56,1024]{1,0:T(8,128)(2,1)S(1)}, bf16[56,1024]{1,0:T(8,128)(2,1)S(1)}, u32[]{:S(2)}, u32[]{:S(2)}) collective-permute-start(bf16[56,1024]{1,0:T(8,128)(2,1)S(1)} %pad_maximum_fusion.y_ref.refs_5_.refs_6_), channel_id=1, source_target_pairs={{0,8},{4,12},{8,0},{12,4},{16,24},{20,28},{24,16},{28,20},{1,9},{5... | collective-permute-start | bytes 344072 | tf_op jit(solution)/shard_map/ppermute | solution.py:152
  14.2 5.9 %collective-permute-start.3 = (bf16[56,1024]{1,0:T(8,128)(2,1)S(1)}, bf16[56,1024]{1,0:T(8,128)(2,1)S(1)}, u32[]{:S(2)}, u32[]{:S(2)}) collective-permute-start(bf16[56,1024]{1,0:T(8,128)(2,1)S(1)} %pad_maximum_fusion.y_ref.refs_5_.refs_6_), channel_id=1, source_target_pairs={{0,24},{4,28},{8,16},{12,20},{16,8},{20,12},{24,0},{28,4},{1,25},{... | collective-permute-start | bytes 344072 | tf_op jit(solution)/shard_map/ppermute | solution.py:152
  18.7 1.8 %collective-permute-start.7 = (bf16[56,1024]{1,0:T(8,128)(2,1)S(1)}, bf16[56,1024]{1,0:T(8,128)(2,1)S(1)}, u32[]{:S(2)}, u32[]{:S(2)}) collective-permute-start(bf16[56,1024]{1,0:T(8,128)(2,1)S(1)} %collective-permute-done.4.refs_2_.refs_7_.refs_8_), channel_id=1, source_target_pairs={{0,4},{4,0},{8,12},{12,8},{16,20},{20,16},{24,28},{28,24},{1,5},{5... | collective-permute-start | bytes 344072 | tf_op jit(solution)/shard_map/ppermute | solution.py:152
  18.7 1.8 %collective-permute-start.8 = (bf16[56,1024]{1,0:T(8,128)(2,1)S(1)}, bf16[56,1024]{1,0:T(8,128)(2,1)S(1)}, u32[]{:S(2)}, u32[]{:S(2)}) collective-permute-start(bf16[56,1024]{1,0:T(8,128)(2,1)S(1)} %collective-permute-done.5.refs_3_.refs_9_.refs_10_), channel_id=1, source_target_pairs={{0,4},{4,0},{8,12},{12,8},{16,20},{20,16},{24,28},{28,24},{1,5},{5... | collective-permute-start | bytes 344072 | tf_op jit(solution)/shard_map/ppermute | solution.py:152
  20.1 1.3 %collective-permute-start.9 = (bf16[56,1024]{1,0:T(8,128)(2,1)S(1)}, bf16[56,1024]{1,0:T(8,128)(2,1)S(1)}, u32[]{:S(2)}, u32[]{:S(2)}) collective-permute-start(bf16[56,1024]{1,0:T(8,128)(2,1)S(1)} %collective-permute-done.3.refs_2_.refs_11_.refs_12_), channel_id=1, source_target_pairs={{0,4},{4,0},{8,12},{12,8},{16,20},{20,16},{24,28},{28,24},{1,5},{5... | collective-permute-start | bytes 344072 | tf_op jit(solution)/shard_map/ppermute | solution.py:152
  23.1 1.3 %collective-permute-start.10 = (f32[8,1024]{1,0:T(8,128)S(1)}, f32[8,1024]{1,0:T(8,128)S(1)}, u32[]{:S(2)}, u32[]{:S(2)}) collective-permute-start(f32[8,1024]{1,0:T(8,128)S(1)} %shard_map.66.t), channel_id=1, source_target_pairs={{0,4},{4,0},{8,12},{12,8},{16,20},{20,16},{24,28},{28,24},{1,5},{5... | collective-permute-start | bytes 98312 | tf_op jit(solution)/shard_map/ppermute | solution.py:152
  24.4 4.1 %collective-permute-start.13 = (bf16[8,1024]{1,0:T(8,128)(2,1)S(1)}, bf16[8,1024]{1,0:T(8,128)(2,1)S(1)}, u32[]{:S(2)}, u32[]{:S(2)}) collective-permute-start(bf16[8,1024]{1,0:T(8,128)(2,1)S(1)} %get-tuple-element.55), channel_id=1, source_target_pairs={{0,28},{4,24},{8,20},{12,16},{16,12},{20,8},{24,4},{28,0},{1,29},{... | collective-permute-start | bytes 49160 | tf_op jit(solution)/shard_map/ppermute | solution.py:152
  26.8 3.2 %collective-permute-start.12 = (bf16[8,1024]{1,0:T(8,128)(2,1)S(1)}, bf16[8,1024]{1,0:T(8,128)(2,1)S(1)}, u32[]{:S(2)}, u32[]{:S(2)}) collective-permute-start(bf16[8,1024]{1,0:T(8,128)(2,1)S(1)} %get-tuple-element.55), channel_id=1, source_target_pairs={{0,20},{4,16},{8,28},{12,24},{16,4},{20,0},{24,12},{28,8},{1,21},{... | collective-permute-start | bytes 49160 | tf_op jit(solution)/shard_map/ppermute | solution.py:152
  27.1 3.2 %collective-permute-start.11 = (bf16[8,1024]{1,0:T(8,128)(2,1)S(1)}, bf16[8,1024]{1,0:T(8,128)(2,1)S(1)}, u32[]{:S(2)}, u32[]{:S(2)}) collective-permute-start(bf16[8,1024]{1,0:T(8,128)(2,1)S(1)} %get-tuple-element.55), channel_id=1, source_target_pairs={{0,12},{4,8},{8,4},{12,0},{16,28},{20,24},{24,20},{28,16},{1,13},{... | collective-permute-start | bytes 49160 | tf_op jit(solution)/shard_map/ppermute | solution.py:152
  33.3 1.4 %collective-permute-start.14 = (bf16[256,256]{1,0:T(8,128)(2,1)S(1)}, bf16[256,256]{1,0:T(8,128)(2,1)S(1)}, u32[]{:S(2)}, u32[]{:S(2)}) collective-permute-start(bf16[256,256]{1,0:T(8,128)(2,1)S(1)} %get-tuple-element.58), channel_id=1, source_target_pairs={{0,4},{4,0},{8,12},{12,8},{16,20},{20,16},{24,28},{28,24},{1,5},{5... | collective-permute-start | bytes 393224 | tf_op jit(solution)/shard_map/ppermute | solution.py:152
  34.8 3.5 %collective-permute-start.15 = (bf16[88,256]{1,0:T(8,128)(2,1)S(1)}, bf16[88,256]{1,0:T(8,128)(2,1)S(1)}, u32[]{:S(2)}, u32[]{:S(2)}) collective-permute-start(bf16[88,256]{1,0:T(8,128)(2,1)S(1)} %get-tuple-element.61), channel_id=1, source_target_pairs={{0,12},{4,8},{8,4},{12,0},{16,28},{20,24},{24,20},{28,16},{1,13},{... | collective-permute-start | bytes 135176 | tf_op jit(solution)/shard_map/ppermute | solution.py:152
  35.3 3.7 %collective-permute-start.16 = (bf16[88,256]{1,0:T(8,128)(2,1)S(1)}, bf16[88,256]{1,0:T(8,128)(2,1)S(1)}, u32[]{:S(2)}, u32[]{:S(2)}) collective-permute-start(bf16[88,256]{1,0:T(8,128)(2,1)S(1)} %get-tuple-element.62), channel_id=1, source_target_pairs={{0,20},{4,16},{8,28},{12,24},{16,4},{20,0},{24,12},{28,8},{1,21},{... | collective-permute-start | bytes 135176 | tf_op jit(solution)/shard_map/ppermute | solution.py:152
  36.6 4.4 %collective-permute-start.17 = (bf16[88,256]{1,0:T(8,128)(2,1)S(1)}, bf16[88,256]{1,0:T(8,128)(2,1)S(1)}, u32[]{:S(2)}, u32[]{:S(2)}) collective-permute-start(bf16[88,256]{1,0:T(8,128)(2,1)S(1)} %get-tuple-element.63), channel_id=1, source_target_pairs={{0,28},{4,24},{8,20},{12,16},{16,12},{20,8},{24,4},{28,0},{1,29},{... | collective-permute-start | bytes 135176 | tf_op jit(solution)/shard_map/ppermute | solution.py:152

commit v5 on v4

--- a/solution.py
+++ b/solution.py
@@ -217,7 +217,7 @@
                     ks[i] = t
             return acc
 
-        raw = {m: swap(y[0], m) for m in range(2, rows, 2)}
+        raw = {m: swap(y[0], m) for m in (*range(2, rows - 2, 2), rows - 1)}
         y[1] = swap(y[0], 1)
         xt, ab, acc, *k = call(
             start_kernel,
@@ -228,16 +228,14 @@
         if kept:
             ks[0] = k[0]
         acc = more([1], acc)
-        evens, odds = list(range(2, rows, 2)), list(range(3, rows, 2))
-        early, late = evens[:-1], evens[-1:]
-        for some in (early, late):
+        early, late = list(raw)[:-1], list(raw)[-1:]
+        for some, others in ((early, []), (late, [m ^ 1 for m in early])):
             *lines, acc = lax.optimization_barrier((*[raw[m] for m in some], acc))
             for m, t in zip(some, lines):
                 y[m] = t
-                y[m + 1] = swap(t, 1)
-            acc = more(some, acc)
-        acc = more(odds[:-1], acc)
-        acc = more(odds[-1:], acc)
+                y[m ^ 1] = swap(t, 1)
+            acc = more(some + others, acc)
+        acc = more([m ^ 1 for m in late], acc)
         matrix = ks if kept else [xt, *y]
 
         def column_sums(k, u, tot, unroll):

time: 42.6 us -> 42.1 us (0.988)
  starting transfers between devices: 17.1 us -> 16 us
  waiting for transfers between devices: 14.8 us -> 15.5 us
    ppermute x15, starting transfers between devices: 11.6 us -> 10.5 us  [swap(): return lax.ppermute(t, 'row', xor_perm(rows, m))]
    ppermute x15, waiting for transfers between devices: 10.9 us -> 11.6 us  [swap(): return lax.ppermute(t, 'row', xor_perm(rows, m))]
    pallas_call x13 -> x12, Pallas kernels: 9.7 us -> 9.54 us  [call(): pl.pallas_call(kernel, out_shape=outs, in_specs=[spec] * len(args), out_s...]
where the time goes in v5:
time: 42.1 us; the launch traced here: 41.8 us
  starting transfers between devices  16 us (38%)
  waiting for transfers between devices  15.5 us (37%)
  Pallas kernels  9.54 us (23%)
  between operations  0.77 us (2%)
    ppermute x15, waiting for transfers between devices, swap(): return lax.ppermute(t, 'row', xor_perm(rows, m))  11.6 us
    ppermute x15, starting transfers between devices, swap(): return lax.ppermute(t, 'row', xor_perm(rows, m))  10.5 us
    pallas_call x12, Pallas kernels, call(): pl.pallas_call(kernel, out_shape=outs, in_specs=[spec] * len(args), out_s...  9.54 us
    ppermute x3, starting transfers between devices, per_device(): lax.ppermute(own, ('row', 'col'), xor_perm(rows * cols, cols + m))  5.48 us
    ppermute x3, waiting for transfers between devices, per_device(): lax.ppermute(own, ('row', 'col'), xor_perm(rows * cols, cols + m))  3.83 us
  transfers between devices with their start and end apart: 18, of which 14 were waited for; matrix products, arithmetic and copies ran while one was open for 0% of the time, Pallas kernels for 6%

profile of v5, /device:TPU:0, one launch (start us, length us, event | category | flops | bytes accessed | tf_op | source)
XLA Modules:
  0.0 41.8 jit_solution(10938974359827007908)
XLA Ops:
  0.6 0.8 %shard_map.59 = bf16[56,384]{1,0:T(8,128)(2,1)S(1)} custom-call(bf16[50,128]{1,0:T(8,128)(2,1)} %x_hbm.1, bf16[50,256]{1,0:T(8,128)(2,1)} %y_hbm.1, bf16[128]{0:T(256)(128)(2,1)} %a_hbm.1, bf16[256]{0:T(256)(128)(2,1)} %b_hbm.1), custom_call_target="tpu_custom_call" | custom-call | tf_op jit(solution)/shard_map/pallas_call | solution.py:141
  1.5 4.6 %collective-permute-start.2 = (bf16[56,384]{1,0:T(8,128)(2,1)S(1)}, bf16[56,384]{1,0:T(8,128)(2,1)S(1)}, u32[]{:S(2)}, u32[]{:S(2)}) collective-permute-start(bf16[56,384]{1,0:T(8,128)(2,1)S(1)} %shard_map.59), channel_id=1, source_target_pairs={{0,7},{1,6},{2,5},{3,4},{4,3},{5,2},{6,1},{7,0},{8,15},{9,14},{10,... | collective-permute-start | bytes 129032 | tf_op jit(solution)/shard_map/ppermute | solution.py:189
  6.0 0.9 %collective-permute-start = (bf16[56,384]{1,0:T(8,128)(2,1)S(1)}, bf16[56,384]{1,0:T(8,128)(2,1)S(1)}, u32[]{:S(2)}, u32[]{:S(2)}) collective-permute-start(bf16[56,384]{1,0:T(8,128)(2,1)S(1)} %shard_map.59), channel_id=1, source_target_pairs={{0,5},{1,4},{2,7},{3,6},{4,1},{5,0},{6,3},{7,2},{8,13},{9,12},{10,... | collective-permute-start | bytes 129032 | tf_op jit(solution)/shard_map/ppermute | solution.py:189
  7.0 1.1 %collective-permute-done.2 = bf16[56,384]{1,0:T(8,128)(2,1)S(1)} collective-permute-done((bf16[56,384]{1,0:T(8,128)(2,1)S(1)}, bf16[56,384]{1,0:T(8,128)(2,1)S(1)}, u32[]{:S(2)}, u32[]{:S(2)}) %collective-permute-start.2) | collective-permute-done | bytes 43040 | tf_op jit(solution)/shard_map/ppermute | solution.py:189
  8.0 2.8 %collective-permute-done.1 = bf16[56,384]{1,0:T(8,128)(2,1)S(1)} collective-permute-done((bf16[56,384]{1,0:T(8,128)(2,1)S(1)}, bf16[56,384]{1,0:T(8,128)(2,1)S(1)}, u32[]{:S(2)}, u32[]{:S(2)}) %collective-permute-start.1) | collective-permute-done | bytes 43040 | tf_op jit(solution)/shard_map/ppermute | solution.py:189
  11.2 1.5 %collective-permute-start.5 = (bf16[56,1024]{1,0:T(8,128)(2,1)S(1)}, bf16[56,1024]{1,0:T(8,128)(2,1)S(1)}, u32[]{:S(2)}, u32[]{:S(2)}) collective-permute-start(bf16[56,1024]{1,0:T(8,128)(2,1)S(1)} %pad_maximum_fusion.y_ref.refs_5_.refs_6_), channel_id=1, source_target_pairs={{0,16},{4,20},{8,24},{12,28},{16,0},{20,4},{24,8},{28,12},{1,17},{... | collective-permute-start | bytes 344072 | tf_op jit(solution)/shard_map/ppermute | solution.py:152
  12.7 1.5 %collective-permute-start.4 = (bf16[56,1024]{1,0:T(8,128)(2,1)S(1)}, bf16[56,1024]{1,0:T(8,128)(2,1)S(1)}, u32[]{:S(2)}, u32[]{:S(2)}) collective-permute-start(bf16[56,1024]{1,0:T(8,128)(2,1)S(1)} %pad_maximum_fusion.y_ref.refs_5_.refs_6_), channel_id=1, source_target_pairs={{0,8},{4,12},{8,0},{12,4},{16,24},{20,28},{24,16},{28,20},{1,9},{5... | collective-permute-start | bytes 344072 | tf_op jit(solution)/shard_map/ppermute | solution.py:152
  14.2 0.5 %shard_map.60 = (bf16[512,56]{1,0:T(8,128)(2,1)S(1)}, f32[512,128]{1,0:T(8,128)S(1)}, f32[512,128]{1,0:T(8,128)S(1)}, f32[512,1024]{1,0:T(8,128)S(1)}) custom-call(bf16[56,512]{1,0:T(8,128)(2,1)S(1)} %pad_maximum_fusion.1.e.refs_1_, bf16[56,1024]{1,0:T(8,128)(2,1)S(1)} %pad_maximum_fusion.y_ref.refs_5_.refs_6_), custom_call_target="tpu_custom_call" | custom-call | flops 1 | bytes 1 | tf_op jit(solution)/shard_map/pallas_call | solution.py:141
  15.2 1.2 %collective-permute-done.5.refs_3_.refs_9_.refs_10_ = bf16[56,1024]{1,0:T(8,128)(2,1)S(1)} collective-permute-done((bf16[56,1024]{1,0:T(8,128)(2,1)S(1)}, bf16[56,1024]{1,0:T(8,128)(2,1)S(1)}, u32[]{:S(2)}, u32[]{:S(2)}) %collective-permute-start.5) | collective-permute-done | bytes 114720 | tf_op jit(solution)/shard_map/ppermute | solution.py:152
  16.4 1.8 %collective-permute-done.4.refs_2_.refs_7_.refs_8_ = bf16[56,1024]{1,0:T(8,128)(2,1)S(1)} collective-permute-done((bf16[56,1024]{1,0:T(8,128)(2,1)S(1)}, bf16[56,1024]{1,0:T(8,128)(2,1)S(1)}, u32[]{:S(2)}, u32[]{:S(2)}) %collective-permute-start.4) | collective-permute-done | bytes 114720 | tf_op jit(solution)/shard_map/ppermute | solution.py:152
  18.3 0.5 %collective-permute-start.8 = (bf16[56,1024]{1,0:T(8,128)(2,1)S(1)}, bf16[56,1024]{1,0:T(8,128)(2,1)S(1)}, u32[]{:S(2)}, u32[]{:S(2)}) collective-permute-start(bf16[56,1024]{1,0:T(8,128)(2,1)S(1)} %collective-permute-done.5.refs_3_.refs_9_.refs_10_), channel_id=1, source_target_pairs={{0,4},{4,0},{8,12},{12,8},{16,20},{20,16},{24,28},{28,24},{1,5},{5... | collective-permute-start | bytes 344072 | tf_op jit(solution)/shard_map/ppermute | solution.py:152
  18.8 0.7 %shard_map.62 = (f32[512,128]{1,0:T(8,128)S(1)}, f32[512,1024]{1,0:T(8,128)S(1)}, f32[512,1024]{1,0:T(8,128)S(1)}) custom-call(bf16[512,56]{1,0:T(8,128)(2,1)S(1)} %get-tuple-element.32.refs_0_.refs_5_, f32[512,128]{1,0:T(8,128)S(1)} %get-tuple-element.35.refs_1_, bf16[56,1024]{1,0:T(8,128)(2,1)S(1)} %collective-permute-done.4.refs_2_.refs_7_.refs_8_, ...), custom_call_target="tpu_custom_call" | custom-call | flops 1 | bytes 1 | tf_op jit(solution)/shard_map/pallas_call | solution.py:141
  19.5 0.9 %collective-permute-done.3.refs_2_.refs_12_.refs_13_ = bf16[56,1024]{1,0:T(8,128)(2,1)S(1)} collective-permute-done((bf16[56,1024]{1,0:T(8,128)(2,1)S(1)}, bf16[56,1024]{1,0:T(8,128)(2,1)S(1)}, u32[]{:S(2)}, u32[]{:S(2)}) %collective-permute-start.3) | collective-permute-done | bytes 114720 | tf_op jit(solution)/shard_map/ppermute | solution.py:152
  20.4 1.0 %shard_map.63 = (f32[512,128]{1,0:T(8,128)S(1)}, f32[512,1024]{1,0:T(8,128)S(1)}, f32[512,1024]{1,0:T(8,128)S(1)}, f32[512,1024]{1,0:T(8,128)S(1)}) custom-call(bf16[512,56]{1,0:T(8,128)(2,1)S(1)} %get-tuple-element.32.refs_0_.refs_5_, f32[512,128]{1,0:T(8,128)S(1)} %get-tuple-element.39.refs_1_, ...), custom_call_target="tpu_custom_call" | custom-call | flops 1 | bytes 1 | tf_op jit(solution)/shard_map/pallas_call | solution.py:141
  22.1 1.2 %shard_map.65.t = f32[8,1024]{1,0:T(8,128)S(1)} custom-call(f32[512,128]{1,0:T(8,128)S(1)} %get-tuple-element.42.refs_0_, f32[512,128]{1,0:T(8,128)S(1)} %get-tuple-element.43.refs_1_.refs_4_, f32[512,1024]{1,0:T(8,128)S(1)} %get-tuple-element.44.refs_2_.refs_13_.refs_14_, f32[512,1024]{1,0:T(8,128)S(1)} %get-tuple-element.45.refs_3_.refs_14_.refs_15_, ...), custom_call_target="tpu_custom_call" | custom-call | tf_op jit(solution)/shard_map/pallas_call | solution.py:141
  23.6 1.0 %collective-permute-done.10.g = f32[8,1024]{1,0:T(8,128)S(1)} collective-permute-done((f32[8,1024]{1,0:T(8,128)S(1)}, f32[8,1024]{1,0:T(8,128)S(1)}, u32[]{:S(2)}, u32[]{:S(2)}) %collective-permute-start.10) | collective-permute-done | bytes 32800 | tf_op jit(solution)/shard_map/ppermute | solution.py:152
  24.7 1.7 %collective-permute-start.13 = (bf16[8,1024]{1,0:T(8,128)(2,1)S(1)}, bf16[8,1024]{1,0:T(8,128)(2,1)S(1)}, u32[]{:S(2)}, u32[]{:S(2)}) collective-permute-start(bf16[8,1024]{1,0:T(8,128)(2,1)S(1)} %get-tuple-element.53), channel_id=1, source_target_pairs={{0,28},{4,24},{8,20},{12,16},{16,12},{20,8},{24,4},{28,0},{1,29},{... | collective-permute-start | bytes 49160 | tf_op jit(solution)/shard_map/ppermute | solution.py:152
  26.3 0.7 %collective-permute-start.12 = (bf16[8,1024]{1,0:T(8,128)(2,1)S(1)}, bf16[8,1024]{1,0:T(8,128)(2,1)S(1)}, u32[]{:S(2)}, u32[]{:S(2)}) collective-permute-start(bf16[8,1024]{1,0:T(8,128)(2,1)S(1)} %get-tuple-element.53), channel_id=1, source_target_pairs={{0,20},{4,16},{8,28},{12,24},{16,4},{20,0},{24,12},{28,8},{1,21},{... | collective-permute-start | bytes 49160 | tf_op jit(solution)/shard_map/ppermute | solution.py:152
  27.0 0.7 %collective-permute-start.11 = (bf16[8,1024]{1,0:T(8,128)(2,1)S(1)}, bf16[8,1024]{1,0:T(8,128)(2,1)S(1)}, u32[]{:S(2)}, u32[]{:S(2)}) collective-permute-start(bf16[8,1024]{1,0:T(8,128)(2,1)S(1)} %get-tuple-element.53), channel_id=1, source_target_pairs={{0,12},{4,8},{8,4},{12,0},{16,28},{20,24},{24,20},{28,16},{1,13},{... | collective-permute-start | bytes 49160 | tf_op jit(solution)/shard_map/ppermute | solution.py:152
  27.7 1.1 %collective-permute-done.13.refs_3_ = bf16[8,1024]{1,0:T(8,128)(2,1)S(1)} collective-permute-done((bf16[8,1024]{1,0:T(8,128)(2,1)S(1)}, bf16[8,1024]{1,0:T(8,128)(2,1)S(1)}, u32[]{:S(2)}, u32[]{:S(2)}) %collective-permute-start.13) | collective-permute-done | bytes 16416 | tf_op jit(solution)/shard_map/ppermute | solution.py:152
  28.8 0.7 %collective-permute-done.12.refs_2_ = bf16[8,1024]{1,0:T(8,128)(2,1)S(1)} collective-permute-done((bf16[8,1024]{1,0:T(8,128)(2,1)S(1)}, bf16[8,1024]{1,0:T(8,128)(2,1)S(1)}, u32[]{:S(2)}, u32[]{:S(2)}) %collective-permute-start.12) | collective-permute-done | bytes 16416 | tf_op jit(solution)/shard_map/ppermute | solution.py:152
  29.5 0.7 %collective-permute-done.11.refs_1_ = bf16[8,1024]{1,0:T(8,128)(2,1)S(1)} collective-permute-done((bf16[8,1024]{1,0:T(8,128)(2,1)S(1)}, bf16[8,1024]{1,0:T(8,128)(2,1)S(1)}, u32[]{:S(2)}, u32[]{:S(2)}) %collective-permute-start.11) | collective-permute-done | bytes 16416 | tf_op jit(solution)/shard_map/ppermute | solution.py:152
  30.2 1.3 %shard_map.67.refs_0_ = f32[512,128]{1,0:T(8,128)S(1)} custom-call(f32[8,1024]{1,0:T(8,128)S(1)} %get-tuple-element.52.refs_0_, bf16[8,1024]{1,0:T(8,128)(2,1)S(1)} %collective-permute-done.11.refs_1_, bf16[8,1024]{1,0:T(8,128)(2,1)S(1)} %collective-permute-done.12.refs_2_, bf16[8,1024]{1,0:T(8,128)(2,1)S(1)} %collective-permute-done.13.refs_3_, ...), custom_call_target="tpu_custom_call" | custom-call | tf_op jit(solution)/shard_map/pallas_call | solution.py:141
  31.5 1.7 %shard_map.68 = (f32[8,1024]{1,0:T(8,128)S(1)}, f32[4,56,256]{2,1,0:T(8,128)S(1)}, bf16[256,256]{1,0:T(8,128)(2,1)S(1)}) custom-call(f32[512,128]{1,0:T(8,128)S(1)} %shard_map.67.refs_0_, bf16[56,512]{1,0:T(8,128)(2,1)S(1)} %pad_maximum_fusion.1.e.refs_1_, f32[512,1024]{1,0:T(8,128)S(1)} %get-tuple-element.44.refs_2_.refs_13_.refs_14_, ...), custom_call_target="tpu_custom_call" | custom-call | tf_op jit(solution)/shard_map/pallas_call | solution.py:141
  33.5 1.1 %collective-permute-done.14.g = bf16[256,256]{1,0:T(8,128)(2,1)S(1)} collective-permute-done((bf16[256,256]{1,0:T(8,128)(2,1)S(1)}, bf16[256,256]{1,0:T(8,128)(2,1)S(1)}, u32[]{:S(2)}, u32[]{:S(2)}) %collective-permute-start.14) | collective-permute-done | bytes 131104 | tf_op jit(solution)/shard_map/ppermute | solution.py:152
  34.7 0.8 %collective-permute-start.15 = (bf16[88,256]{1,0:T(8,128)(2,1)S(1)}, bf16[88,256]{1,0:T(8,128)(2,1)S(1)}, u32[]{:S(2)}, u32[]{:S(2)}) collective-permute-start(bf16[88,256]{1,0:T(8,128)(2,1)S(1)} %get-tuple-element.59), channel_id=1, source_target_pairs={{0,12},{4,8},{8,4},{12,0},{16,28},{20,24},{24,20},{28,16},{1,13},{... | collective-permute-start | bytes 135176 | tf_op jit(solution)/shard_map/ppermute | solution.py:152
  35.4 0.7 %collective-permute-start.16 = (bf16[88,256]{1,0:T(8,128)(2,1)S(1)}, bf16[88,256]{1,0:T(8,128)(2,1)S(1)}, u32[]{:S(2)}, u32[]{:S(2)}) collective-permute-start(bf16[88,256]{1,0:T(8,128)(2,1)S(1)} %get-tuple-element.60), channel_id=1, source_target_pairs={{0,20},{4,16},{8,28},{12,24},{16,4},{20,0},{24,12},{28,8},{1,21},{... | collective-permute-start | bytes 135176 | tf_op jit(solution)/shard_map/ppermute | solution.py:152
  36.1 1.7 %collective-permute-start.17 = (bf16[88,256]{1,0:T(8,128)(2,1)S(1)}, bf16[88,256]{1,0:T(8,128)(2,1)S(1)}, u32[]{:S(2)}, u32[]{:S(2)}) collective-permute-start(bf16[88,256]{1,0:T(8,128)(2,1)S(1)} %get-tuple-element.61), channel_id=1, source_target_pairs={{0,28},{4,24},{8,20},{12,16},{16,12},{20,8},{24,4},{28,0},{1,29},{... | collective-permute-start | bytes 135176 | tf_op jit(solution)/shard_map/ppermute | solution.py:152
  37.7 0.6 %collective-permute-done.15.refs_2_ = bf16[88,256]{1,0:T(8,128)(2,1)S(1)} collective-permute-done((bf16[88,256]{1,0:T(8,128)(2,1)S(1)}, bf16[88,256]{1,0:T(8,128)(2,1)S(1)}, u32[]{:S(2)}, u32[]{:S(2)}) %collective-permute-start.15) | collective-permute-done | bytes 45088 | tf_op jit(solution)/shard_map/ppermute | solution.py:152
  38.4 0.5 %collective-permute-done.16.refs_3_ = bf16[88,256]{1,0:T(8,128)(2,1)S(1)} collective-permute-done((bf16[88,256]{1,0:T(8,128)(2,1)S(1)}, bf16[88,256]{1,0:T(8,128)(2,1)S(1)}, u32[]{:S(2)}, u32[]{:S(2)}) %collective-permute-start.16) | collective-permute-done | bytes 45088 | tf_op jit(solution)/shard_map/ppermute | solution.py:152
  38.9 1.6 %collective-permute-done.17.refs_4_ = bf16[88,256]{1,0:T(8,128)(2,1)S(1)} collective-permute-done((bf16[88,256]{1,0:T(8,128)(2,1)S(1)}, bf16[88,256]{1,0:T(8,128)(2,1)S(1)}, u32[]{:S(2)}, u32[]{:S(2)}) %collective-permute-start.17) | collective-permute-done | bytes 45088 | tf_op jit(solution)/shard_map/ppermute | solution.py:152
  40.4 1.4 %shard_map.70 = (f32[50,128]{1,0:T(8,128)}, f32[50,256]{1,0:T(8,128)}) custom-call(f32[8,1024]{1,0:T(8,128)S(1)} %get-tuple-element.57.refs_0_, f32[56,256]{1,0:T(8,128)S(1)} %get-tuple-element.58.refs_1_, bf16[88,256]{1,0:T(8,128)(2,1)S(1)} %collective-permute-done.15.refs_2_, bf16[88,256]{1,0:T(8,128)(2,1)S(1)} %collective-permute-done.16.refs_3_, ...), custom_call_target="tpu_custom_call" | custom-call | tf_op jit(solution)/shard_map/pallas_call | solution.py:141
  (26 shorter events, 2.2 us)
Async XLA Ops:
  1.5 6.6 %collective-permute-start.2 = (bf16[56,384]{1,0:T(8,128)(2,1)S(1)}, bf16[56,384]{1,0:T(8,128)(2,1)S(1)}, u32[]{:S(2)}, u32[]{:S(2)}) collective-permute-start(bf16[56,384]{1,0:T(8,128)(2,1)S(1)} %shard_map.59), channel_id=1, source_target_pairs={{0,7},{1,6},{2,5},{3,4},{4,3},{5,2},{6,1},{7,0},{8,15},{9,14},{10,... | collective-permute-start | bytes 129032 | tf_op jit(solution)/shard_map/ppermute | solution.py:189
  6.0 4.8 %collective-permute-start.1 = (bf16[56,384]{1,0:T(8,128)(2,1)S(1)}, bf16[56,384]{1,0:T(8,128)(2,1)S(1)}, u32[]{:S(2)}, u32[]{:S(2)}) collective-permute-start(bf16[56,384]{1,0:T(8,128)(2,1)S(1)} %shard_map.59), channel_id=1, source_target_pairs={{0,6},{1,7},{2,4},{3,5},{4,2},{5,3},{6,0},{7,1},{8,14},{9,15},{10,... | collective-permute-start | bytes 129032 | tf_op jit(solution)/shard_map/ppermute | solution.py:189
  6.0 4.8 %collective-permute-start = (bf16[56,384]{1,0:T(8,128)(2,1)S(1)}, bf16[56,384]{1,0:T(8,128)(2,1)S(1)}, u32[]{:S(2)}, u32[]{:S(2)}) collective-permute-start(bf16[56,384]{1,0:T(8,128)(2,1)S(1)} %shard_map.59), channel_id=1, source_target_pairs={{0,5},{1,4},{2,7},{3,6},{4,1},{5,0},{6,3},{7,2},{8,13},{9,12},{10,... | collective-permute-start | bytes 129032 | tf_op jit(solution)/shard_map/ppermute | solution.py:189
  10.8 4.0 %collective-permute-start.6 = (bf16[56,1024]{1,0:T(8,128)(2,1)S(1)}, bf16[56,1024]{1,0:T(8,128)(2,1)S(1)}, u32[]{:S(2)}, u32[]{:S(2)}) collective-permute-start(bf16[56,1024]{1,0:T(8,128)(2,1)S(1)} %pad_maximum_fusion.y_ref.refs_5_.refs_6_), channel_id=1, source_target_pairs={{0,4},{4,0},{8,12},{12,8},{16,20},{20,16},{24,28},{28,24},{1,5},{5... | collective-permute-start | bytes 344072 | tf_op jit(solution)/shard_map/ppermute | solution.py:152
  11.2 5.3 %collective-permute-start.5 = (bf16[56,1024]{1,0:T(8,128)(2,1)S(1)}, bf16[56,1024]{1,0:T(8,128)(2,1)S(1)}, u32[]{:S(2)}, u32[]{:S(2)}) collective-permute-start(bf16[56,1024]{1,0:T(8,128)(2,1)S(1)} %pad_maximum_fusion.y_ref.refs_5_.refs_6_), channel_id=1, source_target_pairs={{0,16},{4,20},{8,24},{12,28},{16,0},{20,4},{24,8},{28,12},{1,17},{... | collective-permute-start | bytes 344072 | tf_op jit(solution)/shard_map/ppermute | solution.py:152
  12.7 5.6 %collective-permute-start.4 = (bf16[56,1024]{1,0:T(8,128)(2,1)S(1)}, bf16[56,1024]{1,0:T(8,128)(2,1)S(1)}, u32[]{:S(2)}, u32[]{:S(2)}) collective-permute-start(bf16[56,1024]{1,0:T(8,128)(2,1)S(1)} %pad_maximum_fusion.y_ref.refs_5_.refs_6_), channel_id=1, source_target_pairs={{0,8},{4,12},{8,0},{12,4},{16,24},{20,28},{24,16},{28,20},{1,9},{5... | collective-permute-start | bytes 344072 | tf_op jit(solution)/shard_map/ppermute | solution.py:152
  14.2 6.2 %collective-permute-start.3 = (bf16[56,1024]{1,0:T(8,128)(2,1)S(1)}, bf16[56,1024]{1,0:T(8,128)(2,1)S(1)}, u32[]{:S(2)}, u32[]{:S(2)}) collective-permute-start(bf16[56,1024]{1,0:T(8,128)(2,1)S(1)} %pad_maximum_fusion.y_ref.refs_5_.refs_6_), channel_id=1, source_target_pairs={{0,28},{4,24},{8,20},{12,16},{16,12},{20,8},{24,4},{28,0},{1,29},{... | collective-permute-start | bytes 344072 | tf_op jit(solution)/shard_map/ppermute | solution.py:152
  18.3 2.1 %collective-permute-start.7 = (bf16[56,1024]{1,0:T(8,128)(2,1)S(1)}, bf16[56,1024]{1,0:T(8,128)(2,1)S(1)}, u32[]{:S(2)}, u32[]{:S(2)}) collective-permute-start(bf16[56,1024]{1,0:T(8,128)(2,1)S(1)} %collective-permute-done.4.refs_2_.refs_7_.refs_8_), channel_id=1, source_target_pairs={{0,4},{4,0},{8,12},{12,8},{16,20},{20,16},{24,28},{28,24},{1,5},{5... | collective-permute-start | bytes 344072 | tf_op jit(solution)/shard_map/ppermute | solution.py:152
  18.3 2.1 %collective-permute-start.8 = (bf16[56,1024]{1,0:T(8,128)(2,1)S(1)}, bf16[56,1024]{1,0:T(8,128)(2,1)S(1)}, u32[]{:S(2)}, u32[]{:S(2)}) collective-permute-start(bf16[56,1024]{1,0:T(8,128)(2,1)S(1)} %collective-permute-done.5.refs_3_.refs_9_.refs_10_), channel_id=1, source_target_pairs={{0,4},{4,0},{8,12},{12,8},{16,20},{20,16},{24,28},{28,24},{1,5},{5... | collective-permute-start | bytes 344072 | tf_op jit(solution)/shard_map/ppermute | solution.py:152
  20.4 1.3 %collective-permute-start.9 = (bf16[56,1024]{1,0:T(8,128)(2,1)S(1)}, bf16[56,1024]{1,0:T(8,128)(2,1)S(1)}, u32[]{:S(2)}, u32[]{:S(2)}) collective-permute-start(bf16[56,1024]{1,0:T(8,128)(2,1)S(1)} %collective-permute-done.3.refs_2_.refs_12_.refs_13_), channel_id=1, source_target_pairs={{0,4},{4,0},{8,12},{12,8},{16,20},{20,16},{24,28},{28,24},{1,5},{5... | collective-permute-start | bytes 344072 | tf_op jit(solution)/shard_map/ppermute | solution.py:152
  23.4 1.3 %collective-permute-start.10 = (f32[8,1024]{1,0:T(8,128)S(1)}, f32[8,1024]{1,0:T(8,128)S(1)}, u32[]{:S(2)}, u32[]{:S(2)}) collective-permute-start(f32[8,1024]{1,0:T(8,128)S(1)} %shard_map.65.t), channel_id=1, source_target_pairs={{0,4},{4,0},{8,12},{12,8},{16,20},{20,16},{24,28},{28,24},{1,5},{5... | collective-permute-start | bytes 98312 | tf_op jit(solution)/shard_map/ppermute | solution.py:152
  24.7 4.1 %collective-permute-start.13 = (bf16[8,1024]{1,0:T(8,128)(2,1)S(1)}, bf16[8,1024]{1,0:T(8,128)(2,1)S(1)}, u32[]{:S(2)}, u32[]{:S(2)}) collective-permute-start(bf16[8,1024]{1,0:T(8,128)(2,1)S(1)} %get-tuple-element.53), channel_id=1, source_target_pairs={{0,28},{4,24},{8,20},{12,16},{16,12},{20,8},{24,4},{28,0},{1,29},{... | collective-permute-start | bytes 49160 | tf_op jit(solution)/shard_map/ppermute | solution.py:152
  26.3 3.2 %collective-permute-start.12 = (bf16[8,1024]{1,0:T(8,128)(2,1)S(1)}, bf16[8,1024]{1,0:T(8,128)(2,1)S(1)}, u32[]{:S(2)}, u32[]{:S(2)}) collective-permute-start(bf16[8,1024]{1,0:T(8,128)(2,1)S(1)} %get-tuple-element.53), channel_id=1, source_target_pairs={{0,20},{4,16},{8,28},{12,24},{16,4},{20,0},{24,12},{28,8},{1,21},{... | collective-permute-start | bytes 49160 | tf_op jit(solution)/shard_map/ppermute | solution.py:152
  27.0 3.2 %collective-permute-start.11 = (bf16[8,1024]{1,0:T(8,128)(2,1)S(1)}, bf16[8,1024]{1,0:T(8,128)(2,1)S(1)}, u32[]{:S(2)}, u32[]{:S(2)}) collective-permute-start(bf16[8,1024]{1,0:T(8,128)(2,1)S(1)} %get-tuple-element.53), channel_id=1, source_target_pairs={{0,12},{4,8},{8,4},{12,0},{16,28},{20,24},{24,20},{28,16},{1,13},{... | collective-permute-start | bytes 49160 | tf_op jit(solution)/shard_map/ppermute | solution.py:152
  33.2 1.4 %collective-permute-start.14 = (bf16[256,256]{1,0:T(8,128)(2,1)S(1)}, bf16[256,256]{1,0:T(8,128)(2,1)S(1)}, u32[]{:S(2)}, u32[]{:S(2)}) collective-permute-start(bf16[256,256]{1,0:T(8,128)(2,1)S(1)} %get-tuple-element.56), channel_id=1, source_target_pairs={{0,4},{4,0},{8,12},{12,8},{16,20},{20,16},{24,28},{28,24},{1,5},{5... | collective-permute-start | bytes 393224 | tf_op jit(solution)/shard_map/ppermute | solution.py:152
  34.7 3.7 %collective-permute-start.15 = (bf16[88,256]{1,0:T(8,128)(2,1)S(1)}, bf16[88,256]{1,0:T(8,128)(2,1)S(1)}, u32[]{:S(2)}, u32[]{:S(2)}) collective-permute-start(bf16[88,256]{1,0:T(8,128)(2,1)S(1)} %get-tuple-element.59), channel_id=1, source_target_pairs={{0,12},{4,8},{8,4},{12,0},{16,28},{20,24},{24,20},{28,16},{1,13},{... | collective-permute-start | bytes 135176 | tf_op jit(solution)/shard_map/ppermute | solution.py:152
  35.4 3.5 %collective-permute-start.16 = (bf16[88,256]{1,0:T(8,128)(2,1)S(1)}, bf16[88,256]{1,0:T(8,128)(2,1)S(1)}, u32[]{:S(2)}, u32[]{:S(2)}) collective-permute-start(bf16[88,256]{1,0:T(8,128)(2,1)S(1)} %get-tuple-element.60), channel_id=1, source_target_pairs={{0,20},{4,16},{8,28},{12,24},{16,4},{20,0},{24,12},{28,8},{1,21},{... | collective-permute-start | bytes 135176 | tf_op jit(solution)/shard_map/ppermute | solution.py:152
  36.1 4.4 %collective-permute-start.17 = (bf16[88,256]{1,0:T(8,128)(2,1)S(1)}, bf16[88,256]{1,0:T(8,128)(2,1)S(1)}, u32[]{:S(2)}, u32[]{:S(2)}) collective-permute-start(bf16[88,256]{1,0:T(8,128)(2,1)S(1)} %get-tuple-element.61), channel_id=1, source_target_pairs={{0,28},{4,24},{8,20},{12,16},{16,12},{20,8},{24,4},{28,0},{1,29},{... | collective-permute-start | bytes 135176 | tf_op jit(solution)/shard_map/ppermute | solution.py:152

commit v6 on v5

--- a/solution.py
+++ b/solution.py
@@ -90,11 +90,20 @@
     groups(k.shape[0], body, unroll=unroll)
 
 
-def col_pass(k, u, width, unroll):
-    def body(rs, carry):
-        return carry + k[rs, :] * spread(u[rs, :], width)
-
-    return groups(k.shape[0], body, jnp.zeros((SUB, width), f32), unroll)
+def col_pass(k, u, width, unroll, z=None):
+    step = 2 * SUB
+
+    def body(i, carry):
+        rs = pl.ds(pl.multiple_of(i * step, step), step)
+        p = k[rs, :] * spread(u[rs, :], width)
+        if z is not None:
+            z[rs, :] = p[:, 0 : z.shape[1]].astype(bf16)
+        return carry + p[0:SUB, :] + p[SUB:, :]
+
+    n = k.shape[0] // step
+    return lax.fori_loop(
+        0, n, body, jnp.zeros((SUB, width), f32), unroll=min(unroll // 2, n)
+    )
 
 
 def scaling(weights, acc, u):
@@ -238,9 +247,9 @@
         acc = more([m ^ 1 for m in late], acc)
         matrix = ks if kept else [xt, *y]
 
-        def column_sums(k, u, tot, unroll):
+        def column_sums(k, u, tot, unroll, z=None):
             for i in range(rows):
-                s = col_pass(k(i), u, T, unroll)
+                s = col_pass(k(i), u, T, unroll, z if z is None else z.at[i])
                 tot[i : i + 1, :] = jnp.sum(s, axis=0, keepdims=True)
 
         def first_sums(*refs):
@@ -303,22 +312,17 @@
         def second_cols(*refs):
             r = Refs(refs)
             u, x, kr = r.take(ONE, ONE, n_held)
-            tot_o, keep_o, send_o = r.take(ONE, ONE, ONE)
-            k = blocks(kr, r.refs)
-            column_sums(k, u, tot_o, 64)
+            tot_o, keep_o, send_o, z = r.take(ONE, ONE, ONE, ONE)
+            column_sums(blocks(kr, r.refs), u, tot_o, 64, z)
 
             def weighted(mask):
-                z = (k(mask)[:, 0:ny] * spread_to(u[...], ny)).astype(bf16)
-                return jnp.dot(x[...], z, preferred_element_type=f32)
+                return jnp.dot(x[...], z[mask], preferred_element_type=f32)
 
             send_o[0:n_tot, :] = pack_tot(tot_o[...])
             for n, mask in enumerate(ends):
                 keep_o[n, :, 0:ny] = weighted(mask)
                 at = n_tot + n * EXT
                 send_o[at : at + EXT, 0:ny] = weighted(mask ^ 1).astype(bf16)
-
-        def spread_to(u, n):
-            return u[:, 0:n] if n <= LANES else spread(u, n)
 
         tot, keep, send = call(
             second_cols,
@@ -328,7 +332,7 @@
                 jax.ShapeDtypeStruct((n_tot + len(ends) * EXT, width), bf16),
             ),
             [u, xe, *matrix],
-            spare,
+            [pltpu.VMEM((rows, X, ny), bf16)] + spare,
         )
 
         def join(t, kp, g, tot_o, keep_o, *sends):

time: 42.1 us -> 41.8 us (level)
  no operation moved by 1% of the time
where the time goes in v6:
time: 41.8 us; the launch traced here: 41.5 us
  starting transfers between devices  16 us (38%)
  waiting for transfers between devices  15.4 us (37%)
  Pallas kernels  9.28 us (22%)
  between operations  0.76 us (2%)
    ppermute x15, waiting for transfers between devices, swap(): return lax.ppermute(t, 'row', xor_perm(rows, m))  11.6 us
    ppermute x15, starting transfers between devices, swap(): return lax.ppermute(t, 'row', xor_perm(rows, m))  10.5 us
    pallas_call x12, Pallas kernels, call(): pl.pallas_call(kernel, out_shape=outs, in_specs=[spec] * len(args), out_s...  9.28 us
    ppermute x3, starting transfers between devices, per_device(): lax.ppermute(own, ('row', 'col'), xor_perm(rows * cols, cols + m))  5.48 us
    ppermute x3, waiting for transfers between devices, per_device(): lax.ppermute(own, ('row', 'col'), xor_perm(rows * cols, cols + m))  3.83 us
  transfers between devices with their start and end apart: 18, of which 14 were waited for; matrix products, arithmetic and copies ran while one was open for 0% of the time, Pallas kernels for 6%

profile of v6, /device:TPU:0, one launch (start us, length us, event | category | flops | bytes accessed | tf_op | source)
XLA Modules:
  0.0 41.5 jit_solution(2814458982231888631)
XLA Ops:
  0.6 0.8 %shard_map.59 = bf16[56,384]{1,0:T(8,128)(2,1)S(1)} custom-call(bf16[50,128]{1,0:T(8,128)(2,1)} %x_hbm.1, bf16[50,256]{1,0:T(8,128)(2,1)} %y_hbm.1, bf16[128]{0:T(256)(128)(2,1)} %a_hbm.1, bf16[256]{0:T(256)(128)(2,1)} %b_hbm.1), custom_call_target="tpu_custom_call" | custom-call | tf_op jit(solution)/shard_map/pallas_call | solution.py:150
  1.5 4.6 %collective-permute-start.2 = (bf16[56,384]{1,0:T(8,128)(2,1)S(1)}, bf16[56,384]{1,0:T(8,128)(2,1)S(1)}, u32[]{:S(2)}, u32[]{:S(2)}) collective-permute-start(bf16[56,384]{1,0:T(8,128)(2,1)S(1)} %shard_map.59), channel_id=1, source_target_pairs={{0,7},{1,6},{2,5},{3,4},{4,3},{5,2},{6,1},{7,0},{8,15},{9,14},{10,... | collective-permute-start | bytes 129032 | tf_op jit(solution)/shard_map/ppermute | solution.py:198
  6.0 0.9 %collective-permute-start = (bf16[56,384]{1,0:T(8,128)(2,1)S(1)}, bf16[56,384]{1,0:T(8,128)(2,1)S(1)}, u32[]{:S(2)}, u32[]{:S(2)}) collective-permute-start(bf16[56,384]{1,0:T(8,128)(2,1)S(1)} %shard_map.59), channel_id=1, source_target_pairs={{0,5},{1,4},{2,7},{3,6},{4,1},{5,0},{6,3},{7,2},{8,13},{9,12},{10,... | collective-permute-start | bytes 129032 | tf_op jit(solution)/shard_map/ppermute | solution.py:198
  7.0 1.1 %collective-permute-done.2 = bf16[56,384]{1,0:T(8,128)(2,1)S(1)} collective-permute-done((bf16[56,384]{1,0:T(8,128)(2,1)S(1)}, bf16[56,384]{1,0:T(8,128)(2,1)S(1)}, u32[]{:S(2)}, u32[]{:S(2)}) %collective-permute-start.2) | collective-permute-done | bytes 43040 | tf_op jit(solution)/shard_map/ppermute | solution.py:198
  8.0 2.8 %collective-permute-done.1 = bf16[56,384]{1,0:T(8,128)(2,1)S(1)} collective-permute-done((bf16[56,384]{1,0:T(8,128)(2,1)S(1)}, bf16[56,384]{1,0:T(8,128)(2,1)S(1)}, u32[]{:S(2)}, u32[]{:S(2)}) %collective-permute-start.1) | collective-permute-done | bytes 43040 | tf_op jit(solution)/shard_map/ppermute | solution.py:198
  11.2 1.5 %collective-permute-start.5 = (bf16[56,1024]{1,0:T(8,128)(2,1)S(1)}, bf16[56,1024]{1,0:T(8,128)(2,1)S(1)}, u32[]{:S(2)}, u32[]{:S(2)}) collective-permute-start(bf16[56,1024]{1,0:T(8,128)(2,1)S(1)} %pad_maximum_fusion.y_ref.refs_5_.refs_6_), channel_id=1, source_target_pairs={{0,16},{4,20},{8,24},{12,28},{16,0},{20,4},{24,8},{28,12},{1,17},{... | collective-permute-start | bytes 344072 | tf_op jit(solution)/shard_map/ppermute | solution.py:161
  12.7 1.5 %collective-permute-start.4 = (bf16[56,1024]{1,0:T(8,128)(2,1)S(1)}, bf16[56,1024]{1,0:T(8,128)(2,1)S(1)}, u32[]{:S(2)}, u32[]{:S(2)}) collective-permute-start(bf16[56,1024]{1,0:T(8,128)(2,1)S(1)} %pad_maximum_fusion.y_ref.refs_5_.refs_6_), channel_id=1, source_target_pairs={{0,8},{4,12},{8,0},{12,4},{16,24},{20,28},{24,16},{28,20},{1,9},{5... | collective-permute-start | bytes 344072 | tf_op jit(solution)/shard_map/ppermute | solution.py:161
  14.2 0.5 %shard_map.60 = (bf16[512,56]{1,0:T(8,128)(2,1)S(1)}, f32[512,128]{1,0:T(8,128)S(1)}, f32[512,128]{1,0:T(8,128)S(1)}, f32[512,1024]{1,0:T(8,128)S(1)}) custom-call(bf16[56,512]{1,0:T(8,128)(2,1)S(1)} %pad_maximum_fusion.1.e.refs_1_, bf16[56,1024]{1,0:T(8,128)(2,1)S(1)} %pad_maximum_fusion.y_ref.refs_5_.refs_6_), custom_call_target="tpu_custom_call" | custom-call | flops 1 | bytes 1 | tf_op jit(solution)/shard_map/pallas_call | solution.py:150
  15.2 1.2 %collective-permute-done.5.refs_3_.refs_9_.refs_10_ = bf16[56,1024]{1,0:T(8,128)(2,1)S(1)} collective-permute-done((bf16[56,1024]{1,0:T(8,128)(2,1)S(1)}, bf16[56,1024]{1,0:T(8,128)(2,1)S(1)}, u32[]{:S(2)}, u32[]{:S(2)}) %collective-permute-start.5) | collective-permute-done | bytes 114720 | tf_op jit(solution)/shard_map/ppermute | solution.py:161
  16.4 1.8 %collective-permute-done.4.refs_2_.refs_7_.refs_8_ = bf16[56,1024]{1,0:T(8,128)(2,1)S(1)} collective-permute-done((bf16[56,1024]{1,0:T(8,128)(2,1)S(1)}, bf16[56,1024]{1,0:T(8,128)(2,1)S(1)}, u32[]{:S(2)}, u32[]{:S(2)}) %collective-permute-start.4) | collective-permute-done | bytes 114720 | tf_op jit(solution)/shard_map/ppermute | solution.py:161
  18.3 0.5 %collective-permute-start.8 = (bf16[56,1024]{1,0:T(8,128)(2,1)S(1)}, bf16[56,1024]{1,0:T(8,128)(2,1)S(1)}, u32[]{:S(2)}, u32[]{:S(2)}) collective-permute-start(bf16[56,1024]{1,0:T(8,128)(2,1)S(1)} %collective-permute-done.5.refs_3_.refs_9_.refs_10_), channel_id=1, source_target_pairs={{0,4},{4,0},{8,12},{12,8},{16,20},{20,16},{24,28},{28,24},{1,5},{5... | collective-permute-start | bytes 344072 | tf_op jit(solution)/shard_map/ppermute | solution.py:161
  18.8 0.7 %shard_map.62 = (f32[512,128]{1,0:T(8,128)S(1)}, f32[512,1024]{1,0:T(8,128)S(1)}, f32[512,1024]{1,0:T(8,128)S(1)}) custom-call(bf16[512,56]{1,0:T(8,128)(2,1)S(1)} %get-tuple-element.32.refs_0_.refs_5_, f32[512,128]{1,0:T(8,128)S(1)} %get-tuple-element.35.refs_1_, bf16[56,1024]{1,0:T(8,128)(2,1)S(1)} %collective-permute-done.4.refs_2_.refs_7_.refs_8_, ...), custom_call_target="tpu_custom_call" | custom-call | flops 1 | bytes 1 | tf_op jit(solution)/shard_map/pallas_call | solution.py:150
  19.5 0.9 %collective-permute-done.3.refs_2_.refs_12_.refs_13_ = bf16[56,1024]{1,0:T(8,128)(2,1)S(1)} collective-permute-done((bf16[56,1024]{1,0:T(8,128)(2,1)S(1)}, bf16[56,1024]{1,0:T(8,128)(2,1)S(1)}, u32[]{:S(2)}, u32[]{:S(2)}) %collective-permute-start.3) | collective-permute-done | bytes 114720 | tf_op jit(solution)/shard_map/ppermute | solution.py:161
  20.4 1.0 %shard_map.63 = (f32[512,128]{1,0:T(8,128)S(1)}, f32[512,1024]{1,0:T(8,128)S(1)}, f32[512,1024]{1,0:T(8,128)S(1)}, f32[512,1024]{1,0:T(8,128)S(1)}) custom-call(bf16[512,56]{1,0:T(8,128)(2,1)S(1)} %get-tuple-element.32.refs_0_.refs_5_, f32[512,128]{1,0:T(8,128)S(1)} %get-tuple-element.39.refs_1_, ...), custom_call_target="tpu_custom_call" | custom-call | flops 1 | bytes 1 | tf_op jit(solution)/shard_map/pallas_call | solution.py:150
  22.1 1.3 %shard_map.65.t = f32[8,1024]{1,0:T(8,128)S(1)} custom-call(f32[512,128]{1,0:T(8,128)S(1)} %get-tuple-element.42.refs_0_, f32[512,128]{1,0:T(8,128)S(1)} %get-tuple-element.43.refs_1_.refs_4_, f32[512,1024]{1,0:T(8,128)S(1)} %get-tuple-element.44.refs_2_.refs_13_.refs_14_, f32[512,1024]{1,0:T(8,128)S(1)} %get-tuple-element.45.refs_3_.refs_14_.refs_15_, ...), custom_call_target="tpu_custom_call" | custom-call | tf_op jit(solution)/shard_map/pallas_call | solution.py:150
  23.6 1.0 %collective-permute-done.10.g = f32[8,1024]{1,0:T(8,128)S(1)} collective-permute-done((f32[8,1024]{1,0:T(8,128)S(1)}, f32[8,1024]{1,0:T(8,128)S(1)}, u32[]{:S(2)}, u32[]{:S(2)}) %collective-permute-start.10) | collective-permute-done | bytes 32800 | tf_op jit(solution)/shard_map/ppermute | solution.py:161
  24.7 1.7 %collective-permute-start.13 = (bf16[8,1024]{1,0:T(8,128)(2,1)S(1)}, bf16[8,1024]{1,0:T(8,128)(2,1)S(1)}, u32[]{:S(2)}, u32[]{:S(2)}) collective-permute-start(bf16[8,1024]{1,0:T(8,128)(2,1)S(1)} %get-tuple-element.53), channel_id=1, source_target_pairs={{0,28},{4,24},{8,20},{12,16},{16,12},{20,8},{24,4},{28,0},{1,29},{... | collective-permute-start | bytes 49160 | tf_op jit(solution)/shard_map/ppermute | solution.py:161
  26.3 0.7 %collective-permute-start.12 = (bf16[8,1024]{1,0:T(8,128)(2,1)S(1)}, bf16[8,1024]{1,0:T(8,128)(2,1)S(1)}, u32[]{:S(2)}, u32[]{:S(2)}) collective-permute-start(bf16[8,1024]{1,0:T(8,128)(2,1)S(1)} %get-tuple-element.53), channel_id=1, source_target_pairs={{0,20},{4,16},{8,28},{12,24},{16,4},{20,0},{24,12},{28,8},{1,21},{... | collective-permute-start | bytes 49160 | tf_op jit(solution)/shard_map/ppermute | solution.py:161
  27.1 0.7 %collective-permute-start.11 = (bf16[8,1024]{1,0:T(8,128)(2,1)S(1)}, bf16[8,1024]{1,0:T(8,128)(2,1)S(1)}, u32[]{:S(2)}, u32[]{:S(2)}) collective-permute-start(bf16[8,1024]{1,0:T(8,128)(2,1)S(1)} %get-tuple-element.53), channel_id=1, source_target_pairs={{0,12},{4,8},{8,4},{12,0},{16,28},{20,24},{24,20},{28,16},{1,13},{... | collective-permute-start | bytes 49160 | tf_op jit(solution)/shard_map/ppermute | solution.py:161
  27.7 1.1 %collective-permute-done.13.refs_3_ = bf16[8,1024]{1,0:T(8,128)(2,1)S(1)} collective-permute-done((bf16[8,1024]{1,0:T(8,128)(2,1)S(1)}, bf16[8,1024]{1,0:T(8,128)(2,1)S(1)}, u32[]{:S(2)}, u32[]{:S(2)}) %collective-permute-start.13) | collective-permute-done | bytes 16416 | tf_op jit(solution)/shard_map/ppermute | solution.py:161
  28.8 0.7 %collective-permute-done.12.refs_2_ = bf16[8,1024]{1,0:T(8,128)(2,1)S(1)} collective-permute-done((bf16[8,1024]{1,0:T(8,128)(2,1)S(1)}, bf16[8,1024]{1,0:T(8,128)(2,1)S(1)}, u32[]{:S(2)}, u32[]{:S(2)}) %collective-permute-start.12) | collective-permute-done | bytes 16416 | tf_op jit(solution)/shard_map/ppermute | solution.py:161
  29.5 0.7 %collective-permute-done.11.refs_1_ = bf16[8,1024]{1,0:T(8,128)(2,1)S(1)} collective-permute-done((bf16[8,1024]{1,0:T(8,128)(2,1)S(1)}, bf16[8,1024]{1,0:T(8,128)(2,1)S(1)}, u32[]{:S(2)}, u32[]{:S(2)}) %collective-permute-start.11) | collective-permute-done | bytes 16416 | tf_op jit(solution)/shard_map/ppermute | solution.py:161
  30.2 1.3 %shard_map.67.refs_0_ = f32[512,128]{1,0:T(8,128)S(1)} custom-call(f32[8,1024]{1,0:T(8,128)S(1)} %get-tuple-element.52.refs_0_, bf16[8,1024]{1,0:T(8,128)(2,1)S(1)} %collective-permute-done.11.refs_1_, bf16[8,1024]{1,0:T(8,128)(2,1)S(1)} %collective-permute-done.12.refs_2_, bf16[8,1024]{1,0:T(8,128)(2,1)S(1)} %collective-permute-done.13.refs_3_, ...), custom_call_target="tpu_custom_call" | custom-call | tf_op jit(solution)/shard_map/pallas_call | solution.py:150
  31.5 1.4 %shard_map.68 = (f32[8,1024]{1,0:T(8,128)S(1)}, f32[4,56,256]{2,1,0:T(8,128)S(1)}, bf16[256,256]{1,0:T(8,128)(2,1)S(1)}) custom-call(f32[512,128]{1,0:T(8,128)S(1)} %shard_map.67.refs_0_, bf16[56,512]{1,0:T(8,128)(2,1)S(1)} %pad_maximum_fusion.1.e.refs_1_, f32[512,1024]{1,0:T(8,128)S(1)} %get-tuple-element.44.refs_2_.refs_13_.refs_14_, ...), custom_call_target="tpu_custom_call" | custom-call | tf_op jit(solution)/shard_map/pallas_call | solution.py:150
  33.2 1.1 %collective-permute-done.14.g = bf16[256,256]{1,0:T(8,128)(2,1)S(1)} collective-permute-done((bf16[256,256]{1,0:T(8,128)(2,1)S(1)}, bf16[256,256]{1,0:T(8,128)(2,1)S(1)}, u32[]{:S(2)}, u32[]{:S(2)}) %collective-permute-start.14) | collective-permute-done | bytes 131104 | tf_op jit(solution)/shard_map/ppermute | solution.py:161
  34.4 0.7 %collective-permute-start.15 = (bf16[88,256]{1,0:T(8,128)(2,1)S(1)}, bf16[88,256]{1,0:T(8,128)(2,1)S(1)}, u32[]{:S(2)}, u32[]{:S(2)}) collective-permute-start(bf16[88,256]{1,0:T(8,128)(2,1)S(1)} %get-tuple-element.59), channel_id=1, source_target_pairs={{0,12},{4,8},{8,4},{12,0},{16,28},{20,24},{24,20},{28,16},{1,13},{... | collective-permute-start | bytes 135176 | tf_op jit(solution)/shard_map/ppermute | solution.py:161
  35.1 0.7 %collective-permute-start.16 = (bf16[88,256]{1,0:T(8,128)(2,1)S(1)}, bf16[88,256]{1,0:T(8,128)(2,1)S(1)}, u32[]{:S(2)}, u32[]{:S(2)}) collective-permute-start(bf16[88,256]{1,0:T(8,128)(2,1)S(1)} %get-tuple-element.60), channel_id=1, source_target_pairs={{0,20},{4,16},{8,28},{12,24},{16,4},{20,0},{24,12},{28,8},{1,21},{... | collective-permute-start | bytes 135176 | tf_op jit(solution)/shard_map/ppermute | solution.py:161
  35.8 1.7 %collective-permute-start.17 = (bf16[88,256]{1,0:T(8,128)(2,1)S(1)}, bf16[88,256]{1,0:T(8,128)(2,1)S(1)}, u32[]{:S(2)}, u32[]{:S(2)}) collective-permute-start(bf16[88,256]{1,0:T(8,128)(2,1)S(1)} %get-tuple-element.61), channel_id=1, source_target_pairs={{0,28},{4,24},{8,20},{12,16},{16,12},{20,8},{24,4},{28,0},{1,29},{... | collective-permute-start | bytes 135176 | tf_op jit(solution)/shard_map/ppermute | solution.py:161
  37.5 0.6 %collective-permute-done.15.refs_2_ = bf16[88,256]{1,0:T(8,128)(2,1)S(1)} collective-permute-done((bf16[88,256]{1,0:T(8,128)(2,1)S(1)}, bf16[88,256]{1,0:T(8,128)(2,1)S(1)}, u32[]{:S(2)}, u32[]{:S(2)}) %collective-permute-start.15) | collective-permute-done | bytes 45088 | tf_op jit(solution)/shard_map/ppermute | solution.py:161
  38.1 0.5 %collective-permute-done.16.refs_3_ = bf16[88,256]{1,0:T(8,128)(2,1)S(1)} collective-permute-done((bf16[88,256]{1,0:T(8,128)(2,1)S(1)}, bf16[88,256]{1,0:T(8,128)(2,1)S(1)}, u32[]{:S(2)}, u32[]{:S(2)}) %collective-permute-start.16) | collective-permute-done | bytes 45088 | tf_op jit(solution)/shard_map/ppermute | solution.py:161
  38.6 1.6 %collective-permute-done.17.refs_4_ = bf16[88,256]{1,0:T(8,128)(2,1)S(1)} collective-permute-done((bf16[88,256]{1,0:T(8,128)(2,1)S(1)}, bf16[88,256]{1,0:T(8,128)(2,1)S(1)}, u32[]{:S(2)}, u32[]{:S(2)}) %collective-permute-start.17) | collective-permute-done | bytes 45088 | tf_op jit(solution)/shard_map/ppermute | solution.py:161
  40.2 1.4 %shard_map.70 = (f32[50,128]{1,0:T(8,128)}, f32[50,256]{1,0:T(8,128)}) custom-call(f32[8,1024]{1,0:T(8,128)S(1)} %get-tuple-element.57.refs_0_, f32[56,256]{1,0:T(8,128)S(1)} %get-tuple-element.58.refs_1_, bf16[88,256]{1,0:T(8,128)(2,1)S(1)} %collective-permute-done.15.refs_2_, bf16[88,256]{1,0:T(8,128)(2,1)S(1)} %collective-permute-done.16.refs_3_, ...), custom_call_target="tpu_custom_call" | custom-call | tf_op jit(solution)/shard_map/pallas_call | solution.py:150
  (26 shorter events, 2.2 us)
Async XLA Ops:
  1.5 6.6 %collective-permute-start.2 = (bf16[56,384]{1,0:T(8,128)(2,1)S(1)}, bf16[56,384]{1,0:T(8,128)(2,1)S(1)}, u32[]{:S(2)}, u32[]{:S(2)}) collective-permute-start(bf16[56,384]{1,0:T(8,128)(2,1)S(1)} %shard_map.59), channel_id=1, source_target_pairs={{0,7},{1,6},{2,5},{3,4},{4,3},{5,2},{6,1},{7,0},{8,15},{9,14},{10,... | collective-permute-start | bytes 129032 | tf_op jit(solution)/shard_map/ppermute | solution.py:198
  6.0 4.8 %collective-permute-start.1 = (bf16[56,384]{1,0:T(8,128)(2,1)S(1)}, bf16[56,384]{1,0:T(8,128)(2,1)S(1)}, u32[]{:S(2)}, u32[]{:S(2)}) collective-permute-start(bf16[56,384]{1,0:T(8,128)(2,1)S(1)} %shard_map.59), channel_id=1, source_target_pairs={{0,6},{1,7},{2,4},{3,5},{4,2},{5,3},{6,0},{7,1},{8,14},{9,15},{10,... | collective-permute-start | bytes 129032 | tf_op jit(solution)/shard_map/ppermute | solution.py:198
  6.0 4.8 %collective-permute-start = (bf16[56,384]{1,0:T(8,128)(2,1)S(1)}, bf16[56,384]{1,0:T(8,128)(2,1)S(1)}, u32[]{:S(2)}, u32[]{:S(2)}) collective-permute-start(bf16[56,384]{1,0:T(8,128)(2,1)S(1)} %shard_map.59), channel_id=1, source_target_pairs={{0,5},{1,4},{2,7},{3,6},{4,1},{5,0},{6,3},{7,2},{8,13},{9,12},{10,... | collective-permute-start | bytes 129032 | tf_op jit(solution)/shard_map/ppermute | solution.py:198
  10.8 4.0 %collective-permute-start.6 = (bf16[56,1024]{1,0:T(8,128)(2,1)S(1)}, bf16[56,1024]{1,0:T(8,128)(2,1)S(1)}, u32[]{:S(2)}, u32[]{:S(2)}) collective-permute-start(bf16[56,1024]{1,0:T(8,128)(2,1)S(1)} %pad_maximum_fusion.y_ref.refs_5_.refs_6_), channel_id=1, source_target_pairs={{0,4},{4,0},{8,12},{12,8},{16,20},{20,16},{24,28},{28,24},{1,5},{5... | collective-permute-start | bytes 344072 | tf_op jit(solution)/shard_map/ppermute | solution.py:161
  11.2 5.3 %collective-permute-start.5 = (bf16[56,1024]{1,0:T(8,128)(2,1)S(1)}, bf16[56,1024]{1,0:T(8,128)(2,1)S(1)}, u32[]{:S(2)}, u32[]{:S(2)}) collective-permute-start(bf16[56,1024]{1,0:T(8,128)(2,1)S(1)} %pad_maximum_fusion.y_ref.refs_5_.refs_6_), channel_id=1, source_target_pairs={{0,16},{4,20},{8,24},{12,28},{16,0},{20,4},{24,8},{28,12},{1,17},{... | collective-permute-start | bytes 344072 | tf_op jit(solution)/shard_map/ppermute | solution.py:161
  12.7 5.6 %collective-permute-start.4 = (bf16[56,1024]{1,0:T(8,128)(2,1)S(1)}, bf16[56,1024]{1,0:T(8,128)(2,1)S(1)}, u32[]{:S(2)}, u32[]{:S(2)}) collective-permute-start(bf16[56,1024]{1,0:T(8,128)(2,1)S(1)} %pad_maximum_fusion.y_ref.refs_5_.refs_6_), channel_id=1, source_target_pairs={{0,8},{4,12},{8,0},{12,4},{16,24},{20,28},{24,16},{28,20},{1,9},{5... | collective-permute-start | bytes 344072 | tf_op jit(solution)/shard_map/ppermute | solution.py:161
  14.2 6.2 %collective-permute-start.3 = (bf16[56,1024]{1,0:T(8,128)(2,1)S(1)}, bf16[56,1024]{1,0:T(8,128)(2,1)S(1)}, u32[]{:S(2)}, u32[]{:S(2)}) collective-permute-start(bf16[56,1024]{1,0:T(8,128)(2,1)S(1)} %pad_maximum_fusion.y_ref.refs_5_.refs_6_), channel_id=1, source_target_pairs={{0,28},{4,24},{8,20},{12,16},{16,12},{20,8},{24,4},{28,0},{1,29},{... | collective-permute-start | bytes 344072 | tf_op jit(solution)/shard_map/ppermute | solution.py:161
  18.3 2.1 %collective-permute-start.7 = (bf16[56,1024]{1,0:T(8,128)(2,1)S(1)}, bf16[56,1024]{1,0:T(8,128)(2,1)S(1)}, u32[]{:S(2)}, u32[]{:S(2)}) collective-permute-start(bf16[56,1024]{1,0:T(8,128)(2,1)S(1)} %collective-permute-done.4.refs_2_.refs_7_.refs_8_), channel_id=1, source_target_pairs={{0,4},{4,0},{8,12},{12,8},{16,20},{20,16},{24,28},{28,24},{1,5},{5... | collective-permute-start | bytes 344072 | tf_op jit(solution)/shard_map/ppermute | solution.py:161
  18.3 2.1 %collective-permute-start.8 = (bf16[56,1024]{1,0:T(8,128)(2,1)S(1)}, bf16[56,1024]{1,0:T(8,128)(2,1)S(1)}, u32[]{:S(2)}, u32[]{:S(2)}) collective-permute-start(bf16[56,1024]{1,0:T(8,128)(2,1)S(1)} %collective-permute-done.5.refs_3_.refs_9_.refs_10_), channel_id=1, source_target_pairs={{0,4},{4,0},{8,12},{12,8},{16,20},{20,16},{24,28},{28,24},{1,5},{5... | collective-permute-start | bytes 344072 | tf_op jit(solution)/shard_map/ppermute | solution.py:161
  20.4 1.3 %collective-permute-start.9 = (bf16[56,1024]{1,0:T(8,128)(2,1)S(1)}, bf16[56,1024]{1,0:T(8,128)(2,1)S(1)}, u32[]{:S(2)}, u32[]{:S(2)}) collective-permute-start(bf16[56,1024]{1,0:T(8,128)(2,1)S(1)} %collective-permute-done.3.refs_2_.refs_12_.refs_13_), channel_id=1, source_target_pairs={{0,4},{4,0},{8,12},{12,8},{16,20},{20,16},{24,28},{28,24},{1,5},{5... | collective-permute-start | bytes 344072 | tf_op jit(solution)/shard_map/ppermute | solution.py:161
  23.4 1.3 %collective-permute-start.10 = (f32[8,1024]{1,0:T(8,128)S(1)}, f32[8,1024]{1,0:T(8,128)S(1)}, u32[]{:S(2)}, u32[]{:S(2)}) collective-permute-start(f32[8,1024]{1,0:T(8,128)S(1)} %shard_map.65.t), channel_id=1, source_target_pairs={{0,4},{4,0},{8,12},{12,8},{16,20},{20,16},{24,28},{28,24},{1,5},{5... | collective-permute-start | bytes 98312 | tf_op jit(solution)/shard_map/ppermute | solution.py:161
  24.7 4.1 %collective-permute-start.13 = (bf16[8,1024]{1,0:T(8,128)(2,1)S(1)}, bf16[8,1024]{1,0:T(8,128)(2,1)S(1)}, u32[]{:S(2)}, u32[]{:S(2)}) collective-permute-start(bf16[8,1024]{1,0:T(8,128)(2,1)S(1)} %get-tuple-element.53), channel_id=1, source_target_pairs={{0,28},{4,24},{8,20},{12,16},{16,12},{20,8},{24,4},{28,0},{1,29},{... | collective-permute-start | bytes 49160 | tf_op jit(solution)/shard_map/ppermute | solution.py:161
  26.3 3.2 %collective-permute-start.12 = (bf16[8,1024]{1,0:T(8,128)(2,1)S(1)}, bf16[8,1024]{1,0:T(8,128)(2,1)S(1)}, u32[]{:S(2)}, u32[]{:S(2)}) collective-permute-start(bf16[8,1024]{1,0:T(8,128)(2,1)S(1)} %get-tuple-element.53), channel_id=1, source_target_pairs={{0,20},{4,16},{8,28},{12,24},{16,4},{20,0},{24,12},{28,8},{1,21},{... | collective-permute-start | bytes 49160 | tf_op jit(solution)/shard_map/ppermute | solution.py:161
  27.1 3.2 %collective-permute-start.11 = (bf16[8,1024]{1,0:T(8,128)(2,1)S(1)}, bf16[8,1024]{1,0:T(8,128)(2,1)S(1)}, u32[]{:S(2)}, u32[]{:S(2)}) collective-permute-start(bf16[8,1024]{1,0:T(8,128)(2,1)S(1)} %get-tuple-element.53), channel_id=1, source_target_pairs={{0,12},{4,8},{8,4},{12,0},{16,28},{20,24},{24,20},{28,16},{1,13},{... | collective-permute-start | bytes 49160 | tf_op jit(solution)/shard_map/ppermute | solution.py:161
  32.9 1.4 %collective-permute-start.14 = (bf16[256,256]{1,0:T(8,128)(2,1)S(1)}, bf16[256,256]{1,0:T(8,128)(2,1)S(1)}, u32[]{:S(2)}, u32[]{:S(2)}) collective-permute-start(bf16[256,256]{1,0:T(8,128)(2,1)S(1)} %get-tuple-element.56), channel_id=1, source_target_pairs={{0,4},{4,0},{8,12},{12,8},{16,20},{20,16},{24,28},{28,24},{1,5},{5... | collective-permute-start | bytes 393224 | tf_op jit(solution)/shard_map/ppermute | solution.py:161
  34.4 3.7 %collective-permute-start.15 = (bf16[88,256]{1,0:T(8,128)(2,1)S(1)}, bf16[88,256]{1,0:T(8,128)(2,1)S(1)}, u32[]{:S(2)}, u32[]{:S(2)}) collective-permute-start(bf16[88,256]{1,0:T(8,128)(2,1)S(1)} %get-tuple-element.59), channel_id=1, source_target_pairs={{0,12},{4,8},{8,4},{12,0},{16,28},{20,24},{24,20},{28,16},{1,13},{... | collective-permute-start | bytes 135176 | tf_op jit(solution)/shard_map/ppermute | solution.py:161
  35.1 3.5 %collective-permute-start.16 = (bf16[88,256]{1,0:T(8,128)(2,1)S(1)}, bf16[88,256]{1,0:T(8,128)(2,1)S(1)}, u32[]{:S(2)}, u32[]{:S(2)}) collective-permute-start(bf16[88,256]{1,0:T(8,128)(2,1)S(1)} %get-tuple-element.60), channel_id=1, source_target_pairs={{0,20},{4,16},{8,28},{12,24},{16,4},{20,0},{24,12},{28,8},{1,21},{... | collective-permute-start | bytes 135176 | tf_op jit(solution)/shard_map/ppermute | solution.py:161
  35.8 4.4 %collective-permute-start.17 = (bf16[88,256]{1,0:T(8,128)(2,1)S(1)}, bf16[88,256]{1,0:T(8,128)(2,1)S(1)}, u32[]{:S(2)}, u32[]{:S(2)}) collective-permute-start(bf16[88,256]{1,0:T(8,128)(2,1)S(1)} %get-tuple-element.61), channel_id=1, source_target_pairs={{0,28},{4,24},{8,20},{12,16},{16,12},{20,8},{24,4},{28,0},{1,29},{... | collective-permute-start | bytes 135176 | tf_op jit(solution)/shard_map/ppermute | solution.py:161
